TPU v7x, 32 devices: a whole 2x2x4 slice. The times are simulated.
32 devices in a mesh: batch: 4 (over y, x), seq: 8 (over z, core).
Axes of the slice: x: 2, y: 2, z: 4, core: 2. Of those that a mesh axis runs over, the one named last changes fastest.
Arguments:
- tokens: bfloat16 [4, 4096, 768], P('batch', 'seq'), may hold values from -6 to 6
- cotangent: bfloat16 [4, 4096, 768], P('batch', 'seq'), may hold values from -6 to 6
- norm_gains: bfloat16 [2, 2, 768], P(None, None, ('batch', 'seq')), may hold values from 0.25 to 1.75
- w_in: bfloat16 [2, 768, 2304], P(None, ('batch', 'seq')), may hold values from -0.21875 to 0.21875
- short_conv: bfloat16 [2, 3, 2304], P(None, None, ('batch', 'seq')), may hold values from -3.5 to 3.5
- w_out: bfloat16 [2, 768, 768], P(None, ('batch', 'seq')), may hold values from -0.21875 to 0.21875
- w_fc: bfloat16 [2, 768, 3072], P(None, ('batch', 'seq')), may hold values from -0.21875 to 0.21875
- w_proj: bfloat16 [2, 3072, 768], P(None, ('batch', 'seq')), may hold values from -0.109375 to 0.109375
- filt_w1: float32 [2, 33, 64], replicated, may hold values from -2.5 to 2.5
- filt_b1: float32 [2, 64], replicated, may hold values from -3.140625 to 3.140625
- filt_w2: float32 [2, 64, 64], replicated, may hold values from -1.25 to 1.25
- filt_b2: float32 [2, 64], replicated, may hold values from -3.140625 to 3.140625
- filt_w3: float32 [2, 64, 768], P(None, None, 'seq'), may hold values from -0.75 to 0.75
- skip_gain: float32 [2, 768], P(None, 'seq'), may hold values from -4 to 4
- decay_rate: float32 [2, 768], P(None, 'seq'), may hold values from 0.3 to 300
Outputs:
- mixed_out: bfloat16 [4, 4096, 768], P('batch', 'seq')
- grad_tokens: float32 [4, 4096, 768], P('batch', 'seq')
- grad_gains: float32 [2, 2, 768], P(None, None, ('batch', 'seq'))
- grad_w_in: float32 [2, 768, 2304], P(None, ('batch', 'seq'))
- grad_short_conv: float32 [2, 3, 2304], P(None, None, ('batch', 'seq'))
- grad_w_out: float32 [2, 768, 768], P(None, ('batch', 'seq'))
- grad_w_fc: float32 [2, 768, 3072], P(None, ('batch', 'seq'))
- grad_w_proj: float32 [2, 3072, 768], P(None, ('batch', 'seq'))
- grad_filt_w1: float32 [2, 33, 64], replicated
- grad_filt_b1: float32 [2, 64], replicated
- grad_filt_w2: float32 [2, 64, 64], replicated
- grad_filt_b2: float32 [2, 64], replicated
- grad_filt_w3: float32 [2, 64, 768], P(None, None, 'seq')
- grad_skip: float32 [2, 768], P(None, 'seq')
All inputs are finite; a program needn't handle non-finite values.
Results may differ from a plain program's by a relative error of at most 0.02.
Values may be sent and summed in bfloat16 or wider, within the bound.
A program may use at most 384 MiB of HBM per device.

v0:
```python
import functools
import math

import jax
import jax.numpy as jnp
from jax import lax
from jax.sharding import PartitionSpec as P

highest = lax.Precision.HIGHEST


def shifted(value, axis, steps):
    count = lax.axis_size(axis)
    first, last = (max(0, -steps), min(count, count - steps))
    return lax.ppermute(value, axis, [(source, source + steps) for source in range(first, last)])


def matmul_hi(left_mat, right_mat):
    return jnp.dot(left_mat, right_mat, precision=highest)


def product(left_mat, right_mat):
    return jnp.dot(left_mat, right_mat, preferred_element_type=jnp.float32)


def product_tn(left_mat, right_mat):
    return lax.dot_general(
        left_mat, right_mat, (((0,), (0,)), ((), ())), preferred_element_type=jnp.float32
    )


def product_nt(left_mat, right_mat):
    return lax.dot_general(
        left_mat, right_mat, (((1,), (1,)), ((), ())), preferred_element_type=jnp.float32
    )


def position_table(length, emb_width):
    positions = jnp.arange(length, dtype=jnp.int32)
    band_ids = jnp.arange(1, (emb_width - 1) // 2 + 1, dtype=jnp.int32)
    phases = positions[:, None] * band_ids[None, :] % length
    angles = 2.0 * math.pi / length * phases.astype(jnp.float32)
    ramp_col = positions.astype(jnp.float32)[:, None] / length
    return jnp.concatenate([ramp_col, jnp.cos(angles), jnp.sin(angles)], axis=1)


def make_filter(pos_table, decay_row, first_w, first_b, second_w, second_b, third_w):
    length = pos_table.shape[0]
    first_act = jnp.sin(matmul_hi(pos_table, first_w) + first_b)
    second_act = jnp.sin(matmul_hi(first_act, second_w) + second_b)
    raw_taps = matmul_hi(second_act, third_w)
    ramp_col = jnp.arange(length, dtype=jnp.float32)[:, None] / length
    shaped = raw_taps * jnp.exp(-ramp_col * decay_row[None, :])
    norm_scale = lax.rsqrt(jnp.mean(shaped * shaped, axis=0, keepdims=True) + 1e-05)
    return shaped * norm_scale * length ** (-0.5)


def rotation(row_count, col_count, modulus):
    row_ids = jnp.arange(row_count, dtype=jnp.int32)
    col_ids = jnp.arange(col_count, dtype=jnp.int32)
    phases = row_ids[:, None] * col_ids[None, :] % modulus
    angles = 2.0 * math.pi / modulus * phases.astype(jnp.float32)
    return (jnp.cos(angles), jnp.sin(angles))


def split_sizes(length):
    upper_limit = math.isqrt(2 * length)
    inner_len = 1
    for divisor in range(upper_limit, 0, -1):
        if length % divisor == 0:
            inner_len = divisor
            break
    return (2 * length // inner_len, inner_len)


def contract_last(values_arr, table):
    return jnp.einsum("ckm,mj->ckj", values_arr, table, precision=highest)


def contract_first(table, values_arr):
    return jnp.einsum("kn,cnm->ckm", table, values_arr, precision=highest)


def spectrum(chan_rows, outer_len, inner_len):
    half_len = outer_len // 2
    blocks = chan_rows.reshape(chan_rows.shape[0], half_len, inner_len)
    outer_cos, outer_sin = rotation(outer_len, half_len, outer_len)
    first_re = contract_first(outer_cos, blocks)
    first_im = -contract_first(outer_sin, blocks)
    twist_cos, twist_sin = rotation(outer_len, inner_len, outer_len * inner_len)
    turned_re = first_re * twist_cos + first_im * twist_sin
    turned_im = first_im * twist_cos - first_re * twist_sin
    inner_cos, inner_sin = rotation(inner_len, inner_len, inner_len)
    spec_re = contract_last(turned_re, inner_cos) + contract_last(turned_im, inner_sin)
    spec_im = contract_last(turned_im, inner_cos) - contract_last(turned_re, inner_sin)
    return (spec_re, spec_im)


def inverse_real(spec_re, spec_im, outer_len, inner_len):
    half_len = outer_len // 2
    inner_cos, inner_sin = rotation(inner_len, inner_len, inner_len)
    back_re = contract_last(spec_re, inner_cos) - contract_last(spec_im, inner_sin)
    back_im = contract_last(spec_re, inner_sin) + contract_last(spec_im, inner_cos)
    twist_cos, twist_sin = rotation(outer_len, inner_len, outer_len * inner_len)
    turned_re = back_re * twist_cos - back_im * twist_sin
    turned_im = back_re * twist_sin + back_im * twist_cos
    outer_cos, outer_sin = rotation(half_len, outer_len, outer_len)
    real_part = contract_first(outer_cos, turned_re) - contract_first(outer_sin, turned_im)
    return real_part.reshape(real_part.shape[0], half_len * inner_len) / (outer_len * inner_len)


def channel_mix(signal_chan, filter_taps, skip_row, outer_len, inner_len):
    signal_f = signal_chan.astype(jnp.float32)
    sig_re, sig_im = spectrum(signal_f.T, outer_len, inner_len)
    tap_re, tap_im = spectrum(filter_taps.T, outer_len, inner_len)
    mixed = inverse_real(
        sig_re * tap_re - sig_im * tap_im, sig_re * tap_im + sig_im * tap_re, outer_len, inner_len
    )
    return mixed.T + skip_row[None, :] * signal_f


def channel_back(signal_chan, grad_long_chan, filter_taps, skip_row, outer_len, inner_len):
    signal_f = signal_chan.astype(jnp.float32)
    grad_f = grad_long_chan.astype(jnp.float32)
    sig_re, sig_im = spectrum(signal_f.T, outer_len, inner_len)
    tap_re, tap_im = spectrum(filter_taps.T, outer_len, inner_len)
    grad_re, grad_im = spectrum(grad_f.T, outer_len, inner_len)
    back_signal = inverse_real(
        tap_re * grad_re + tap_im * grad_im,
        tap_re * grad_im - tap_im * grad_re,
        outer_len,
        inner_len,
    ).T
    back_taps = inverse_real(
        sig_re * grad_re + sig_im * grad_im,
        sig_re * grad_im - sig_im * grad_re,
        outer_len,
        inner_len,
    ).T
    grad_skip_row = jnp.sum(grad_f * signal_f, axis=0)
    return (back_signal + skip_row[None, :] * grad_f, back_taps, grad_skip_row)


def layer_norm_parts(stream):
    mean_val = jnp.mean(stream, axis=-1, keepdims=True)
    centered = stream - mean_val
    inv_std = lax.rsqrt(jnp.mean(centered * centered, axis=-1, keepdims=True) + 1e-05)
    return (centered * inv_std, inv_std)


def norm_back(grad_normed, normed, inv_std):
    mean_grad = jnp.mean(grad_normed, axis=-1, keepdims=True)
    mean_cross = jnp.mean(grad_normed * normed, axis=-1, keepdims=True)
    return inv_std * (grad_normed - mean_grad - normed * mean_cross)


def short_mix(extended, conv_weights):
    return (
        conv_weights[0] * extended[:-2]
        + conv_weights[1] * extended[1:-1]
        + conv_weights[2] * extended[2:]
    )


def layer_forward(stream, weights, make_taps, filter_parts, skip_row, outer_len, inner_len):
    gain_pair = weights[0].astype(jnp.float32)
    in_mat, out_mat, fc_mat, proj_mat = (weights[1], weights[3], weights[4], weights[5])
    conv_weights = weights[2].astype(jnp.float32)
    model_width = stream.shape[1]
    normed, inv_std = layer_norm_parts(stream)
    norm_in = (normed * gain_pair[0]).astype(jnp.bfloat16)
    mixed_in = product(norm_in, in_mat).astype(jnp.bfloat16)
    left_rim = shifted(mixed_in[-2:], "seq", 1)
    extended = jnp.concatenate([left_rim, mixed_in], axis=0).astype(jnp.float32)
    short_out = short_mix(extended, conv_weights)
    queries = short_out[:, :model_width]
    signal = (short_out[:, model_width : 2 * model_width] * short_out[:, 2 * model_width :]).astype(
        jnp.bfloat16
    )
    signal_chan = lax.all_to_all(signal, "seq", split_axis=1, concat_axis=0, tiled=True)
    filter_taps = make_taps(*filter_parts)
    long_chan = channel_mix(signal_chan, filter_taps, skip_row, outer_len, inner_len).astype(
        jnp.bfloat16
    )
    long_tok = lax.all_to_all(long_chan, "seq", split_axis=0, concat_axis=1, tiled=True).astype(
        jnp.float32
    )
    gated_out = (queries * long_tok).astype(jnp.bfloat16)
    middle = stream + product(gated_out, out_mat)
    normed_mid, inv_mid = layer_norm_parts(middle)
    hidden_in = (normed_mid * gain_pair[1]).astype(jnp.bfloat16)
    hidden_pre = product(hidden_in, fc_mat)
    hidden_act = jax.nn.gelu(hidden_pre).astype(jnp.bfloat16)
    result = middle + product(hidden_act, proj_mat)
    saved = (
        normed,
        inv_std,
        norm_in,
        extended,
        signal_chan,
        long_tok,
        gated_out,
        normed_mid,
        inv_mid,
        hidden_in,
        hidden_pre,
        hidden_act,
    )
    return (result, saved)


def layer_backward(
    grad_stream, weights, saved, make_taps, filter_parts, skip_row, outer_len, inner_len
):
    gain_pair = weights[0].astype(jnp.float32)
    in_mat, out_mat, fc_mat, proj_mat = (weights[1], weights[3], weights[4], weights[5])
    conv_weights = weights[2].astype(jnp.float32)
    (
        normed,
        inv_std,
        norm_in,
        extended,
        signal_chan,
        long_tok,
        gated_out,
        normed_mid,
        inv_mid,
        hidden_in,
        hidden_pre,
        hidden_act,
    ) = saved
    model_width = grad_stream.shape[1]
    grad_top = grad_stream.astype(jnp.bfloat16)
    grad_act = product_nt(grad_top, proj_mat)
    grad_proj = product_tn(hidden_act, grad_top)
    gelu_pull = jax.vjp(jax.nn.gelu, hidden_pre)[1]
    grad_pre = gelu_pull(grad_act)[0].astype(jnp.bfloat16)
    grad_hidden_in = product_nt(grad_pre, fc_mat)
    grad_fc = product_tn(hidden_in, grad_pre)
    grad_gain_mid = jnp.sum(grad_hidden_in * normed_mid, axis=0)
    grad_middle = grad_stream + norm_back(grad_hidden_in * gain_pair[1], normed_mid, inv_mid)
    grad_mix = grad_middle.astype(jnp.bfloat16)
    grad_gated = product_nt(grad_mix, out_mat)
    grad_out_mat = product_tn(gated_out, grad_mix)
    short_out = short_mix(extended, conv_weights)
    queries = short_out[:, :model_width]
    keys_part = short_out[:, model_width : 2 * model_width]
    values_part = short_out[:, 2 * model_width :]
    grad_queries = grad_gated * long_tok
    grad_long = (grad_gated * queries).astype(jnp.bfloat16)
    grad_long_chan = lax.all_to_all(grad_long, "seq", split_axis=1, concat_axis=0, tiled=True)
    filter_taps, filter_pull = jax.vjp(make_taps, *filter_parts)
    grad_signal_chan, grad_taps, grad_skip_row = channel_back(
        signal_chan, grad_long_chan, filter_taps, skip_row, outer_len, inner_len
    )
    filter_grads = filter_pull(grad_taps)
    grad_signal = lax.all_to_all(
        grad_signal_chan.astype(jnp.bfloat16), "seq", split_axis=0, concat_axis=1, tiled=True
    ).astype(jnp.float32)
    grad_short = jnp.concatenate(
        [grad_queries, grad_signal * values_part, grad_signal * keys_part], axis=1
    )
    right_rim = shifted(grad_short[:2], "seq", -1)
    grad_ext = jnp.concatenate([grad_short, right_rim], axis=0)
    grad_mixed = (
        conv_weights[2] * grad_ext[:-2]
        + conv_weights[1] * grad_ext[1:-1]
        + conv_weights[0] * grad_ext[2:]
    ).astype(jnp.bfloat16)
    grad_conv = jnp.stack(
        [
            jnp.sum(grad_short * extended[:-2], axis=0),
            jnp.sum(grad_short * extended[1:-1], axis=0),
            jnp.sum(grad_short * extended[2:], axis=0),
        ]
    )
    grad_norm_in = product_nt(grad_mixed, in_mat)
    grad_in_mat = product_tn(norm_in, grad_mixed)
    grad_gain_in = jnp.sum(grad_norm_in * normed, axis=0)
    grad_below = grad_middle + norm_back(grad_norm_in * gain_pair[0], normed, inv_std)
    block_grads = (
        jnp.stack([grad_gain_in, grad_gain_mid]),
        grad_in_mat,
        grad_conv,
        grad_out_mat,
        grad_fc,
        grad_proj,
    )
    shared_grads = (filter_grads[0], filter_grads[1], filter_grads[2], filter_grads[3])
    column_grads = (filter_grads[4], grad_skip_row)
    return (grad_below, block_grads, shared_grads, column_grads)


def stack_layers(per_layer):
    member_count = len(per_layer[0])
    return tuple(
        (
            jnp.stack([layer_grads[member_idx] for layer_grads in per_layer])
            for member_idx in range(member_count)
        )
    )


def on_device(
    tokens,
    cotangent,
    norm_gains,
    w_in,
    short_conv,
    w_out,
    w_fc,
    w_proj,
    filt_w1,
    filt_b1,
    filt_w2,
    filt_b2,
    filt_w3,
    skip_gain,
    decay_rate,
):
    layer_count = w_in.shape[0]
    stream = tokens[0].astype(jnp.float32)
    tok_rows = stream.shape[0]
    length = tok_rows * lax.axis_size("seq")
    outer_len, inner_len = split_sizes(length)
    pos_table = position_table(length, filt_w1.shape[1])
    saved_acts = []
    for layer_idx in range(layer_count):
        weights = (
            lax.all_gather(norm_gains[layer_idx], ("batch", "seq"), axis=1, tiled=True),
            lax.all_gather(w_in[layer_idx], ("batch", "seq"), axis=0, tiled=True),
            lax.all_gather(short_conv[layer_idx], ("batch", "seq"), axis=1, tiled=True),
            lax.all_gather(w_out[layer_idx], ("batch", "seq"), axis=0, tiled=True),
            lax.all_gather(w_fc[layer_idx], ("batch", "seq"), axis=0, tiled=True),
            lax.all_gather(w_proj[layer_idx], ("batch", "seq"), axis=0, tiled=True),
        )
        make_taps = functools.partial(make_filter, pos_table, decay_rate[layer_idx])
        filter_parts = (
            filt_w1[layer_idx],
            filt_b1[layer_idx],
            filt_w2[layer_idx],
            filt_b2[layer_idx],
            filt_w3[layer_idx],
        )
        stream, saved = layer_forward(
            stream, weights, make_taps, filter_parts, skip_gain[layer_idx], outer_len, inner_len
        )
        saved_acts.append((None, saved))
    grad_stream = cotangent[0].astype(jnp.float32)
    block_list = []
    shared_list = []
    column_list = []
    for layer_idx in reversed(range(layer_count)):
        weights = (
            lax.all_gather(norm_gains[layer_idx], ("batch", "seq"), axis=1, tiled=True),
            lax.all_gather(w_in[layer_idx], ("batch", "seq"), axis=0, tiled=True),
            lax.all_gather(short_conv[layer_idx], ("batch", "seq"), axis=1, tiled=True),
            lax.all_gather(w_out[layer_idx], ("batch", "seq"), axis=0, tiled=True),
            lax.all_gather(w_fc[layer_idx], ("batch", "seq"), axis=0, tiled=True),
            lax.all_gather(w_proj[layer_idx], ("batch", "seq"), axis=0, tiled=True),
        )
        make_taps = functools.partial(make_filter, pos_table, decay_rate[layer_idx])
        filter_parts = (
            filt_w1[layer_idx],
            filt_b1[layer_idx],
            filt_w2[layer_idx],
            filt_b2[layer_idx],
            filt_w3[layer_idx],
        )
        grad_stream, block_grads, shared_grads, column_grads = layer_backward(
            grad_stream,
            weights,
            saved_acts[layer_idx][1],
            make_taps,
            filter_parts,
            skip_gain[layer_idx],
            outer_len,
            inner_len,
        )
        shared_list.insert(
            0,
            lax.psum(
                (shared_grads[0], shared_grads[1], shared_grads[2], shared_grads[3]),
                ("batch", "seq"),
            ),
        )
        column_list.insert(0, lax.psum((column_grads[0], column_grads[1]), "batch"))
        block_grads = (
            lax.psum_scatter(block_grads[0], ("batch", "seq"), scatter_dimension=1, tiled=True),
            lax.psum_scatter(block_grads[1], ("batch", "seq"), scatter_dimension=0, tiled=True),
            lax.psum_scatter(block_grads[2], ("batch", "seq"), scatter_dimension=1, tiled=True),
            lax.psum_scatter(block_grads[3], ("batch", "seq"), scatter_dimension=0, tiled=True),
            lax.psum_scatter(block_grads[4], ("batch", "seq"), scatter_dimension=0, tiled=True),
            lax.psum_scatter(block_grads[5], ("batch", "seq"), scatter_dimension=0, tiled=True),
        )
        block_list.insert(0, block_grads)
    block_stack = stack_layers(block_list)
    shared_stack = stack_layers(shared_list)
    column_stack = stack_layers(column_list)
    return (
        stream[None].astype(jnp.bfloat16),
        grad_stream[None],
        block_stack[0],
        block_stack[1],
        block_stack[2],
        block_stack[3],
        block_stack[4],
        block_stack[5],
        shared_stack[0],
        shared_stack[1],
        shared_stack[2],
        shared_stack[3],
        column_stack[0],
        column_stack[1],
    )


def solution(mesh):
    in_specs = (
        P("batch", "seq", None),
        P("batch", "seq", None),
        P(None, None, ("batch", "seq")),
        P(None, ("batch", "seq"), None),
        P(None, None, ("batch", "seq")),
        P(None, ("batch", "seq"), None),
        P(None, ("batch", "seq"), None),
        P(None, ("batch", "seq"), None),
        P(),
        P(),
        P(),
        P(),
        P(None, None, "seq"),
        P(None, "seq"),
        P(None, "seq"),
    )
    out_specs = (
        P("batch", "seq", None),
        P("batch", "seq", None),
        P(None, None, ("batch", "seq")),
        P(None, ("batch", "seq"), None),
        P(None, None, ("batch", "seq")),
        P(None, ("batch", "seq"), None),
        P(None, ("batch", "seq"), None),
        P(None, ("batch", "seq"), None),
        P(),
        P(),
        P(),
        P(),
        P(None, None, "seq"),
        P(None, "seq"),
    )
    return jax.shard_map(
        on_device, mesh=mesh, in_specs=in_specs, out_specs=out_specs, check_vma=False
    )
```

profile of v0, /device:TPU:0, one launch (start us, length us, event | category | flops | bytes accessed | tf_op | source)
XLA Modules:
  0.0 2223.5 jit_solution(6264464457041172535)
XLA Ops:
  67.0 45.0 %all-gather.1 = bf16[1,2,768]{1,0,2:T(2,128)(2,1)S(1)} all-gather(bf16[1,2,24]{1,0,2:T(2,128)(2,1)S(1)} %copy.221), channel_id=3, replica_groups=mesh['batch'=4,'seq'=8] {'batch','seq'}, dimensions={2}, use_global_device_ids=true | all-gather | bytes 3168 | tf_op jit(solution)/shard_map/all_gather | solution.py:330
  117.0 43.1 %all-gather = bf16[1,3,2304]{1,0,2:T(2,128)(2,1)S(1)} all-gather(bf16[1,3,72]{1,0,2:T(2,128)(2,1)S(1)} %copy.220), channel_id=2, replica_groups=mesh['batch'=4,'seq'=8] {'batch','seq'}, dimensions={2}, use_global_device_ids=true | all-gather | bytes 14256 | tf_op jit(solution)/shard_map/all_gather | solution.py:332
  161.4 69.1 %slice_reduce_fusion.5 = (f32[2304]{0:T(1024)S(1)}, f32[2304]{0:T(1024)S(1)}, f32[2304]{0:T(1024)S(1)}) fusion(f32[1,3,2304]{1,0,2:T(1,128)S(1)} %convert_element_type.555), kind=kLoop, calls=%fused_computation.315 | loop fusion | bytes 55296 | tf_op jit(solution)/shard_map/slice | solution.py:159
  262.5 48.0 %all-gather.7 = bf16[1,2,768]{1,0,2:T(2,128)(2,1)S(1)} all-gather(bf16[1,2,24]{1,0,2:T(2,128)(2,1)S(1)} %copy.224), channel_id=9, replica_groups=mesh['batch'=4,'seq'=8] {'batch','seq'}, dimensions={2}, use_global_device_ids=true | all-gather | bytes 3168 | tf_op jit(solution)/shard_map/all_gather | solution.py:330
  311.7 44.6 %all-gather.6 = bf16[1,3,2304]{1,0,2:T(2,128)(2,1)S(1)} all-gather(bf16[1,3,72]{1,0,2:T(2,128)(2,1)S(1)} %copy.223), channel_id=8, replica_groups=mesh['batch'=4,'seq'=8] {'batch','seq'}, dimensions={2}, use_global_device_ids=true | all-gather | bytes 14256 | tf_op jit(solution)/shard_map/all_gather | solution.py:332
  449.1 69.6 %slice_reduce_fusion.2 = (f32[2304]{0:T(1024)S(1)}, f32[2304]{0:T(1024)S(1)}, f32[2304]{0:T(1024)S(1)}) fusion(f32[1,3,2304]{1,0,2:T(1,128)S(1)} %copy-done.47), kind=kLoop, calls=%fused_computation.312 | loop fusion | bytes 55296 | tf_op jit(solution)/shard_map/slice | solution.py:159
  652.1 23.8 %all_to_all.128 = bf16[8,512,96]{1,2,0:T(8,128)(2,1)S(1)} all-to-all(bf16[8,512,96]{1,2,0:T(8,128)(2,1)S(1)} %bitcast.742), channel_id=1, replica_groups=mesh['batch'=4,'seq'=8] {'seq'}, dimensions={0} | all-to-all | bytes 1572864 | tf_op jit(solution)/shard_map/all_to_all | solution.py:185
  715.9 24.4 %all_to_all.129 = bf16[512,8,96]{0,2,1:T(8,128)(2,1)S(1)} all-to-all(bf16[512,8,96]{0,2,1:T(8,128)(2,1)} %bitcast.743), channel_id=1, replica_groups=mesh['batch'=4,'seq'=8] {'seq'}, dimensions={1} | all-to-all | bytes 1572864 | tf_op jit(solution)/shard_map/all_to_all | solution.py:251
  768.5 10.8 multiply_subtract_fusion
  822.9 12.3 all-to-all-done.5
  862.3 9.5 fusion.6
  931.9 10.9 multiply_subtract_fusion.1
  1083.0 9.7 fusion.222
  1094.2 9.6 fusion.228
  1137.5 15.6 all-reduce.5
  1157.4 35.3 %all-reduce.8.cloned.1.call-done = (f32[2,768]{1,0:T(2,128)}, f32[2,768]{1,0:T(2,128)}, f32[3,2304]{1,0:T(4,128)}, f32[3,2304]{1,0:T(4,128)}, f32[1,33,64]{2,1,0...) async-done(((f32[2,768]{1,0:T(2,128)}, f32[2,768]{1,0:T(2,128)}, ...) | async-done | bytes 118288
  1202.1 96.7 %reduce-scatter.19.cloned.1.call-done = f32[24,768]{1,0:T(8,128)} async-done(((f32[768,768]{1,0:T(8,128)}), f32[24,768]{1,0:T(8,128)}) %reduce-scatter.19.cloned.1.call-update) | async-done | bytes 73744 | tf_op jit(solution)/shard_map/reduce_scatter | solution.py:392
  1298.8 103.3 %reduce-scatter.17.cloned.1.call-done = f32[24,768]{1,0:T(8,128)} async-done(((f32[768,768]{1,0:T(8,128)}), f32[24,768]{1,0:T(8,128)}) %reduce-scatter.17.cloned.1.call-update) | async-done | bytes 73744 | tf_op jit(solution)/shard_map/reduce_scatter | solution.py:392
  1403.7 123.0 %reduce-scatter.15.cloned.1.call-done = f32[24,2304]{1,0:T(8,128)} async-done(((f32[768,2304]{1,0:T(8,128)}), f32[24,2304]{1,0:T(8,128)}) %reduce-scatter.15.cloned.1.call-update) | async-done | bytes 221200 | tf_op jit(solution)/shard_map/reduce_scatter | solution.py:390
  1526.7 124.1 %reduce-scatter.13.cloned.1.call-done = f32[24,2304]{1,0:T(8,128)} async-done(((f32[768,2304]{1,0:T(8,128)}), f32[24,2304]{1,0:T(8,128)}) %reduce-scatter.13.cloned.1.call-update) | async-done | bytes 221200 | tf_op jit(solution)/shard_map/reduce_scatter | solution.py:390
  1652.7 139.8 %reduce-scatter.27.cloned.1.call-done = f32[96,768]{1,0:T(8,128)} async-done(((f32[3072,768]{1,0:T(8,128)}), f32[96,768]{1,0:T(8,128)}) %reduce-scatter.27.cloned.1.call-update) | async-done | bytes 294928 | tf_op jit(solution)/shard_map/reduce_scatter | solution.py:394
  1792.5 140.1 %reduce-scatter.25.cloned.1.call-done = f32[96,768]{1,0:T(8,128)} async-done(((f32[3072,768]{1,0:T(8,128)}), f32[96,768]{1,0:T(8,128)}) %reduce-scatter.25.cloned.1.call-update) | async-done | bytes 294928 | tf_op jit(solution)/shard_map/reduce_scatter | solution.py:394
  1934.5 139.8 %reduce-scatter.23.cloned.1.call-done = f32[24,3072]{1,0:T(8,128)} async-done(((f32[768,3072]{1,0:T(8,128)}), f32[24,3072]{1,0:T(8,128)}) %reduce-scatter.23.cloned.1.call-update) | async-done | bytes 294928 | tf_op jit(solution)/shard_map/reduce_scatter | solution.py:393
  2074.3 140.4 %reduce-scatter.21.cloned.1.call-done = f32[24,3072]{1,0:T(8,128)} async-done(((f32[768,3072]{1,0:T(8,128)}), f32[24,3072]{1,0:T(8,128)}) %reduce-scatter.21.cloned.1.call-update) | async-done | bytes 294928 | tf_op jit(solution)/shard_map/reduce_scatter | solution.py:393
  (644 shorter events, 717.6 us)
Async XLA Ops:
  7.2 223.4 %all-gather.21.cloned.1.call-start = ((), (), s32[]{:S(2)}) async-start(), calls=%async_computation.24 | async-start | bytes 3649536 | tf_op jit(solution)/shard_map/all_gather | solution.py:331
  8.9 518.2 %all-gather.23.cloned.1.call-start = ((), (), s32[]{:S(2)}) async-start(), calls=%async_computation.25 | async-start | bytes 1216512 | tf_op jit(solution)/shard_map/all_gather | solution.py:333
  10.4 520.8 %all-gather.25.cloned.1.call-start = ((), (), s32[]{:S(2)}) async-start(), calls=%async_computation.26 | async-start | bytes 4866048 | tf_op jit(solution)/shard_map/all_gather | solution.py:334
  12.2 527.5 %all-gather.27.cloned.1.call-start = ((), (), s32[]{:S(2)}) async-start(), calls=%async_computation.27 | async-start | bytes 4866048 | tf_op jit(solution)/shard_map/all_gather | solution.py:335
  14.0 535.7 %all-gather.29.cloned.1.call-start = ((), (), s32[]{:S(2)}) async-start(), calls=%async_computation.28 | async-start | bytes 3649536 | tf_op jit(solution)/shard_map/all_gather | solution.py:331
  14.6 668.7 %all-gather.31.cloned.1.call-start = ((), (), s32[]{:S(2)}) async-start(), calls=%async_computation.29 | async-start | bytes 1216512 | tf_op jit(solution)/shard_map/all_gather | solution.py:333
  15.1 672.5 %all-gather.33.cloned.1.call-start = ((), (), s32[]{:S(2)}) async-start(), calls=%async_computation.30 | async-start | bytes 4866048 | tf_op jit(solution)/shard_map/all_gather | solution.py:334
  15.9 679.9 %all-gather.35.cloned.1.call-start = ((), (), s32[]{:S(2)}) async-start(), calls=%async_computation.31 | async-start | bytes 4866048 | tf_op jit(solution)/shard_map/all_gather | solution.py:335
  235.1 7.5 collective-permute-start
  250.8 128.8 %all-to-all-start = ((bf16[512,8,96]{0,2,1:T(8,128)(2,1)}), bf16[512,8,96]{0,2,1:T(8,128)(2,1)}, u32[]{:S(2)}, u32[]{:S(2)}) async-start(bf16[512,8,96]{0,2,1:T(8,128)(2,1)} %bitcast.738), calls=%async_computation | async-start | bytes 1572864 | tf_op jit(solution)/shard_map/all_to_all | solution.py:180
  430.8 87.8 %all-to-all-start.1 = ((bf16[8,512,96]{1,2,0:T(8,128)(2,1)}), bf16[8,512,96]{1,2,0:T(8,128)(2,1)}, u32[]{:S(2)}, u32[]{:S(2)}) async-start(bf16[8,512,96]{1,2,0:T(8,128)(2,1)} %bitcast.707), calls=%async_computation.1 | async-start | bytes 1572864 | tf_op jit(solution)/shard_map/all_to_all | solution.py:185
  570.2 26.3 %all-to-all-start.2 = ((bf16[512,8,96]{0,2,1:T(8,128)(2,1)}), bf16[512,8,96]{0,2,1:T(8,128)(2,1)}, u32[]{:S(2)}, u32[]{:S(2)}) async-start(bf16[512,8,96]{0,2,1:T(8,128)(2,1)} %bitcast.740), calls=%async_computation.2 | async-start | bytes 1572864 | tf_op jit(solution)/shard_map/all_to_all | solution.py:180
  809.8 25.4 %all-to-all-start.5 = ((bf16[8,512,96]{1,2,0:T(8,128)(2,1)}), bf16[8,512,96]{1,2,0:T(8,128)(2,1)}, u32[]{:S(2)}, u32[]{:S(2)}) async-start(bf16[8,512,96]{1,2,0:T(8,128)(2,1)} %bitcast.741), calls=%async_computation.5 | async-start | bytes 1572864 | tf_op jit(solution)/shard_map/all_to_all | solution.py:257
  883.5 25.6 %all-to-all-start.6 = ((bf16[512,8,96]{0,2,1:T(8,128)(2,1)}), bf16[512,8,96]{0,2,1:T(8,128)(2,1)}, u32[]{:S(2)}, u32[]{:S(2)}) async-start(bf16[512,8,96]{0,2,1:T(8,128)(2,1)} %bitcast.739), calls=%async_computation.6 | async-start | bytes 1572864 | tf_op jit(solution)/shard_map/all_to_all | solution.py:251
  1004.2 33.8 %all-to-all-start.7 = ((bf16[8,512,96]{1,2,0:T(8,128)(2,1)}), bf16[8,512,96]{1,2,0:T(8,128)(2,1)}, u32[]{:S(2)}, u32[]{:S(2)}) async-start(bf16[8,512,96]{1,2,0:T(8,128)(2,1)} %bitcast.737), calls=%async_computation.7 | async-start | bytes 1572864 | tf_op jit(solution)/shard_map/all_to_all | solution.py:257
  1008.5 184.2 %all-reduce.8.cloned.1.call-start = ((), (), s32[]{:S(2)}) async-start(), calls=%async_computation.32 | async-start | bytes 389120
  1060.3 238.5 %reduce-scatter.19.cloned.1.call-start = ((), (), s32[]{:S(2)}) async-start(), calls=%async_computation.19 | async-start | bytes 2433024 | tf_op jit(solution)/shard_map/reduce_scatter | solution.py:392
  1063.8 338.3 %reduce-scatter.17.cloned.1.call-start = ((), (), s32[]{:S(2)}) async-start(), calls=%async_computation.18 | async-start | bytes 2433024 | tf_op jit(solution)/shard_map/reduce_scatter | solution.py:392
  1067.4 459.3 %reduce-scatter.15.cloned.1.call-start = ((), (), s32[]{:S(2)}) async-start(), calls=%async_computation.17 | async-start | bytes 7299072 | tf_op jit(solution)/shard_map/reduce_scatter | solution.py:390
  1074.1 576.7 %reduce-scatter.13.cloned.1.call-start = ((), (), s32[]{:S(2)}) async-start(), calls=%async_computation.16 | async-start | bytes 7299072 | tf_op jit(solution)/shard_map/reduce_scatter | solution.py:390
  1081.9 710.6 %reduce-scatter.27.cloned.1.call-start = ((), (), s32[]{:S(2)}) async-start(), calls=%async_computation.23 | async-start | bytes 9732096 | tf_op jit(solution)/shard_map/reduce_scatter | solution.py:394
  1092.8 839.8 %reduce-scatter.25.cloned.1.call-start = ((), (), s32[]{:S(2)}) async-start(), calls=%async_computation.22 | async-start | bytes 9732096 | tf_op jit(solution)/shard_map/reduce_scatter | solution.py:394
  1103.8 970.4 %reduce-scatter.23.cloned.1.call-start = ((), (), s32[]{:S(2)}) async-start(), calls=%async_computation.21 | async-start | bytes 9732096 | tf_op jit(solution)/shard_map/reduce_scatter | solution.py:393
  1112.5 1102.2 %reduce-scatter.21.cloned.1.call-start = ((), (), s32[]{:S(2)}) async-start(), calls=%async_computation.20 | async-start | bytes 9732096 | tf_op jit(solution)/shard_map/reduce_scatter | solution.py:393
  (161 other events, 2250.5 us)
Sparse Core Ops, SparseCore 0:
  11.6 63.0 all-gather.20
  78.3 53.6 all-gather.22
  135.0 63.1 all-gather.24
  201.1 66.3 all-gather.26
  270.3 64.7 all-gather.28
  338.6 52.2 all-gather.30
  393.9 75.1 all-gather.32
  472.7 61.4 all-gather.34
  1060.4 132.1 all-reduce.7
  1198.6 100.0 reduce-scatter.18
  1304.0 98.0 reduce-scatter.16
  1408.6 118.1 reduce-scatter.14
  1532.4 118.4 reduce-scatter.12
  1657.6 134.8 reduce-scatter.26
  1798.2 134.3 reduce-scatter.24
  1939.4 134.8 reduce-scatter.22
  2080.0 134.6 reduce-scatter.20
where the time goes:
time: 2240 us; the launch traced here: 2220 us
  waiting for transfers between devices  1070 us (48%)
  matrix products  498 us (22%)
  local copies, waits for them, and re-layouts  282 us (13%)
  blocking collectives  244 us (11%)
  other arithmetic  79.6 us (4%)
  starting transfers between devices  35.1 us (2%)
    reduce_scatter x2, waiting for transfers between devices, on_device(): lax.psum_scatter(block_grads[4], ('batch', 'seq'), scatter_dimension=0, t...  280 us
    reduce_scatter x2, waiting for transfers between devices, on_device(): lax.psum_scatter(block_grads[5], ('batch', 'seq'), scatter_dimension=0, t...  280 us
    reduce_scatter x2, waiting for transfers between devices, on_device(): lax.psum_scatter(block_grads[1], ('batch', 'seq'), scatter_dimension=0, t...  247 us
    dot_general x48, matrix products, contract_last(): return jnp.einsum('ckm,mj->ckj', values_arr, table, precision=highest)  225 us
    reduce_scatter x2, waiting for transfers between devices, on_device(): lax.psum_scatter(block_grads[3], ('batch', 'seq'), scatter_dimension=0, t...  200 us
    slice x2, local copies, waits for them, and re-layouts, short_mix(): conv_weights[0] * extended[:-2] + conv_weights[1] * extended[1:-1]  139 us
    all_gather x2, blocking collectives, on_device(): lax.all_gather(norm_gains[layer_idx], ('batch', 'seq'), axis=1, tiled=True)  93 us
    all_gather x2, blocking collectives, on_device(): lax.all_gather(short_conv[layer_idx], ('batch', 'seq'), axis=1, tiled=True)  87.6 us
  transfers between devices with their start and end apart: 27, of which 13 were waited for; matrix products, arithmetic and copies ran while one was open for 27% of the time, Pallas kernels for 0%

commit v1 on v0

v1 whole, which is shorter than its diff:
```python
import functools
import math

import jax
import jax.numpy as jnp
import numpy as np
from jax import lax
from jax.experimental import pallas as pl
from jax.experimental.pallas import tpu as pltpu
from jax.sharding import PartitionSpec as P

MESH = pl.DeviceIdType.MESH
LANES = 128
VMEM_LIMIT = 56 * 1024 * 1024
f32 = jnp.float32
bf16 = jnp.bfloat16
HIGH = lax.Precision.HIGHEST


def product(left_mat, right_mat):
    return jnp.dot(left_mat, right_mat, preferred_element_type=f32)


def contract(left_mat, right_mat, left_dim, right_dim):
    return lax.dot_general(
        left_mat, right_mat, (((left_dim,), (right_dim,)), ((), ())), preferred_element_type=f32
    )


def layer_norm_parts(stream):
    mean_val = jnp.mean(stream, axis=-1, keepdims=True)
    centered = stream - mean_val
    inv_std = lax.rsqrt(jnp.mean(centered * centered, axis=-1, keepdims=True) + 1e-05)
    return (centered * inv_std, inv_std)


def norm_back(grad_normed, normed, inv_std):
    mean_grad = jnp.mean(grad_normed, axis=-1, keepdims=True)
    mean_cross = jnp.mean(grad_normed * normed, axis=-1, keepdims=True)
    return inv_std * (grad_normed - mean_grad - normed * mean_cross)


def shifted(value, axis, steps):
    count = lax.axis_size(axis)
    first, last = (max(0, -steps), min(count, count - steps))
    return lax.ppermute(value, axis, [(source, source + steps) for source in range(first, last)])


def split_bf16(table):
    high = table.astype(np.float32).astype(jnp.bfloat16)
    low = (table - high.astype(np.float64)).astype(np.float32).astype(jnp.bfloat16)
    return jnp.asarray(high), jnp.asarray(low)


def transform_tables(blocks):
    length = blocks * LANES
    n1 = np.arange(blocks)
    n2 = np.arange(LANES)
    outer = 2 * np.pi * ((n1[:, None] * (4 * n1[None, :] + 1)) % (4 * blocks)) / (4 * blocks)
    eye = np.eye(8)
    forward = np.concatenate([np.cos(outer).T, -np.sin(outer).T], axis=0)
    left_fwd = np.kron(forward, eye)
    left_inv = np.kron(np.concatenate([np.cos(outer), -np.sin(outer)], axis=1), eye) / length
    inner = 2 * np.pi * ((n2[:, None] * n2[None, :]) % LANES) / LANES
    cos2, sin2 = np.cos(inner), np.sin(inner)
    right_fwd = np.block([[cos2, -sin2], [sin2, cos2]])
    right_inv = np.block([[cos2, sin2], [-sin2, cos2]])
    twist = 2 * np.pi * (n2[None, :] * (4 * n1[:, None] + 1)) / (4 * length)
    twist_cos = np.repeat(np.cos(twist), 8, axis=0).astype(np.float32)
    twist_sin = np.repeat(np.sin(twist), 8, axis=0).astype(np.float32)
    tables = []
    for table in (left_fwd, right_fwd, left_inv, right_inv):
        tables.extend(split_bf16(table))
    return tuple(tables) + (jnp.asarray(twist_cos), jnp.asarray(twist_sin))


def dot_split(left_high, left_low, right):
    high = right.astype(bf16)
    low = (right - high.astype(f32)).astype(bf16)
    return product(left_high, high) + product(left_low, high) + product(left_high, low)


def dot_right_split(left, right_high, right_low):
    high = left.astype(bf16)
    low = (left - high.astype(f32)).astype(bf16)
    return product(high, right_high) + product(high, right_low) + product(low, right_high)


def to_points(x, tables, exact):
    left_high, left_low, right_high, right_low = [t[...] for t in tables[:4]]
    twist_cos, twist_sin = tables[8][...], tables[9][...]
    rows = x.shape[0] * 8
    flat = x.reshape(rows, LANES)
    if exact:
        flat = flat.astype(bf16)
        turned = product(left_high, flat) + product(left_low, flat)
    else:
        turned = dot_split(left_high, left_low, flat)
    re, im = turned[:rows], turned[rows:]
    both = jnp.concatenate([re * twist_cos + im * twist_sin, im * twist_cos - re * twist_sin], axis=1)
    points = dot_right_split(both, right_high, right_low)
    return points[:, :LANES], points[:, LANES:]


def from_points(re, im, tables):
    left_high, left_low, right_high, right_low = [t[...] for t in tables[4:8]]
    twist_cos, twist_sin = tables[8][...], tables[9][...]
    rows = re.shape[0]
    back = dot_right_split(jnp.concatenate([re, im], axis=1), right_high, right_low)
    re, im = back[:, :LANES], back[:, LANES:]
    both = jnp.concatenate([re * twist_cos - im * twist_sin, re * twist_sin + im * twist_cos], axis=0)
    return dot_split(left_high, left_low, both).reshape(rows // 8, 8, LANES)


def position_rows(length, emb_width):
    positions = np.arange(length, dtype=np.int64)
    bands = np.arange(1, (emb_width - 1) // 2 + 1, dtype=np.int64)
    angles = 2.0 * np.pi / length * ((bands[:, None] * positions[None, :]) % length)
    table = np.concatenate([positions[None, :] / length, np.cos(angles), np.sin(angles)], axis=0)
    return jnp.asarray(table.astype(np.float32))


def filter_forward(pos_rows, first_w, first_b, second_w, second_b, third_w, decay_col):
    length = pos_rows.shape[1]
    first_arg = jnp.dot(first_w.T, pos_rows, precision=HIGH) + first_b[:, None]
    first_act = jnp.sin(first_arg)
    second_arg = jnp.dot(second_w.T, first_act, precision=HIGH) + second_b[:, None]
    second_act = jnp.sin(second_arg)
    raw = jnp.dot(third_w.T, second_act, precision=HIGH)
    ramp = jnp.arange(length, dtype=f32)[None, :] / length
    window = jnp.exp(-ramp * decay_col[:, None])
    shaped = raw * window
    scale = lax.rsqrt(jnp.mean(shaped * shaped, axis=1, keepdims=True) + 1e-05)
    taps = shaped * scale * length ** (-0.5)
    return taps


class Place:
    def __init__(self, ns):
        self.nz = ns // 2
        self.b = lax.axis_index("batch")
        self.s = lax.axis_index("seq")
        self.z = lax.div(self.s, 2)
        self.c = lax.rem(self.s, 2)
        self.x_peer = (lax.bitwise_xor(self.b, 1), self.s)
        self.y_peer = (lax.bitwise_xor(self.b, 2), self.s)
        self.core_peer = (self.b, lax.bitwise_xor(self.s, 1))
        self.up_peer = (self.b, lax.min(self.s + 2, ns - 1))
        self.down_peer = (self.b, lax.max(self.s - 2, 0))


def remote(src, dst, send, recv, peer):
    return pltpu.make_async_remote_copy(
        src_ref=src, dst_ref=dst, send_sem=send, recv_sem=recv, device_id=peer, device_id_type=MESH
    )


def greet(place, seq_peers):
    bar = pltpu.get_barrier_semaphore()

    def hello(peer):
        pl.semaphore_signal(bar, inc=1, device_id=peer, device_id_type=MESH)

    hello(place.x_peer)
    hello(place.y_peer)
    if seq_peers:
        ns = 2 * place.nz
        for step in range(1, ns):
            hello((place.b, lax.rem(place.s + step, ns)))
        pl.semaphore_wait(bar, 2 + ns - 1)
    else:
        hello(place.core_peer)
        pl.when(place.z + 1 < place.nz)(lambda: hello(place.up_peer))
        pl.when(place.z > 0)(lambda: hello(place.down_peer))
        ends = jnp.where(place.z == 0, 1, 0) + jnp.where(place.z == place.nz - 1, 1, 0)
        pl.semaphore_wait(bar, 5 - ends)


def gather_sems(nz):
    return [
        pltpu.SemaphoreType.DMA((4,)),
        pltpu.SemaphoreType.DMA((2, nz)),
        pltpu.SemaphoreType.DMA((nz,)),
        pltpu.SemaphoreType.DMA((4, nz)),
        pltpu.SemaphoreType.DMA((4, nz)),
    ]


def gather_task(place, src, dst, sems):
    one, chain_send, chain_recv, send, recv = sems
    b, z, c, nz = place.b, place.z, place.c, place.nz
    bx, by, bd = place.x_peer[0], place.y_peer[0], lax.bitwise_xor(b, 3)
    own = dst.at[b, z, c]
    local = pltpu.make_async_copy(src, own, one.at[0])

    def chain(source, shard, up):
        row = 0 if up else 1
        peer = place.up_peer if up else place.down_peer
        return remote(source, dst.at[b, shard, c], chain_send.at[row, shard], chain_recv.at[shard], peer)

    def across(source, shard, along):
        peer = place.y_peer if along else place.x_peer
        return remote(source, dst.at[b, shard, c], send.at[along, shard], recv.at[along, shard], peer)

    def onward(shard, along):
        peer = place.y_peer if along else place.x_peer
        part = dst.at[bx if along else by, shard, c]
        return remote(part, part, send.at[2 + along, shard], recv.at[2 + along, shard], peer)

    local.start()
    pl.when(z + 1 < nz)(lambda: chain(src, z, True).start())
    pl.when(z > 0)(lambda: chain(src, z, False).start())
    across(src, z, 0).start()
    across(src, z, 1).start()
    yield
    for hop in range(1, nz):
        below, above = z - hop, z + hop

        @pl.when(below >= 0)
        def _():
            chain(src, below, True).wait_recv()
            part = dst.at[b, below, c]
            pl.when(z + 1 < nz)(lambda: chain(part, below, True).start())
            across(part, below, 0).start()
            across(part, below, 1).start()

        @pl.when(above < nz)
        def _():
            chain(src, above, False).wait_recv()
            part = dst.at[b, above, c]
            pl.when(z > 0)(lambda: chain(part, above, False).start())
            across(part, above, 0).start()
            across(part, above, 1).start()

        yield

    def pass_on(shard):
        across(src, shard, 0).wait_recv()
        across(src, shard, 1).wait_recv()
        even = lax.rem(shard, 2) == 0
        pl.when(even)(lambda: onward(shard, 1).start())
        pl.when(jnp.logical_not(even))(lambda: onward(shard, 0).start())

    pass_on(z)
    for hop in range(1, nz):
        pl.when(z - hop >= 0)(lambda: pass_on(z - hop))
        pl.when(z + hop < nz)(lambda: pass_on(z + hop))
    yield
    for shard in range(nz):
        onward(shard, 1 - shard % 2).wait_recv()
    local.wait()
    column = dst.at[:, :, c]
    core = remote(column, column, one.at[1], one.at[2], place.core_peer)
    core.start()
    yield
    for shard in range(nz):
        if shard > 0:
            pl.when(jnp.logical_and(z >= shard, z + 1 < nz))(
                lambda: chain(src, z - shard, True).wait_send()
            )
            pl.when(jnp.logical_and(z + shard < nz, z > 0))(
                lambda: chain(src, z + shard, False).wait_send()
            )
        else:
            pl.when(z + 1 < nz)(lambda: chain(src, z, True).wait_send())
            pl.when(z > 0)(lambda: chain(src, z, False).wait_send())
        across(src, shard, 0).wait_send()
        across(src, shard, 1).wait_send()
        onward(shard, 1 - shard % 2).wait_send()
    core.wait()
    yield


def run_staggered(tasks):
    live = []
    waiting = list(tasks)
    while live or waiting:
        if waiting:
            live.append(waiting.pop(0))
        for task in reversed(list(live)):
            if next(task, "end") == "end":
                live.remove(task)


def gather_kernel(ns, picks, *refs):
    count = len(picks)
    srcs, dsts, sems = refs[:count], refs[count : 2 * count], refs[2 * count :]
    place = Place(ns)
    greet(place, False)
    run_staggered(
        gather_task(place, srcs[i].at[layer], dsts[i], sems[5 * i : 5 * i + 5])
        for i, layer in enumerate(picks)
    )


def gather(arrays, picks, collective_id):
    nb, ns = lax.axis_size("batch"), lax.axis_size("seq")
    nz = ns // 2
    count = len(arrays)
    scratch = []
    for _ in arrays:
        scratch.extend(gather_sems(nz))
    results = pl.pallas_call(
        functools.partial(gather_kernel, ns, picks),
        out_shape=[jax.ShapeDtypeStruct((nb, nz, 2) + a.shape[1:], a.dtype) for a in arrays],
        in_specs=[pl.BlockSpec(memory_space=pl.ANY)] * count,
        out_specs=[pl.BlockSpec(memory_space=pl.ANY)] * count,
        scratch_shapes=scratch,
        compiler_params=pltpu.CompilerParams(collective_id=collective_id, has_side_effects=True),
        name="gather_weights",
    )(*arrays)
    return [r.reshape((nb * ns,) + a.shape[1:]) for r, a in zip(results, arrays)]


def reduce_scratch(nz, shape, dtype):
    half = (nz,) + shape
    return [
        pltpu.VMEM((4,) + half, dtype),
        pltpu.VMEM((4,) + half, dtype),
        pltpu.VMEM((5,) + half, dtype),
        pltpu.VMEM(shape, f32),
        pltpu.SemaphoreType.DMA((4,)),
        pltpu.SemaphoreType.DMA((5, nz)),
        pltpu.SemaphoreType.DMA((5, nz)),
    ]


def reduce_task(place, src, out, scratch):
    acc, other, box, total, one, send, recv = scratch
    kind = acc.dtype
    b, z, c, nz = place.b, place.z, place.c, place.nz
    bx, by, bd = place.x_peer[0], place.y_peer[0], lax.bitwise_xor(b, 3)
    far, via_x, via_y, up, down = range(5)

    def add(target, lane, shard):
        acc[target, shard] = (
            acc[target, shard].astype(f32) + box[lane, shard].astype(f32)
        ).astype(kind)

    def move(part, shard, lane, peer):
        return remote(acc.at[part, shard], box.at[lane, shard], send.at[lane, shard], recv.at[lane, shard], peer)

    mine = pltpu.make_async_copy(src.at[:, :, c], acc, one.at[0])
    core = remote(src.at[:, :, 1 - c], other, one.at[1], one.at[2], place.core_peer)
    core.start()
    mine.start()
    yield
    mine.wait()
    core.wait()

    @pl.loop(0, 4 * nz)
    def _(i):
        part, shard = lax.div(i, nz), lax.rem(i, nz)
        acc[part, shard] = (
            acc[part, shard].astype(f32) + other[part, shard].astype(f32)
        ).astype(kind)

    for shard in range(nz):
        if shard % 2 == 0:
            move(bd, shard, far, place.x_peer).start()
            move(bx, shard, via_x, place.x_peer).start()
        else:
            move(bd, shard, far, place.y_peer).start()
            move(by, shard, via_y, place.y_peer).start()
    yield
    for shard in range(nz):
        move(bd, shard, far, place.x_peer).wait_recv()
        if shard % 2 == 0:
            add(by, far, shard)
            move(by, shard, via_y, place.y_peer).start()
        else:
            add(bx, far, shard)
            move(bx, shard, via_x, place.x_peer).start()
    yield
    for shard in range(nz):
        move(bx, shard, via_x, place.x_peer).wait_recv()
        move(by, shard, via_y, place.y_peer).wait_recv()
        acc[b, shard] = (
            acc[b, shard].astype(f32) + box[via_x, shard].astype(f32) + box[via_y, shard].astype(f32)
        ).astype(kind)
    yield
    for shard in reversed(range(nz)):

        @pl.when(z < shard)
        def _():
            @pl.when(z > 0)
            def _():
                move(b, shard, up, place.up_peer).wait_recv()
                add(b, up, shard)

            move(b, shard, up, place.up_peer).start()

    for shard in range(nz):

        @pl.when(z > shard)
        def _():
            @pl.when(z + 1 < nz)
            def _():
                move(b, shard, down, place.down_peer).wait_recv()
                add(b, down, shard)

            move(b, shard, down, place.down_peer).start()

    yield
    total[...] = acc[b, z].astype(f32)

    @pl.when(z > 0)
    def _():
        move(b, z, up, place.up_peer).wait_recv()
        total[...] += box[up, z].astype(f32)

    @pl.when(z + 1 < nz)
    def _():
        move(b, z, down, place.down_peer).wait_recv()
        total[...] += box[down, z].astype(f32)

    result = pltpu.make_async_copy(total, out, one.at[3])
    result.start()
    for shard in range(nz):
        for lane in (far, via_x, via_y):
            move(b, shard, lane, place.x_peer).wait_send()
        pl.when(z < shard)(lambda: move(b, shard, up, place.up_peer).wait_send())
        pl.when(z > shard)(lambda: move(b, shard, down, place.down_peer).wait_send())
    result.wait()
    yield


def reduce_kernel(ns, count, *refs):
    srcs, outs, scratch = refs[:count], refs[count : 2 * count], refs[2 * count :]
    place = Place(ns)
    greet(place, False)
    run_staggered(
        reduce_task(place, srcs[i], outs[i], scratch[7 * i : 7 * i + 7]) for i in range(count)
    )


def total_scratch(nz, shape, shared):
    return [
        pltpu.VMEM((3,) + shape, f32),
        pltpu.VMEM((2,) + shape, f32),
        pltpu.VMEM((2, nz, shared, LANES), f32),
        pltpu.SemaphoreType.DMA((2, 3)),
        pltpu.SemaphoreType.DMA((2, nz)),
    ]


def total_task(place, src, out, scratch):
    box, sums, lines, pair, chain = scratch
    z, c, nz = place.z, place.c, place.nz
    rows = src.shape[0]
    shared = lines.shape[2]
    tail = pl.ds(rows - shared, shared)

    def swap(source, dst, i, peer):
        return remote(source, dst, pair.at[0, i], pair.at[1, i], peer)

    first = swap(src, box.at[0], 0, place.x_peer)
    first.start()
    yield
    first.wait()
    sums[0] = src[...] + box[0]
    second = swap(sums.at[0], box.at[1], 1, place.y_peer)
    second.start()
    yield
    second.wait()
    sums[1] = sums[0] + box[1]
    third = swap(sums.at[1, tail], box.at[2, tail], 2, place.core_peer)
    third.start()
    yield
    third.wait()
    lines[0, z] = sums[1, tail] + box[2, tail]

    def along(step):
        peer = lax.rem(z + step, nz)
        return remote(lines.at[0, z], lines.at[1, z], chain.at[0, step], chain.at[1, step], (place.b, 2 * peer + c))

    for step in range(1, nz):
        along(step).start()
    lines[1, z] = lines[0, z]
    yield
    for step in range(1, nz):
        along(step).wait_recv()
    value = lines[1, 0]
    for shard in range(1, nz):
        value = value + lines[1, shard]
    out[: rows - shared] = sums[1, : rows - shared]
    out[tail] = value
    for step in range(1, nz):
        along(step).wait_send()
    yield


def last_kernel(ns, count, *refs):
    srcs, payload = refs[:count], refs[count]
    outs, totals = refs[count + 1 : 2 * count + 1], refs[2 * count + 1]
    scratch = refs[2 * count + 2 :]
    place = Place(ns)
    greet(place, True)
    tasks = [reduce_task(place, srcs[i], outs[i], scratch[7 * i : 7 * i + 7]) for i in range(count)]
    run_staggered([total_task(place, payload, totals, scratch[7 * count :])] + tasks)


def last_reduce(arrays, payload, shared, collective_id):
    nb, ns = lax.axis_size("batch"), lax.axis_size("seq")
    nz = ns // 2
    count = len(arrays)
    scratch = []
    for a in arrays:
        scratch.extend(reduce_scratch(nz, a.shape[1:], a.dtype))
    scratch.extend(total_scratch(nz, payload.shape, shared))
    hbm = pl.BlockSpec(memory_space=pl.ANY)
    *summed, totals = pl.pallas_call(
        functools.partial(last_kernel, ns, count),
        out_shape=[jax.ShapeDtypeStruct(a.shape[1:], f32) for a in arrays]
        + [jax.ShapeDtypeStruct(payload.shape, f32)],
        in_specs=[hbm] * count + whole(1),
        out_specs=[hbm] * count + whole(1),
        scratch_shapes=scratch,
        compiler_params=pltpu.CompilerParams(
            collective_id=collective_id, has_side_effects=True, vmem_limit_bytes=VMEM_LIMIT
        ),
        name="last_reduce",
    )(*[a.reshape((nb, nz, 2) + a.shape[1:]) for a in arrays], payload)
    return summed, totals


def reduce_scatter(arrays, collective_id):
    nb, ns = lax.axis_size("batch"), lax.axis_size("seq")
    nz = ns // 2
    count = len(arrays)
    scratch = []
    for a in arrays:
        scratch.extend(reduce_scratch(nz, a.shape[1:], a.dtype))
    return pl.pallas_call(
        functools.partial(reduce_kernel, ns, count),
        out_shape=[jax.ShapeDtypeStruct(a.shape[1:], f32) for a in arrays],
        in_specs=[pl.BlockSpec(memory_space=pl.ANY)] * count,
        out_specs=[pl.BlockSpec(memory_space=pl.ANY)] * count,
        scratch_shapes=scratch,
        compiler_params=pltpu.CompilerParams(
            collective_id=collective_id, has_side_effects=True, vmem_limit_bytes=VMEM_LIMIT
        ),
        name="reduce_grads",
    )(*[a.reshape((nb, nz, 2) + a.shape[1:]) for a in arrays])


def conv_lanes(value, rim_near, rim_far):
    lane = lax.broadcasted_iota(jnp.int32, value.shape, 1)
    near = jnp.where(lane == 0, rim_near, pltpu.roll(value, 1, 1))
    far = jnp.where(lane == 0, rim_far, jnp.where(lane == 1, rim_near, pltpu.roll(value, 2, 1)))
    return near, far


def short_out(mixed, aux, stream, block):
    value = mixed[stream, block].astype(f32)
    side = aux[stream, block]
    near, far = conv_lanes(value, side[:, 3:4], side[:, 4:5])
    return side[:, 0:1] * far + side[:, 1:2] * near + side[:, 2:3] * value


def rows_of(refs, group, index):
    return [ref[group, index] for ref in refs]


def sub_rows(chans):
    return 16 if chans % 16 == 0 else chans


def seq_send(place, ns, step, src_of, dst, send, recv):
    peer = lax.rem(place.s + step, ns)
    return remote(src_of(peer), dst, send, recv, (place.b, peer))


def mix_kernel(ns, groups, mixed, aux, spec_re, spec_im, skip, *refs):
    tables = refs[:10]
    long_out, gated, sig_re, sig_im = refs[10:14]
    signal, chan_in, chan_out, tok_in, send, recv = refs[14:]
    place = Place(ns)
    quarters = signal.shape[2]
    chans = signal.shape[3]
    take = sub_rows(chans)
    greet(place, True)

    def to_chan(g, step):
        peer = lax.rem(place.s + step, ns)
        return remote(
            signal.at[peer, g],
            chan_in.at[g, pl.ds(place.s * quarters, quarters)],
            send.at[0, g, step],
            recv.at[0, g, step],
            (place.b, peer),
        )

    def to_tok(g, step):
        peer = lax.rem(place.s + step, ns)
        return remote(
            chan_out.at[g, pl.ds(peer * quarters, quarters)],
            tok_in.at[place.s, g],
            send.at[1, g, step],
            recv.at[1, g, step],
            (place.b, peer),
        )

    for g in range(groups):

        @pl.loop(1, ns + 1)
        def _(step):
            peer = lax.rem(place.s + step, ns)
            block = peer * groups + g
            value = (
                short_out(mixed, aux, 1, block) * short_out(mixed, aux, 2, block)
            ).astype(bf16)

            @pl.when(step < ns)
            def _():
                for q in range(quarters):
                    signal[peer, g, q] = value[:, q * LANES : (q + 1) * LANES]
                to_chan(g, step).start()

            @pl.when(step == ns)
            def _():
                for q in range(quarters):
                    chan_in[g, place.s * quarters + q] = value[:, q * LANES : (q + 1) * LANES]

    for g in range(groups):

        @pl.loop(1, ns)
        def _(step):
            to_chan(g, step).wait_recv()

        @pl.loop(0, chans // take)
        def _(i):
            at = pl.ds(pl.multiple_of(i * take, take), take)
            block = chan_in[g, :, at, :].astype(f32)
            parts = []
            for j in range(take // 8):
                index = (g * chans) // 8 + i * (take // 8) + j
                x = block[:, 8 * j : 8 * j + 8, :]
                re, im = to_points(x, tables, True)
                sig_re[index] = re
                sig_im[index] = im
                tap_re, tap_im = spec_re[index], spec_im[index]
                y = from_points(re * tap_re - im * tap_im, re * tap_im + im * tap_re, tables)
                parts.append(y + skip[index][None] * x)
            chan_out[g, :, at, :] = jnp.concatenate(parts, axis=1).astype(bf16)

        @pl.loop(1, ns)
        def _(step):
            to_tok(g, step).start()

        for q in range(quarters):
            tok_in[place.s, g, q] = chan_out[g, place.s * quarters + q]

    for g in range(groups):

        @pl.loop(1, ns)
        def _(step):
            to_tok(g, step).wait_recv()

        @pl.loop(0, ns)
        def _(owner):
            block = owner * groups + g
            value = jnp.concatenate([tok_in[owner, g, q] for q in range(quarters)], axis=1)
            long_out[block] = value
            gated[block] = (short_out(mixed, aux, 0, block) * value.astype(f32)).astype(bf16)

    for g in range(groups):

        @pl.loop(1, ns)
        def _(step):
            to_chan(g, step).wait_send()
            to_tok(g, step).wait_send()


def whole(count):
    return [pl.BlockSpec(memory_space=pltpu.VMEM)] * count


def mix(mixed, aux, spec, skip, tables, collective_id):
    ns = lax.axis_size("seq")
    _, nblocks, chans, toks = mixed.shape
    groups, quarters = nblocks // ns, toks // LANES
    n1 = ns * quarters
    rows = (groups * chans // 8, n1 * 8, LANES)
    pieces = (ns, groups, quarters, chans, LANES)
    lines = (groups, n1, chans, LANES)
    return pl.pallas_call(
        functools.partial(mix_kernel, ns, groups),
        out_shape=[
            jax.ShapeDtypeStruct((nblocks, chans, toks), bf16),
            jax.ShapeDtypeStruct((nblocks, chans, toks), bf16),
            jax.ShapeDtypeStruct(rows, f32),
            jax.ShapeDtypeStruct(rows, f32),
        ],
        in_specs=whole(15),
        out_specs=whole(4),
        scratch_shapes=[
            pltpu.VMEM(pieces, bf16),
            pltpu.VMEM(lines, bf16),
            pltpu.VMEM(lines, bf16),
            pltpu.VMEM(pieces, bf16),
            pltpu.SemaphoreType.DMA((2, groups, ns)),
            pltpu.SemaphoreType.DMA((2, groups, ns)),
        ],
        compiler_params=pltpu.CompilerParams(
            collective_id=collective_id, has_side_effects=True, vmem_limit_bytes=VMEM_LIMIT
        ),
        name="mix",
    )(mixed, aux, spec[0], spec[1], skip, *tables)


def unmix_kernel(ns, groups, mixed, aux, long_out, grad_gated, spec_re, spec_im, sig_re, sig_im, skip, *refs):
    tables = refs[:10]
    grad_taps, grad_short, grad_conv = refs[10:13]
    pull, chan_in, chan_out, tok_in, send, recv = refs[13:]
    place = Place(ns)
    quarters = pull.shape[2]
    chans = pull.shape[3]
    take = sub_rows(chans)
    greet(place, True)

    def to_chan(g, step):
        peer = lax.rem(place.s + step, ns)
        return remote(
            pull.at[peer, g],
            chan_in.at[g, pl.ds(place.s * quarters, quarters)],
            send.at[0, g, step],
            recv.at[0, g, step],
            (place.b, peer),
        )

    def to_tok(g, step):
        peer = lax.rem(place.s + step, ns)
        return remote(
            chan_out.at[g, pl.ds(peer * quarters, quarters)],
            tok_in.at[place.s, g],
            send.at[1, g, step],
            recv.at[1, g, step],
            (place.b, peer),
        )

    for g in range(groups):

        @pl.loop(1, ns + 1)
        def _(step):
            peer = lax.rem(place.s + step, ns)
            block = peer * groups + g
            value = (grad_gated[block] * short_out(mixed, aux, 0, block)).astype(bf16)

            @pl.when(step < ns)
            def _():
                for q in range(quarters):
                    pull[peer, g, q] = value[:, q * LANES : (q + 1) * LANES]
                to_chan(g, step).start()

            @pl.when(step == ns)
            def _():
                for q in range(quarters):
                    chan_in[g, place.s * quarters + q] = value[:, q * LANES : (q + 1) * LANES]

    for g in range(groups):

        @pl.loop(1, ns)
        def _(step):
            to_chan(g, step).wait_recv()

        @pl.loop(0, chans // take)
        def _(i):
            at = pl.ds(pl.multiple_of(i * take, take), take)
            block = chan_in[g, :, at, :].astype(f32)
            parts = []
            for j in range(take // 8):
                index = (g * chans) // 8 + i * (take // 8) + j
                x = block[:, 8 * j : 8 * j + 8, :]
                re, im = to_points(x, tables, True)
                tap_re, tap_im = spec_re[index], spec_im[index]
                y = from_points(tap_re * re + tap_im * im, tap_re * im - tap_im * re, tables)
                parts.append(y + skip[index][None] * x)
                own_re, own_im = sig_re[index], sig_im[index]
                grad_taps[index] = from_points(
                    own_re * re + own_im * im, own_re * im - own_im * re, tables
                )
            chan_out[g, :, at, :] = jnp.concatenate(parts, axis=1).astype(bf16)

        @pl.loop(1, ns)
        def _(step):
            to_tok(g, step).start()

        for q in range(quarters):
            tok_in[place.s, g, q] = chan_out[g, place.s * quarters + q]

    def backward(stream, block, grad):
        grad_short[stream, block] = grad
        value = mixed[stream, block].astype(f32)
        side = aux[stream, block]
        near, far = conv_lanes(value, side[:, 3:4], side[:, 4:5])
        sums = [jnp.sum(grad * v, axis=1, keepdims=True) for v in (far, near, value)]
        lane = lax.broadcasted_iota(jnp.int32, side.shape, 1)
        grad_conv[stream, block] = jnp.where(
            lane == 0, sums[0], jnp.where(lane == 1, sums[1], jnp.where(lane == 2, sums[2], 0.0))
        )

    @pl.loop(0, ns * groups)
    def _(block):
        backward(0, block, grad_gated[block] * long_out[block].astype(f32))

    for g in range(groups):

        @pl.loop(1, ns)
        def _(step):
            to_tok(g, step).wait_recv()

        @pl.loop(0, ns)
        def _(owner):
            block = owner * groups + g
            value = jnp.concatenate(
                [tok_in[owner, g, q] for q in range(quarters)], axis=1
            ).astype(f32)
            backward(1, block, value * short_out(mixed, aux, 2, block))
            backward(2, block, value * short_out(mixed, aux, 1, block))

    for g in range(groups):

        @pl.loop(1, ns)
        def _(step):
            to_chan(g, step).wait_send()
            to_tok(g, step).wait_send()


def unmix(mixed, aux, long_out, grad_gated, spec, sig, skip, tables, collective_id):
    ns = lax.axis_size("seq")
    _, nblocks, chans, toks = mixed.shape
    groups, quarters = nblocks // ns, toks // LANES
    n1 = ns * quarters
    pieces = (ns, groups, quarters, chans, LANES)
    lines = (groups, n1, chans, LANES)
    return pl.pallas_call(
        functools.partial(unmix_kernel, ns, groups),
        out_shape=[
            jax.ShapeDtypeStruct((groups * chans // 8, n1, 8, LANES), f32),
            jax.ShapeDtypeStruct(mixed.shape, f32),
            jax.ShapeDtypeStruct(aux.shape, f32),
        ],
        in_specs=whole(19),
        out_specs=whole(3),
        scratch_shapes=[
            pltpu.VMEM(pieces, bf16),
            pltpu.VMEM(lines, bf16),
            pltpu.VMEM(lines, bf16),
            pltpu.VMEM(pieces, bf16),
            pltpu.SemaphoreType.DMA((2, groups, ns)),
            pltpu.SemaphoreType.DMA((2, groups, ns)),
        ],
        compiler_params=pltpu.CompilerParams(
            collective_id=collective_id, has_side_effects=True, vmem_limit_bytes=VMEM_LIMIT
        ),
        name="unmix",
    )(mixed, aux, long_out, grad_gated, spec[0], spec[1], sig[0], sig[1], skip, *tables)


def short_back_kernel(grad_short, aux, grad_mixed):
    toks = grad_short.shape[3]

    @pl.loop(0, grad_short.shape[1])
    def _(block):
        value = grad_short[0, block]
        side = aux[0, block]
        lane = lax.broadcasted_iota(jnp.int32, value.shape, 1)
        near = jnp.where(lane == toks - 1, side[:, 3:4], pltpu.roll(value, toks - 1, 1))
        far = jnp.where(
            lane == toks - 1,
            side[:, 4:5],
            jnp.where(lane == toks - 2, side[:, 3:4], pltpu.roll(value, toks - 2, 1)),
        )
        grad_mixed[0, block] = (
            side[:, 2:3] * value + side[:, 1:2] * near + side[:, 0:1] * far
        ).astype(bf16)


def short_back(grad_short, aux):
    streams, nblocks, chans, toks = grad_short.shape
    at = lambda k: (k, 0, 0, 0)
    return pl.pallas_call(
        short_back_kernel,
        grid=(streams,),
        out_shape=jax.ShapeDtypeStruct(grad_short.shape, bf16),
        in_specs=[
            pl.BlockSpec((1, nblocks, chans, toks), at),
            pl.BlockSpec((1, nblocks, chans, LANES), at),
        ],
        out_specs=pl.BlockSpec((1, nblocks, chans, toks), at),
        compiler_params=pltpu.CompilerParams(vmem_limit_bytes=VMEM_LIMIT),
        name="short_back",
    )(grad_short, aux)


def tap_points_kernel(taps, *refs):
    tables, (out_re, out_im) = refs[:10], refs[10:]
    n1, rows = out_re.shape[1] // 8, 8
    value = taps[...]
    x = jnp.concatenate(
        [value[:, i * LANES : (i + 1) * LANES][None] for i in range(n1)], axis=0
    )
    re, im = to_points(x, tables, False)
    out_re[0] = re
    out_im[0] = im


def tap_points(taps, tables):
    chans, length = taps.shape
    rows = length // LANES * 8
    full = lambda t: pl.BlockSpec(t.shape, lambda i: (0, 0))
    out = jax.ShapeDtypeStruct((chans // 8, rows, LANES), f32)
    return pl.pallas_call(
        tap_points_kernel,
        grid=(chans // 8,),
        out_shape=[out, out],
        in_specs=[pl.BlockSpec((8, length), lambda i: (i, 0))] + [full(t) for t in tables],
        out_specs=[pl.BlockSpec((1, rows, LANES), lambda i: (i, 0, 0))] * 2,
        compiler_params=pltpu.CompilerParams(vmem_limit_bytes=VMEM_LIMIT),
        name="tap_points",
    )(taps, *tables)


def side_table(conv, near, far):
    columns = jnp.concatenate([conv.T, near, far], axis=1)
    return jnp.pad(columns, ((0, 0), (0, LANES - 5)))


def on_device(
    tokens,
    cotangent,
    norm_gains,
    w_in,
    short_conv,
    w_out,
    w_fc,
    w_proj,
    filt_w1,
    filt_b1,
    filt_w2,
    filt_b2,
    filt_w3,
    skip_gain,
    decay_rate,
):
    layers, _, width3 = w_in.shape
    width = width3 // 3
    ns = lax.axis_size("seq")
    devices = lax.axis_size("batch") * ns
    stream = tokens[0].astype(f32)
    toks = stream.shape[0]
    length = toks * ns
    n1 = length // LANES
    own_chans = width // ns
    chans = 32 if own_chans % 32 == 0 else own_chans
    groups = own_chans // chans
    nblocks = ns * groups
    blocked = (3, nblocks, chans)
    tables = transform_tables(n1)
    pos_rows = position_rows(length, filt_w1.shape[1])

    gain_cols, conv_cols = norm_gains.shape[2], short_conv.shape[2]
    small = jnp.concatenate(
        [
            jnp.pad(norm_gains.reshape(2 * layers, gain_cols).astype(f32), ((0, 0), (0, LANES - gain_cols))),
            jnp.pad(short_conv.reshape(3 * layers, conv_cols).astype(f32), ((0, 0), (0, LANES - conv_cols))),
        ],
        axis=0,
    )
    small = jnp.pad(small, ((0, -small.shape[0] % 8), (0, 0)))[None]

    arrays, picks = [small], [0]
    for layer in range(layers):
        arrays += [w_in, w_out, w_fc, w_proj]
        picks += [layer] * 4
    gathered = gather(arrays, tuple(picks), 0)
    small_all = gathered[0]
    gains = jnp.swapaxes(small_all[:, : 2 * layers, :gain_cols], 0, 1).reshape(layers, 2, width)
    convs = jnp.swapaxes(
        small_all[:, 2 * layers : 5 * layers, :conv_cols], 0, 1
    ).reshape(layers, 3, width3)
    weights = []
    for layer in range(layers):
        in_mat, out_mat, fc_mat, proj_mat = gathered[1 + 4 * layer : 5 + 4 * layer]
        weights.append(
            (
                in_mat.reshape(width, width3),
                out_mat.reshape(width, width),
                fc_mat.reshape(width, -1),
                proj_mat.reshape(-1, width),
            )
        )

    make_taps = []
    specs = []
    skips = []
    for layer in range(layers):
        parts = (
            filt_w1[layer],
            filt_b1[layer],
            filt_w2[layer],
            filt_b2[layer],
            filt_w3[layer],
        )
        run = lambda *p, layer=layer: filter_forward(pos_rows, *p, decay_rate[layer])
        taps, pull = jax.vjp(run, *parts)
        make_taps.append(pull)
        specs.append(tap_points(taps, tables))
        skips.append(
            jnp.broadcast_to(skip_gain[layer].reshape(-1, 8, 1), (own_chans // 8, 8, LANES))
        )

    saved = []
    for layer in range(layers):
        in_mat, out_mat, fc_mat, proj_mat = weights[layer]
        normed, inv_std = layer_norm_parts(stream)
        norm_in = (normed * gains[layer, 0]).astype(bf16)
        mixed = contract(in_mat, norm_in, 0, 1).astype(bf16)
        rim = shifted(mixed[:, -2:], "seq", 1).astype(f32)
        aux = side_table(convs[layer], rim[:, 1:2], rim[:, 0:1]).reshape(blocked + (LANES,))
        mixed = mixed.reshape(blocked + (toks,))
        long_out, gated, sig_re, sig_im = mix(
            mixed, aux, specs[layer], skips[layer], tables, 1 + layer
        )
        gated = gated.reshape(width, toks)
        middle = stream + contract(gated, out_mat, 0, 0)
        normed_mid, inv_mid = layer_norm_parts(middle)
        hidden_in = (normed_mid * gains[layer, 1]).astype(bf16)
        hidden_pre = product(hidden_in, fc_mat)
        hidden_act = jax.nn.gelu(hidden_pre).astype(bf16)
        saved.append(
            (normed, inv_std, norm_in, mixed, aux, long_out, gated, (sig_re, sig_im))
            + (normed_mid, inv_mid, hidden_in, hidden_pre, hidden_act)
        )
        stream = middle + product(hidden_act, proj_mat)
    mixed_out = stream.astype(bf16)

    grad = cotangent[0].astype(f32)
    block_grads = [None] * layers
    small_grads = [None] * layers
    for layer in reversed(range(layers)):
        in_mat, out_mat, fc_mat, proj_mat = weights[layer]
        (normed, inv_std, norm_in, mixed, aux, long_out, gated, sig) = saved[layer][:8]
        (normed_mid, inv_mid, hidden_in, hidden_pre, hidden_act) = saved[layer][8:]
        grad_top = grad.astype(bf16)
        grad_act = contract(grad_top, proj_mat, 1, 1)
        grad_proj = contract(hidden_act, grad_top, 0, 0).astype(bf16)
        grad_pre = jax.vjp(jax.nn.gelu, hidden_pre)[1](grad_act)[0].astype(bf16)
        grad_hidden = contract(grad_pre, fc_mat, 1, 1)
        grad_fc = contract(hidden_in, grad_pre, 0, 0).astype(bf16)
        grad_gain_mid = jnp.sum(grad_hidden * normed_mid, axis=0)
        grad_middle = grad + norm_back(grad_hidden * gains[layer, 1], normed_mid, inv_mid)
        grad_mix = grad_middle.astype(bf16)
        grad_gated = contract(out_mat, grad_mix, 1, 1).reshape(nblocks, chans, toks)
        grad_out = contract(gated, grad_mix, 1, 0).astype(bf16)
        grad_taps, grad_short, grad_conv = unmix(
            mixed, aux, long_out, grad_gated, specs[layer], sig, skips[layer], tables, 3 + layer
        )
        rim = shifted(grad_short[..., :2], "seq", -1)
        back_aux = side_table(
            convs[layer], rim[..., 0].reshape(-1, 1), rim[..., 1].reshape(-1, 1)
        ).reshape(blocked + (LANES,))
        grad_mixed = short_back(grad_short, back_aux).reshape(width3, toks)
        grad_norm_in = contract(grad_mixed, in_mat, 0, 1)
        grad_in = contract(norm_in, grad_mixed, 0, 1).astype(bf16)
        grad_gain_in = jnp.sum(grad_norm_in * normed, axis=0)
        grad = grad_middle + norm_back(grad_norm_in * gains[layer, 0], normed, inv_std)
        block_grads[layer] = [
            g.reshape(devices, -1, g.shape[1]) for g in (grad_in, grad_out, grad_fc, grad_proj)
        ]
        taps_rows = jnp.swapaxes(grad_taps, 1, 2).reshape(own_chans, length)
        filter_grads = make_taps[layer](taps_rows)
        small_grads[layer] = (
            jnp.stack([grad_gain_in, grad_gain_mid]),
            jnp.swapaxes(grad_conv.reshape(width3, LANES)[:, :3], 0, 1),
            filter_grads,
            taps_rows[:, 0],
        )

    def rows_for(values, cols):
        pieces = jnp.swapaxes(values.reshape(values.shape[0], devices, cols), 0, 1)
        return jnp.pad(pieces, ((0, 0), (0, 0), (0, LANES - cols)))

    small_rows = jnp.concatenate(
        [rows_for(small_grads[layer][0], gain_cols) for layer in range(layers)]
        + [rows_for(small_grads[layer][1], conv_cols) for layer in range(layers)],
        axis=1,
    )
    small_rows = jnp.pad(small_rows, ((0, 0), (0, -small_rows.shape[1] % 8), (0, 0)))
    hidden = filt_w2.shape[1]
    emb = filt_w1.shape[1]
    payload = []
    for layer in range(layers):
        grad_w3, grad_skip = small_grads[layer][2][4], small_grads[layer][3]
        part = jnp.concatenate([grad_w3, grad_skip[None]], axis=0)
        payload.append(jnp.pad(part, ((0, 7), (0, LANES - own_chans))))
    for layer in range(layers):
        first_w, first_b, second_w, second_b = small_grads[layer][2][:4]
        part = jnp.concatenate([first_w, first_b[None], second_b[None]], axis=0)
        part = jnp.pad(part, ((0, hidden - part.shape[0]), (0, 0)))
        payload.append(jnp.concatenate([part, second_w], axis=1))
    payload = jnp.concatenate(payload, axis=0)

    summed = [None] * layers
    for layer in reversed(range(1, layers)):
        summed[layer] = reduce_scatter(block_grads[layer], 5 + layer)
    last, totals = last_reduce(block_grads[0] + [small_rows], payload, layers * hidden, 5)
    summed[0], small_sum = last[:-1], last[-1]
    columns = totals[: layers * (hidden + 8)].reshape(layers, hidden + 8, LANES)
    shared = totals[layers * (hidden + 8) :].reshape(layers, hidden, LANES)
    block = [jnp.stack([summed[layer][i] for layer in range(layers)]) for i in range(4)]
    gains_grad = small_sum[: 2 * layers, :gain_cols].reshape(layers, 2, gain_cols)
    conv_grad = small_sum[2 * layers : 5 * layers, :conv_cols].reshape(layers, 3, conv_cols)
    return (
        mixed_out[None],
        grad[None],
        gains_grad,
        block[0],
        conv_grad,
        block[1],
        block[2],
        block[3],
        shared[:, :emb, :hidden],
        shared[:, emb, :hidden],
        shared[:, :, hidden:],
        shared[:, emb + 1, :hidden],
        columns[:, :hidden, :own_chans],
        columns[:, hidden, :own_chans],
    )


def solution(mesh):
    both = ("batch", "seq")
    in_specs = (
        P("batch", "seq", None),
        P("batch", "seq", None),
        P(None, None, both),
        P(None, both, None),
        P(None, None, both),
        P(None, both, None),
        P(None, both, None),
        P(None, both, None),
        P(),
        P(),
        P(),
        P(),
        P(None, None, "seq"),
        P(None, "seq"),
        P(None, "seq"),
    )
    out_specs = in_specs[:14]
    return jax.shard_map(
        on_device, mesh=mesh, in_specs=in_specs, out_specs=out_specs, check_vma=False
    )
```

time: 2240 us -> 826 us (0.37)
  waiting for transfers between devices: 1070 us -> 0.01 us
  Pallas kernels: 0 us -> 591 us
  matrix products: 498 us -> 152 us
  blocking collectives: 244 us -> 0 us
  local copies, waits for them, and re-layouts: 282 us -> 40.8 us
  other arithmetic: 79.6 us -> 24.8 us
  starting transfers between devices: 35.1 us -> 7.42 us
    reduce_scatter x8 -> x0, waiting for transfers between devices: 1010 us -> none  [the longest x2 280 us: on_device(): lax.psum_scatter(block_grads[4], ('batch', 'seq'), scatter_dimension=0, t...]
    pallas_call x0 -> x11, Pallas kernels: none -> 591 us  [the longest x1 130 us: gather(): pl.pallas_call(functools.partial(gather_kernel, ns, picks), out_shape=[ja...]
    dot_general x112 -> x40, matrix products: 498 us -> 152 us  [the longest x20 80.2 us: contract(): lax.dot_general(left_mat, right_mat, (((left_dim,), (right_dim,)), ((), (...]
    all_gather x4 -> x0, blocking collectives: 181 us -> none  [the longest x2 93 us: on_device(): lax.all_gather(norm_gains[layer_idx], ('batch', 'seq'), axis=1, tiled=True)]
    slice x15 -> x30, local copies, waits for them, and re-layouts: 155 us -> 14.1 us  [the longest x4 3.7 us: on_device(): rim = shifted(grad_short[..., :2], 'seq', -1)]
    all_to_all x2 -> x0, blocking collectives: 48.2 us -> none  [the longest x1 24.4 us: layer_backward(): lax.all_to_all(grad_long, 'seq', split_axis=1, concat_axis=0, tiled=True)]
    div x12 -> x0, local copies, waits for them, and re-layouts: 38.4 us -> none  [inverse_real(): real_part.reshape(real_part.shape[0], half_len * inner_len)]
    unnamed x18 -> x0, waiting for transfers between devices: 37.9 us -> none
  transfers between devices with their start and end apart: 27 -> 4, of which waited for: 13 -> 0; matrix products, arithmetic and copies ran while one was open for 27% -> 4% of each run, Pallas kernels for 0% -> 16%
where the time goes in v1:
time: 826 us; the launch traced here: 818 us
  Pallas kernels  591 us (72%)
  matrix products  152 us (18%)
  local copies, waits for them, and re-layouts  40.8 us (5%)
  other arithmetic  24.8 us (3%)
    pallas_call x1, Pallas kernels, gather(): pl.pallas_call(functools.partial(gather_kernel, ns, picks), out_shape=[ja...  130 us
    pallas_call x2, Pallas kernels, unmix(): pl.pallas_call(functools.partial(unmix_kernel, ns, groups), out_shape=[ja...  115 us
    pallas_call x1, Pallas kernels, last_reduce(): pl.pallas_call(functools.partial(last_kernel, ns, count), out_shape=[jax....  104 us
    pallas_call x1, Pallas kernels, reduce_scatter(): pl.pallas_call(functools.partial(reduce_kernel, ns, count), out_shape=[ja...  102 us
    pallas_call x2, Pallas kernels, mix(): pl.pallas_call(functools.partial(mix_kernel, ns, groups), out_shape=[jax....  89.9 us
    dot_general x20, matrix products, contract(): lax.dot_general(left_mat, right_mat, (((left_dim,), (right_dim,)), ((), (...  80.2 us
    pallas_call x2, Pallas kernels, tap_points(): pl.pallas_call(tap_points_kernel, grid=(chans // 8,), out_shape=[out, out...  25.1 us
    pallas_call x2, Pallas kernels, short_back(): pl.pallas_call(short_back_kernel, grid=(streams,), out_shape=jax.ShapeDty...  24.7 us
  transfers between devices with their start and end apart: 4, of which 0 were waited for; matrix products, arithmetic and copies ran while one was open for 4% of the time, Pallas kernels for 16%

profile of v1, /device:TPU:0, one launch (start us, length us, event | category | flops | bytes accessed | tf_op | source)
XLA Modules:
  0.0 818.5 jit_solution(6948447235835580971)
XLA Ops:
  4.9 129.8 %gather_weights.1 = (f32[4,4,2,16,128]{4,3,2,1,0:T(8,128)}, bf16[4,4,2,24,2304]{4,3,2,1,0:T(8,128)(2,1)}, bf16[4,4,2,24,768]{4,3,2,1,0:T(8,128)(2,1)}, bf16[4,4,...) custom-call(f32[1,16,128]{2,1,0:T(8,128)} %bitcast_convert_fusion.re, ...), custom_call_target="tpu_custom_call" | custom-call | tf_op jit(solution)/shard_map/gather_weights/pallas_call | solution.py:303
  145.1 5.9 fusion.103
  151.0 5.3 fusion.104
  158.6 5.7 fusion.99
  164.3 5.3 fusion.100
  174.0 12.4 %tap_points.2 = (f32[12,256,128]{2,1,0:T(8,128)}, f32[12,256,128]{2,1,0:T(8,128)}) custom-call(f32[96,4096]{1,0:T(8,128)} %multiply_multiply_fusion.5.taps, bf16[512,256]{1,0:T(8,128)(2,1)} %constant.74.clone.refs_0_, bf16[512,256]{1,0:T(8,128)(2,1)} %constant.75.clone.refs_1_, bf16[256,256]{1,0:T(8,128)(2,1)} %constant.76.clone.refs_2_, ...), custom_call_target="tpu_custom_call" | custom-call | tf_op jit(solution)/shard_map/tap_points/pallas_call | solution.py:914
  191.0 44.4 %mix.2 = (bf16[24,32,512]{2,1,0:T(8,128)(2,1)}, bf16[24,32,512]{2,1,0:T(8,128)(2,1)}, f32[12,256,128]{2,1,0:T(8,128)}, f32[12,256,128]{2,1,0:T(8,128)}) custom-call(bf16[3,24,32,512]{3,2,1,0:T(8,128)(2,1)} %bitcast.286, f32[3,24,32,128]{3,2,1,0:T(8,128)} %bitcast.290, f32[12,256,128]{2,1,0:T(8,128)} %get-tuple-element.53.spec_re, ...), custom_call_target="tpu_custom_call" | custom-call | tf_op jit(solution)/shard_map/mix/pallas_call | solution.py:687
  237.8 5.4 fusion.84
  257.4 12.6 %tap_points.3 = (f32[12,256,128]{2,1,0:T(8,128)}, f32[12,256,128]{2,1,0:T(8,128)}) custom-call(f32[96,4096]{1,0:T(8,128)} %multiply_multiply_fusion.4.taps, bf16[512,256]{1,0:T(8,128)(2,1)} %constant.74.clone.refs_0_, bf16[512,256]{1,0:T(8,128)(2,1)} %constant.75.clone.refs_1_, bf16[256,256]{1,0:T(8,128)(2,1)} %constant.76.clone.refs_2_, ...), custom_call_target="tpu_custom_call" | custom-call | tf_op jit(solution)/shard_map/tap_points/pallas_call | solution.py:914
  274.7 45.5 %mix.3 = (bf16[24,32,512]{2,1,0:T(8,128)(2,1)}, bf16[24,32,512]{2,1,0:T(8,128)(2,1)}, f32[12,256,128]{2,1,0:T(8,128)}, f32[12,256,128]{2,1,0:T(8,128)}) custom-call(bf16[3,24,32,512]{3,2,1,0:T(8,128)(2,1)} %bitcast.288, f32[3,24,32,128]{3,2,1,0:T(8,128)} %bitcast.292, f32[12,256,128]{2,1,0:T(8,128)} %get-tuple-element.60.spec_re, ...), custom_call_target="tpu_custom_call" | custom-call | tf_op jit(solution)/shard_map/mix/pallas_call | solution.py:687
  332.2 6.5 fusion.13
  338.7 4.9 convolution_convert_fusion
  356.4 55.5 %unmix.2 = (f32[12,32,8,128]{3,2,1,0:T(8,128)}, f32[3,24,32,512]{3,2,1,0:T(8,128)}, f32[3,24,32,128]{3,2,1,0:T(8,128)}) custom-call(bf16[3,24,32,512]{3,2,1,0:T(8,128)(2,1)} %bitcast.289, f32[3,24,32,128]{3,2,1,0:T(8,128)} %bitcast.293, bf16[24,32,512]{2,1,0:T(8,128)(2,1)} %get-tuple-element.66.long_out, f32[24,32,512]{2,1,0:T(8,128)} %fusion.42.grad_gated, ...), custom_call_target="tpu_custom_call" | custom-call | tf_op jit(solution)/shard_map/unmix/pallas_call | solution.py:837
  416.1 5.0 fusion.106
  436.1 12.3 %short_back.2 = bf16[3,24,32,512]{3,2,1,0:T(8,128)(2,1)} custom-call(f32[3,24,32,512]{3,2,1,0:T(8,128)} %get-tuple-element.69.grad_short, f32[3,24,32,128]{3,2,1,0:T(8,128)} %bitcast.300), custom_call_target="tpu_custom_call" | custom-call | tf_op jit(solution)/shard_map/short_back/pallas_call | solution.py:883
  448.5 5.3 multiply_reduce_fusion.3
  454.4 9.5 %fusion.6 = bf16[512,3072]{1,0:T(8,128)(2,1)S(1)} fusion(f32[512,3072]{1,0:T(8,128)} %copy-done.75, bf16[3072,768]{1,0:T(8,128)(2,1)} %bitcast.358, f32[512,768]{1,0:T(8,128)S(1)} %multiply_add_fusion.1), kind=kOutput, calls=%fused_computation.10 | convolution fusion | flops 2447769600 | bytes 15728640 | tf_op jit(solution)/shard_map/dot_general | solution.py:25
  464.0 5.1 convolution_convert_fusion.3
  490.0 59.9 %unmix.3 = (f32[12,32,8,128]{3,2,1,0:T(8,128)}, f32[3,24,32,512]{3,2,1,0:T(8,128)}, f32[3,24,32,128]{3,2,1,0:T(8,128)}) custom-call(bf16[3,24,32,512]{3,2,1,0:T(8,128)(2,1)} %bitcast.287, f32[3,24,32,128]{3,2,1,0:T(8,128)} %bitcast.291, bf16[24,32,512]{2,1,0:T(8,128)(2,1)} %get-tuple-element.70.long_out, f32[24,32,512]{2,1,0:T(8,128)} %fusion.40.grad_gated, ...), custom_call_target="tpu_custom_call" | custom-call | tf_op jit(solution)/shard_map/unmix/pallas_call | solution.py:837
  554.1 5.0 fusion.108
  571.8 102.5 %reduce_grads.1 = (f32[24,2304]{1,0:T(8,128)}, f32[24,768]{1,0:T(8,128)}, f32[24,3072]{1,0:T(8,128)}, f32[96,768]{1,0:T(8,128)}) custom-call(bf16[4,4,2,24,2304]{4,3,2,1,0:T(8,128)(2,1)} %bitcast.304, bf16[4,4,2,24,768]{4,3,2,1,0:T(8,128)(2,1)} %bitcast.294, bf16[4,4,2,24,3072]{4,3,2,1,0:T(8,128)(2,1)} %bitcast.297, bf16[4,4,2,96,768]{4,3,2,1,0:T(8,128)(2,1)} %bitcast.296), custom_call_target="tpu_custom_call" | custom-call | tf_op jit(solution)/shard_map/reduce_grads/pallas_call | solution.py:534
  676.0 12.4 %short_back.3 = bf16[3,24,32,512]{3,2,1,0:T(8,128)(2,1)} custom-call(f32[3,24,32,512]{3,2,1,0:T(8,128)} %get-tuple-element.73.grad_short, f32[3,24,32,128]{3,2,1,0:T(8,128)} %bitcast.301), custom_call_target="tpu_custom_call" | custom-call | tf_op jit(solution)/shard_map/short_back/pallas_call | solution.py:883
  688.4 5.4 fusion.31
  698.9 104.0 %last_reduce.1 = (f32[24,2304]{1,0:T(8,128)}, f32[24,768]{1,0:T(8,128)}, f32[24,3072]{1,0:T(8,128)}, f32[96,768]{1,0:T(8,128)}, f32[16,128]{1,0:T(8,128)}, /*index=5*/f32[272,128]{1,0:T(8,128)}) custom-call(bf16[4,4,2,24,2304]{4,3,2,1,0:T(8,128)(2,1)} %bitcast.305, bf16[4,4,2,24,768]{4,3,2,1,0:T(8,128)(2,1)} %bitcast.295, ...), custom_call_target="tpu_custom_call" | custom-call | tf_op jit(solution)/shard_map/last_reduce/pallas_call | solution.py:512
  (332 shorter events, 150.6 us)
Async XLA Ops:
  2.7 133.7 %copy-start.20 = (bf16[1,512,768]{2,1,0:T(8,128)(2,1)S(1)}, bf16[1,512,768]{2,1,0:T(8,128)(2,1)}, u32[]{:S(2)}) copy-start(bf16[1,512,768]{2,1,0:T(8,128)(2,1)} %param.26) | copy-start | bytes 2359300
  2.7 133.1 %copy-start.50 = (f32[512]{0:T(512)}, f32[512]{0:T(512)S(1)}, u32[]{:S(2)}) copy-start(f32[512]{0:T(512)S(1)} %broadcast_multiply_fusion.11) | copy-start | bytes 6148
  4.3 136.3 %copy-start.58 = (f32[512]{0:T(512)}, f32[512]{0:T(512)S(1)}, u32[]{:S(2)}) copy-start(f32[512]{0:T(512)S(1)} %add_rsqrt_fusion.3) | copy-start | bytes 6148
  135.8 111.7 %copy-start.54 = (f32[768]{0:T(1024)}, f32[768]{0:T(1024)S(1)}, u32[]{:S(2)}) copy-start(f32[768]{0:T(1024)S(1)} %get-tuple-element.143) | copy-start | bytes 9220
  142.5 43.9 %collective-permute-start = (bf16[2304,2]{0,1:T(2,128)(2,1)S(1)}, bf16[2304,2]{0,1:T(2,128)(2,1)S(1)}, u32[]{:S(2)}, u32[]{:S(2)}) collective-permute-start(bf16[2304,2]{0,1:T(2,128)(2,1)S(1)} %copy.71), channel_id=1, source_target_pairs={{0,1},{1,2},{2,3},{3,4},{4,5},{5,6},{6,7},{8,9},{9,10},{10,11},{11... | collective-permute-start | bytes 27656 | tf_op jit(solution)/shard_map/ppermute | solution.py:46
  145.0 24.6 %copy-start.56 = (f32[96]{0:T(128)}, f32[96]{0:T(128)S(1)}, u32[]{:S(2)}) copy-start(f32[96]{0:T(128)S(1)} %get-tuple-element.163) | copy-start | bytes 1156
  191.0 44.4 %copy-start.21 = (bf16[1,512,768]{2,1,0:T(8,128)(2,1)S(1)}, bf16[1,512,768]{2,1,0:T(8,128)(2,1)}, u32[]{:S(2)}) copy-start(bf16[1,512,768]{2,1,0:T(8,128)(2,1)} %param.26) | copy-start | bytes 2359300
  191.0 44.5 %copy-start.35 = (bf16[4,4,2,24,768]{4,3,2,1,0:T(8,128)(2,1)S(1)}, bf16[4,4,2,24,768]{4,3,2,1,0:T(8,128)(2,1)}, u32[]{:S(2)}) copy-start(bf16[4,4,2,24,768]{4,3,2,1,0:T(8,128)(2,1)} %get-tuple-element.56) | copy-start | bytes 3538948
  253.5 16.6 %collective-permute-start.1 = (bf16[2304,2]{0,1:T(2,128)(2,1)S(1)}, bf16[2304,2]{0,1:T(2,128)(2,1)S(1)}, u32[]{:S(2)}, u32[]{:S(2)}) collective-permute-start(bf16[2304,2]{0,1:T(2,128)(2,1)S(1)} %copy.75), channel_id=1, source_target_pairs={{0,1},{1,2},{2,3},{3,4},{4,5},{5,6},{6,7},{8,9},{9,10},{10,11},{11... | collective-permute-start | bytes 27656 | tf_op jit(solution)/shard_map/ppermute | solution.py:46
  274.7 45.5 %copy-start.5 = (f32[512,768]{1,0:T(8,128)S(1)}, f32[512,768]{1,0:T(8,128)}, u32[]{:S(2)}) copy-start(f32[512,768]{1,0:T(8,128)} %copy-done.4) | copy-start | bytes 4718596
  274.7 45.5 %copy-start.26 = (bf16[4,4,2,24,768]{4,3,2,1,0:T(8,128)(2,1)S(1)}, bf16[4,4,2,24,768]{4,3,2,1,0:T(8,128)(2,1)}, u32[]{:S(2)}) copy-start(bf16[4,4,2,24,768]{4,3,2,1,0:T(8,128)(2,1)} %get-tuple-element.63) | copy-start | bytes 3538948
  327.4 16.2 %slice-start.4 = ((s8[4718592]{0:T(1024)(128)(4,1)}), s8[4194304]{0:T(1024)(128)(4,1)S(1)}, s32[]{:S(2)}) async-start(s8[4718592]{0:T(1024)(128)(4,1)} %bitcast.363), calls=%async_computation.4 | async-start | bytes 8388608
  430.0 4.4 collective-permute-start.2
  436.1 12.3 %copy-start.55 = (f32[768]{0:T(1024)S(1)}, f32[768]{0:T(1024)}, u32[]{:S(2)}) copy-start(f32[768]{0:T(1024)} %copy-done.54) | copy-start | bytes 9220
  436.1 12.3 %copy-start.63 = (f32[512]{0:T(512)S(1)}, f32[512]{0:T(512)}, u32[]{:S(2)}) copy-start(f32[512]{0:T(512)} %copy-done.62) | copy-start | bytes 6148
  454.4 18.7 %slice-start = ((s8[4718592]{0:T(1024)(128)(4,1)}), s8[4194304]{0:T(1024)(128)(4,1)S(1)}, s32[]{:S(2)}) async-start(s8[4718592]{0:T(1024)(128)(4,1)} %bitcast.355), calls=%async_computation | async-start | bytes 8388608
  567.8 106.4 %collective-permute-start.3 = (f32[3,24,32,2]{2,1,3,0:T(8,128)S(1)}, f32[3,24,32,2]{2,1,3,0:T(8,128)S(1)}, u32[]{:S(2)}, u32[]{:S(2)}) collective-permute-start(f32[3,24,32,2]{2,1,3,0:T(8,128)S(1)} %copy.81), channel_id=1, source_target_pairs={{1,0},{2,1},{3,2},{4,3},{5,4},{6,5},{7,6},{9,8},{10,9},{11,10},{12... | collective-permute-start | bytes 55304 | tf_op jit(solution)/shard_map/ppermute | solution.py:46
  676.0 12.4 %copy-start.22 = (bf16[1,512,768]{2,1,0:T(8,128)(2,1)S(1)}, bf16[1,512,768]{2,1,0:T(8,128)(2,1)}, u32[]{:S(2)}) copy-start(bf16[1,512,768]{2,1,0:T(8,128)(2,1)} %param.26) | copy-start | bytes 2359300
  676.0 12.4 %copy-start.51 = (f32[512]{0:T(512)S(1)}, f32[512]{0:T(512)}, u32[]{:S(2)}) copy-start(f32[512]{0:T(512)} %copy-done.50) | copy-start | bytes 6148
  676.0 12.4 %copy-start.53 = (f32[768]{0:T(1024)S(1)}, f32[768]{0:T(1024)}, u32[]{:S(2)}) copy-start(f32[768]{0:T(1024)} %copy-done.52) | copy-start | bytes 9220
  676.0 12.4 %copy-start.59 = (f32[512]{0:T(512)S(1)}, f32[512]{0:T(512)}, u32[]{:S(2)}) copy-start(f32[512]{0:T(512)} %copy-done.58) | copy-start | bytes 6148
  676.0 12.4 %copy-start.73 = (bf16[4,4,2,24,2304]{4,3,2,1,0:T(8,128)(2,1)S(1)}, bf16[4,4,2,24,2304]{4,3,2,1,0:T(8,128)(2,1)}, u32[]{:S(2)}) copy-start(bf16[4,4,2,24,2304]{4,3,2,1,0:T(8,128)(2,1)} %get-tuple-element.51) | copy-start | bytes 10616836
  802.9 12.8 %copy-start.39 = (f32[96,768]{1,0:T(8,128)S(1)}, f32[96,768]{1,0:T(8,128)}, u32[]{:S(2)}) copy-start(f32[96,768]{1,0:T(8,128)} %get-tuple-element.86) | copy-start | bytes 884740
  802.9 12.8 %copy-start.41 = (f32[96,768]{1,0:T(8,128)S(1)}, f32[96,768]{1,0:T(8,128)}, u32[]{:S(2)}) copy-start(f32[96,768]{1,0:T(8,128)} %get-tuple-element.85) | copy-start | bytes 884740
  (66 other events, 290.3 us)

commit v2 on v1

v2 whole, which is shorter than its diff:
```python
import functools
import itertools
import math

import jax
import jax.numpy as jnp
import numpy as np
from jax import lax
from jax.experimental import pallas as pl
from jax.experimental.pallas import tpu as pltpu
from jax.sharding import PartitionSpec as P

MESH = pl.DeviceIdType.MESH
LANES = 128
VMEM_LIMIT = 58 * 1024 * 1024
GATHER_PLANS = [[0, 1, 3, 5, 7, 9, 12], [0, 1, 3, 5, 7, 9, 12], [0, 2, 4, 6, 8, 10, 12], [0, 2, 5, 8, 10, 12, 14], [0, 3, 6, 9, 12, 14, 16]]
COLUMN_PLANS = [[2, 5, 8, 11, 14], [2, 5, 8, 11, 14], [3, 7, 10, 13, 15], [4, 8, 12, 14, 16]]
PLANE_PLANS = [[0, 3, 5, 7], [0, 4, 6, 8], [2, 6, 8, 10]]
REDUCE_PLANS = [[0, 1, 2, 4, 5, 7, 8, 12], [0, 3, 4, 6, 7, 9, 10, 12], [0, 5, 6, 8, 9, 11, 12, 13]]
LAST_PLANS = [[0, 1, 1, 2, 2, 3, 3, 5], [0, 1, 1, 3, 3, 5, 5, 7], [0, 2, 2, 4, 5, 7, 8, 9]]
f32 = jnp.float32
bf16 = jnp.bfloat16


def product(left_mat, right_mat):
    return jnp.dot(left_mat, right_mat, preferred_element_type=f32)


def contract(left_mat, right_mat, left_dim, right_dim):
    return lax.dot_general(
        left_mat, right_mat, (((left_dim,), (right_dim,)), ((), ())), preferred_element_type=f32
    )


def layer_norm_parts(stream):
    mean_val = jnp.mean(stream, axis=-1, keepdims=True)
    centered = stream - mean_val
    inv_std = lax.rsqrt(jnp.mean(centered * centered, axis=-1, keepdims=True) + 1e-05)
    return (centered * inv_std, inv_std)


def norm_back(grad_normed, normed, inv_std):
    mean_grad = jnp.mean(grad_normed, axis=-1, keepdims=True)
    mean_cross = jnp.mean(grad_normed * normed, axis=-1, keepdims=True)
    return inv_std * (grad_normed - mean_grad - normed * mean_cross)


def split_bf16(table):
    high = table.astype(np.float32).astype(jnp.bfloat16)
    return high, (table - high.astype(np.float64)).astype(np.float32).astype(jnp.bfloat16)


def transform_tables(length):
    blocks = min(length // LANES, 32)
    inside = length // blocks
    n1 = np.arange(blocks)
    n2 = np.arange(inside)
    outer = 2 * np.pi * ((n1[:, None] * (4 * n1[None, :] + 1)) % (4 * blocks)) / (4 * blocks)
    eye = np.eye(8)
    forward = np.concatenate([np.cos(outer).T, -np.sin(outer).T], axis=0)
    left_fwd = np.kron(forward, eye)
    left_inv = np.kron(np.concatenate([np.cos(outer), -np.sin(outer)], axis=1), eye) / length
    inner = 2 * np.pi * ((n2[:, None] * n2[None, :]) % inside) / inside
    cos2, sin2 = np.cos(inner), np.sin(inner)
    right_fwd = np.block([[cos2, -sin2], [sin2, cos2]])
    right_inv = np.block([[cos2, sin2], [-sin2, cos2]])
    twist = 2 * np.pi * (n2[None, :] * (4 * n1[:, None] + 1)) / (4 * length)
    twist_cos = np.repeat(np.cos(twist), 8, axis=0).astype(np.float32)
    twist_sin = np.repeat(np.sin(twist), 8, axis=0).astype(np.float32)
    tables = []
    for table, axis in ((left_fwd, 1), (right_fwd, 0), (left_inv, 1), (right_inv, 0)):
        high, low = split_bf16(table)
        tables.append(jnp.asarray(np.concatenate([high, low, high], axis=axis)))
    return tuple(tables) + (jnp.asarray(twist_cos), jnp.asarray(twist_sin))


TABLES = 6


def in_two(value):
    high = value.astype(bf16)
    return high, (value - high.astype(f32)).astype(bf16)


def left_product(left, right):
    high, low = in_two(right)
    return product(left[...], jnp.concatenate([high, high, low], axis=0))


def right_product(left, right):
    high, low = in_two(left)
    return product(jnp.concatenate([high, high, low], axis=1), right[...])


def to_points(x, tables, exact):
    left, right, _, _, twist_cos, twist_sin = tables
    rows, inside = twist_cos.shape
    split = x.reshape(rows // 8, inside // LANES, 8, LANES)
    flat = jnp.concatenate([split[:, k] for k in range(inside // LANES)], axis=2).reshape(rows, inside)
    if exact:
        flat = flat.astype(bf16)
        turned = product(left[:, : 2 * rows], jnp.concatenate([flat, flat], axis=0))
    else:
        turned = left_product(left, flat)
    re, im = turned[:rows], turned[rows:]
    cos, sin = twist_cos[...], twist_sin[...]
    both = jnp.concatenate([re * cos + im * sin, im * cos - re * sin], axis=1)
    points = right_product(both, right)
    return points[:, :inside], points[:, inside:]


def from_points(re, im, tables):
    _, _, left, right, twist_cos, twist_sin = tables
    rows, inside = twist_cos.shape
    back = right_product(jnp.concatenate([re, im], axis=1), right)
    re, im = back[:, :inside], back[:, inside:]
    cos, sin = twist_cos[...], twist_sin[...]
    both = jnp.concatenate([re * cos - im * sin, re * sin + im * cos], axis=0)
    flat = left_product(left, both).reshape(rows // 8, 8, inside)
    split = [flat[:, None, :, k * LANES : (k + 1) * LANES] for k in range(inside // LANES)]
    return jnp.concatenate(split, axis=1).reshape(-1, 8, LANES)


FEATURES = 48
SPAN = 512


def position_rows(length, emb_width):
    positions = np.arange(length, dtype=np.int64)
    bands = np.arange(1, (emb_width - 1) // 2 + 1, dtype=np.int64)
    angles = 2.0 * np.pi / length * ((bands[:, None] * positions[None, :]) % length)
    table = np.zeros((FEATURES, length), np.float32)
    table[0] = positions / length
    table[1 : 1 + bands.size] = np.cos(angles)
    table[1 + bands.size : emb_width] = np.sin(angles)
    table[emb_width] = 1.0
    return jnp.asarray(table)


def near_dot(left, right, left_dim, right_dim):
    left_high, left_low = in_two(left)
    right_high, right_low = in_two(right)
    return contract(
        jnp.concatenate([left_high, left_high, left_low], axis=left_dim),
        jnp.concatenate([right_high, right_low, right_high], axis=right_dim),
        left_dim,
        right_dim,
    )


def in_three(value):
    high = value.astype(bf16)
    rest = value - high.astype(f32)
    middle = rest.astype(bf16)
    return high, middle, (rest - middle.astype(f32)).astype(bf16)


def full_dot(left, right):
    a, b, c = in_three(left)
    d, e, f = in_three(right)
    return contract(
        jnp.concatenate([a, a, a, b, b, c], axis=0), jnp.concatenate([d, e, f, d, e, d], axis=0), 0, 0
    )


def sin_cos(x):
    turns = jnp.round(x * (2.0 / math.pi))
    r = ((x - turns * 1.5703125) - turns * 4.837512969970703125e-4) - turns * 7.54978995489188216e-8
    z = r * r
    sine = r + r * z * (-1.6666654611e-1 + z * (8.3321608736e-3 - z * 1.9515295891e-4))
    cosine = 1.0 - 0.5 * z + z * z * (
        4.166664568298827e-2 + z * (-1.388731625493765e-3 + z * 2.443315711809948e-5)
    )
    turn = lax.bitwise_and(turns.astype(jnp.int32), 3)
    odd = lax.bitwise_and(turn, 1) == 1
    first = jnp.where(odd, cosine, sine)
    second = jnp.where(odd, sine, cosine)
    return (
        jnp.where(turn >= 2, -first, first),
        jnp.where(jnp.logical_or(turn == 1, turn == 2), -second, second),
    )


def window_of(decay, start, shape, length):
    lane = lax.broadcasted_iota(jnp.int32, shape, 1) + start
    return jnp.exp(lane.astype(f32) * (-1.0 / length) * decay)


def filter_span(layer, start, pos, first_w, second_w, third_w, cols, decay, acts, shaped, squares):
    length = pos.shape[1]
    at = pl.ds(start, SPAN)
    act, slope = sin_cos(full_dot(first_w[layer], pos[:, at]))
    acts[layer, 0, :, at] = act
    acts[layer, 1, :, at] = slope
    act, slope = sin_cos(full_dot(second_w[layer], act) + cols[layer][:, :1])
    acts[layer, 2, :, at] = act
    acts[layer, 3, :, at] = slope
    raw = near_dot(third_w[layer], act, 0, 0)
    value = raw * window_of(decay[layer][:, :1], start, raw.shape, length)
    shaped[layer, :, at] = value
    squares[layer] += jnp.sum(value * value, axis=1, keepdims=True)


def filter_points(layer, group, tables, shaped, squares, spec_re, spec_im):
    length = shaped.shape[2]
    rows = pl.ds(pl.multiple_of(group * 8, 8), 8)
    scale = lax.rsqrt(squares[layer, rows, :1] * (1.0 / length) + 1e-05) * length ** (-0.5)
    value = shaped[layer, rows, :] * scale
    x = jnp.concatenate(
        [value[:, i * LANES : (i + 1) * LANES][None] for i in range(length // LANES)], axis=0
    )
    re, im = to_points(x, tables, False)
    spec_re[group] = re
    spec_im[group] = im


def filter_back_dot(layer, start, shaped, grad_taps, dots):
    at = pl.ds(start, SPAN)
    grad = taps_span(grad_taps, start)
    dots[layer] += jnp.sum(shaped[layer, :, at] * grad, axis=1, keepdims=True)


def taps_span(grad_taps, start):
    first = lax.div(start, LANES)
    pieces = []
    for i in range(SPAN // LANES):
        piece = grad_taps[:, first + i]
        pieces.append(piece.reshape(-1, LANES))
    return jnp.concatenate(pieces, axis=1)


def filter_back_span(
    layer, start, pos, second_w, third_w, decay, acts, shaped, squares, grad_taps, dots, grads
):
    length = pos.shape[1]
    at = pl.ds(start, SPAN)
    grad_third, grad_second, grad_first = grads
    mean_square = squares[layer][:, :1] * (1.0 / length)
    scale = lax.rsqrt(mean_square + 1e-05)
    cross = dots[layer][:, :1] * (1.0 / length) * scale * scale
    grad = taps_span(grad_taps, start)
    value = shaped[layer, :, at]
    grad = (grad - value * cross) * (scale * length ** (-0.5))
    grad = grad * window_of(decay[layer][:, :1], start, grad.shape, length)
    grad_third[layer] += near_dot(acts[layer, 2, :, at], grad, 1, 1)
    second = near_dot(third_w[layer], grad, 1, 0) * acts[layer, 3, :, at]
    grad_second[layer] += near_dot(acts[layer, 0, :, at], second, 1, 1)
    first = near_dot(second_w[layer], second, 1, 0) * acts[layer, 1, :, at]
    grad_first[layer] += near_dot(pos[:, at], jnp.concatenate([first, second], axis=0), 1, 1)


class Place:
    def __init__(self, ns):
        self.nz = ns // 2
        self.b = lax.axis_index("batch")
        self.s = lax.axis_index("seq")
        self.z = lax.div(self.s, 2)
        self.c = lax.rem(self.s, 2)
        self.x_peer = (lax.bitwise_xor(self.b, 1), self.s)
        self.y_peer = (lax.bitwise_xor(self.b, 2), self.s)
        self.core_peer = (self.b, lax.bitwise_xor(self.s, 1))
        self.up_peer = (self.b, lax.min(self.s + 2, ns - 1))
        self.down_peer = (self.b, lax.max(self.s - 2, 0))


def remote(src, dst, send, recv, peer):
    return pltpu.make_async_remote_copy(
        src_ref=src, dst_ref=dst, send_sem=send, recv_sem=recv, device_id=peer, device_id_type=MESH
    )


def greet(place, seq_peers):
    bar = pltpu.get_barrier_semaphore()

    def hello(peer):
        pl.semaphore_signal(bar, inc=1, device_id=peer, device_id_type=MESH)

    hello(place.x_peer)
    hello(place.y_peer)
    if seq_peers:
        ns = 2 * place.nz
        for step in range(1, ns):
            hello((place.b, lax.rem(place.s + step, ns)))
        pl.semaphore_wait(bar, 2 + ns - 1)
    else:
        hello(place.core_peer)
        pl.when(place.z + 1 < place.nz)(lambda: hello(place.up_peer))
        pl.when(place.z > 0)(lambda: hello(place.down_peer))
        ends = jnp.where(place.z == 0, 1, 0) + jnp.where(place.z == place.nz - 1, 1, 0)
        pl.semaphore_wait(bar, 5 - ends)


class Job:
    def __init__(self, arrays, results, scratch, task, plan):
        self.arrays, self.results, self.scratch, self.task = arrays, results, scratch, task
        self.plan = plan


class Runner:
    def __init__(self, tasks, plans):
        self.tasks = [[task, list(plan)] for task, plan in zip(tasks, plans, strict=True)]
        self.now = 0

    def add(self, task):
        self.tasks.insert(0, [task, []])

    def step(self, entry):
        if next(entry[0], "end") == "end":
            self.tasks.remove(entry)

    def phase(self):
        for entry in list(self.tasks):
            while entry[1] and entry[1][0] <= self.now:
                entry[1].pop(0)
                self.step(entry)
        self.now += 1

    def finish(self):
        while any(entry[1] for entry in self.tasks):
            self.phase()
        while self.tasks:
            for entry in list(self.tasks):
                self.step(entry)


def room(items):
    total = 0
    for item in items:
        if len(item.shape) < 2 or not jnp.issubdtype(item.dtype, jnp.floating):
            continue
        size = jnp.dtype(item.dtype).itemsize
        *outer, rows, lanes = item.shape
        tile = 32 // size
        total += math.prod(outer) * -(-rows // tile) * tile * -(-lanes // LANES) * LANES * size
    return total


def fused_call(name, body, arrays, results, scratch, jobs, seq_peers, ids):
    free = VMEM_LIMIT - room([*arrays, *results, *scratch])
    if body is not None and room([item for job in jobs for item in job.scratch]) > free:
        found, _ = fused_call(name, body, arrays, results, scratch, [], seq_peers, ids)
        alone = [fused_call(name + "_job", None, [], [], [], [job], seq_peers, ids)[1][0] for job in jobs]
        return found, alone
    collective_id = next(ids)
    ns = lax.axis_size("seq")
    counts = [len(arrays)] + [len(j.arrays) for j in jobs]
    counts += [len(results)] + [len(j.results) for j in jobs]
    counts += [len(scratch)] + [len(j.scratch) for j in jobs]
    n = 1 + len(jobs)

    def kernel(*refs):
        parts, start = [], 0
        for count in counts:
            parts.append(refs[start : start + count])
            start += count
        place = Place(ns)
        greet(place, seq_peers)
        tasks = [
            job.task(place, *parts[1 + k], *parts[n + 1 + k], parts[2 * n + 1 + k])
            for k, job in enumerate(jobs)
        ]
        runner = Runner(tasks, [job.plan for job in jobs])
        if body is not None:
            body(place, runner, parts[0], parts[n], parts[2 * n])
        runner.finish()

    hbm = pl.BlockSpec(memory_space=pl.ANY)
    flat = lambda pick: [item for job in jobs for item in pick(job)]
    found = pl.pallas_call(
        kernel,
        out_shape=list(results) + flat(lambda j: j.results),
        in_specs=whole(counts[0]) + [hbm] * sum(counts[1:n]),
        out_specs=whole(counts[n]) + [hbm] * sum(counts[n + 1 : 2 * n]),
        scratch_shapes=list(scratch) + flat(lambda j: j.scratch),
        compiler_params=pltpu.CompilerParams(
            collective_id=collective_id, has_side_effects=True, vmem_limit_bytes=VMEM_LIMIT
        ),
        name=name,
    )(*arrays, *flat(lambda j: j.arrays))
    return found[: counts[n]], found[counts[n] :]


def whole(count):
    return [pl.BlockSpec(memory_space=pltpu.VMEM)] * count


def gather_sems(nz):
    return [
        pltpu.SemaphoreType.DMA((1,)),
        pltpu.SemaphoreType.DMA((2, nz)),
        pltpu.SemaphoreType.DMA((nz,)),
        pltpu.SemaphoreType.DMA((4, nz)),
        pltpu.SemaphoreType.DMA((4, nz)),
        pltpu.SemaphoreType.DMA((4,)),
        pltpu.SemaphoreType.DMA((4,)),
    ]


def gather_task(place, src, dst, sems):
    one, chain_send, chain_recv, send, recv, core_send, core_recv = sems
    b, z, c, nz = place.b, place.z, place.c, place.nz
    bx, by, bd = place.x_peer[0], place.y_peer[0], lax.bitwise_xor(b, 3)
    local = pltpu.make_async_copy(src, dst.at[b, z, c], one.at[0])

    def chain(source, shard, up):
        row = 0 if up else 1
        peer = place.up_peer if up else place.down_peer
        return remote(source, dst.at[b, shard, c], chain_send.at[row, shard], chain_recv.at[shard], peer)

    def across(source, shard, along):
        peer = place.y_peer if along else place.x_peer
        return remote(source, dst.at[b, shard, c], send.at[along, shard], recv.at[along, shard], peer)

    def onward(shard, along):
        peer = place.y_peer if along else place.x_peer
        part = dst.at[bx if along else by, shard, c]
        return remote(part, part, send.at[2 + along, shard], recv.at[2 + along, shard], peer)

    def core(batch, i):
        part = dst.at[batch, :, c]
        return remote(part, part, core_send.at[i], core_recv.at[i], place.core_peer)

    def pass_on(shard):
        across(src, shard, 0).wait_recv()
        across(src, shard, 1).wait_recv()
        even = lax.rem(shard, 2) == 0
        pl.when(even)(lambda: onward(shard, 1).start())
        pl.when(jnp.logical_not(even))(lambda: onward(shard, 0).start())

    def pass_on_from(hop):
        if hop == 0:
            pass_on(z)
        else:
            pl.when(z - hop >= 0)(lambda: pass_on(z - hop))
            pl.when(z + hop < nz)(lambda: pass_on(z + hop))

    local.start()
    pl.when(z + 1 < nz)(lambda: chain(src, z, True).start())
    pl.when(z > 0)(lambda: chain(src, z, False).start())
    across(src, z, 0).start()
    across(src, z, 1).start()
    yield
    for hop in range(1, nz):
        below, above = z - hop, z + hop

        @pl.when(below >= 0)
        def _():
            chain(src, below, True).wait_recv()
            part = dst.at[b, below, c]
            pl.when(z + 1 < nz)(lambda: chain(part, below, True).start())
            across(part, below, 0).start()
            across(part, below, 1).start()

        @pl.when(above < nz)
        def _():
            chain(src, above, False).wait_recv()
            part = dst.at[b, above, c]
            pl.when(z > 0)(lambda: chain(part, above, False).start())
            across(part, above, 0).start()
            across(part, above, 1).start()

        pass_on_from(hop - 1)
        yield
    local.wait()
    core(b, 0).start()
    pass_on_from(nz - 1)
    core(bx, 1).start()
    core(by, 2).start()
    yield
    for shard in range(nz):
        onward(shard, 1 - shard % 2).wait_recv()
    core(bd, 3).start()
    yield
    for hop in range(nz):
        pl.when(jnp.logical_and(z >= hop, z + 1 < nz))(lambda: chain(src, z - hop, True).wait_send())
        pl.when(jnp.logical_and(z + hop < nz, z > 0))(lambda: chain(src, z + hop, False).wait_send())
    for shard in range(nz):
        across(src, shard, 0).wait_send()
        across(src, shard, 1).wait_send()
        onward(shard, 1 - shard % 2).wait_send()
    for i in range(4):
        core(b, i).wait()
    yield


def gather_job(array, layer, plan):
    nz = lax.axis_size("seq") // 2
    result = jax.ShapeDtypeStruct((4, nz, 2) + array.shape[1:], array.dtype)
    task = lambda place, src, dst, sems: gather_task(place, src.at[layer], dst, sems)
    return Job([array], [result], gather_sems(nz), task, plan)


def column_task(place, src, dst, sems):
    one, chain_send, chain_recv = sems
    z, nz = place.z, place.nz
    local = pltpu.make_async_copy(src, dst.at[z], one.at[0])

    def chain(source, shard, up):
        row = 0 if up else 1
        peer = place.up_peer if up else place.down_peer
        return remote(source, dst.at[shard], chain_send.at[row, shard], chain_recv.at[shard], peer)

    local.start()
    pl.when(z + 1 < nz)(lambda: chain(src, z, True).start())
    pl.when(z > 0)(lambda: chain(src, z, False).start())
    yield
    for hop in range(1, nz):
        below, above = z - hop, z + hop

        @pl.when(below >= 0)
        def _():
            chain(src, below, True).wait_recv()
            pl.when(z + 1 < nz)(lambda: chain(dst.at[below], below, True).start())

        @pl.when(above < nz)
        def _():
            chain(src, above, False).wait_recv()
            pl.when(z > 0)(lambda: chain(dst.at[above], above, False).start())

        yield
    for hop in range(nz):
        pl.when(jnp.logical_and(z >= hop, z + 1 < nz))(lambda: chain(src, z - hop, True).wait_send())
        pl.when(jnp.logical_and(z + hop < nz, z > 0))(lambda: chain(src, z + hop, False).wait_send())
    local.wait()
    yield


def column_job(array, layer, plan):
    nz = lax.axis_size("seq") // 2
    result = jax.ShapeDtypeStruct((nz,) + array.shape[1:], array.dtype)
    sems = [
        pltpu.SemaphoreType.DMA((1,)),
        pltpu.SemaphoreType.DMA((2, nz)),
        pltpu.SemaphoreType.DMA((nz,)),
    ]
    task = lambda place, src, dst, sems: column_task(place, src.at[layer], dst, sems)
    return Job([array], [result], sems, task, plan)


def plane_task(place, src, dst, sems):
    one, send, recv, core_send, core_recv = sems
    b, c, nz = place.b, place.c, place.nz
    bx, by, bd = place.x_peer[0], place.y_peer[0], lax.bitwise_xor(b, 3)
    half = nz // 2
    local = pltpu.make_async_copy(src, dst.at[b, :, c], one.at[0])
    over_x = remote(src, dst.at[b, :, c], send.at[0], recv.at[0], place.x_peer)
    over_y = remote(src, dst.at[b, :, c], send.at[1], recv.at[1], place.y_peer)
    low, high = pl.ds(0, half), pl.ds(half, nz - half)
    far_y = remote(dst.at[bx, low, c], dst.at[bx, low, c], send.at[2], recv.at[2], place.y_peer)
    far_x = remote(dst.at[by, high, c], dst.at[by, high, c], send.at[3], recv.at[3], place.x_peer)

    def core(source, batch, i):
        return remote(source, dst.at[batch, :, c], core_send.at[i], core_recv.at[i], place.core_peer)

    over_x.start()
    over_y.start()
    core(src, b, 0).start()
    local.start()
    yield
    over_x.wait_recv()
    far_y.start()
    over_y.wait_recv()
    far_x.start()
    core(dst.at[bx, :, c], bx, 1).start()
    core(dst.at[by, :, c], by, 2).start()
    yield
    far_y.wait_recv()
    far_x.wait_recv()
    core(dst.at[bd, :, c], bd, 3).start()
    yield
    for copy in (over_x, over_y, far_y, far_x):
        copy.wait_send()
    local.wait()
    for i in range(4):
        core(src, b, i).wait()
    yield


def plane_job(array, plan):
    nz = array.shape[0]
    result = jax.ShapeDtypeStruct((4, nz, 2) + array.shape[1:], array.dtype)
    sems = [pltpu.SemaphoreType.DMA((1,))] + [pltpu.SemaphoreType.DMA((4,))] * 4
    return Job([array], [result], sems, plane_task, plan)


def reduce_scratch(nz, shape, dtype):
    half = (nz,) + shape
    return [
        pltpu.VMEM((4,) + half, dtype),
        pltpu.VMEM((4,) + half, dtype),
        pltpu.VMEM((5,) + half, dtype),
        pltpu.VMEM(shape, f32),
        pltpu.SemaphoreType.DMA((1,)),
        pltpu.SemaphoreType.DMA((3, nz)),
        pltpu.SemaphoreType.DMA((5, nz)),
        pltpu.SemaphoreType.DMA((5, nz)),
    ]


def far_first(place):
    nz = place.nz
    tables = [sorted(range(nz), key=lambda k: (-abs(k - z), k)) for z in range(nz)]
    order = []
    for j in range(nz):
        shard = jnp.int32(tables[0][j])
        for z in range(1, nz):
            shard = jnp.where(place.z == z, tables[z][j], shard)
        order.append(shard)
    return order


def reduce_task(place, src, out, scratch):
    acc, other, box, total, one, near, send, recv = scratch
    kind = acc.dtype
    b, z, c, nz = place.b, place.z, place.c, place.nz
    bx, by, bd = place.x_peer[0], place.y_peer[0], lax.bitwise_xor(b, 3)
    far, via_x, via_y, up, down = range(5)
    order = far_first(place)
    halves = [range(0, nz // 2), range(nz // 2, nz)]

    def add(target, shard, *lanes):
        value = acc[target, shard].astype(f32)
        for lane in lanes:
            value += box[lane, shard].astype(f32)
        acc[target, shard] = value.astype(kind)

    def move(part, shard, lane, peer):
        return remote(acc.at[part, shard], box.at[lane, shard], send.at[lane, shard], recv.at[lane, shard], peer)

    def mine(shard):
        return pltpu.make_async_copy(src.at[:, shard, c], acc.at[:, shard], near.at[0, shard])

    def core(shard):
        return remote(src.at[:, shard, 1 - c], other.at[:, shard], near.at[1, shard], near.at[2, shard], place.core_peer)

    for shard in order:
        core(shard).start()
        mine(shard).start()
    yield
    for half in halves:
        for j in half:
            shard = order[j]
            mine(shard).wait()
            core(shard).wait_recv()

            @pl.loop(0, 4)
            def _(part):
                acc[part, shard] = (
                    acc[part, shard].astype(f32) + other[part, shard].astype(f32)
                ).astype(kind)

            if j % 2 == 0:
                move(bd, shard, far, place.x_peer).start()
                move(bx, shard, via_x, place.x_peer).start()
            else:
                move(bd, shard, far, place.y_peer).start()
                move(by, shard, via_y, place.y_peer).start()
        yield
    for half in halves:
        for j in half:
            shard = order[j]
            move(bd, shard, far, place.x_peer).wait_recv()
            if j % 2 == 0:
                add(by, shard, far)
                move(by, shard, via_y, place.y_peer).start()
            else:
                add(bx, shard, far)
                move(bx, shard, via_x, place.x_peer).start()
        yield
    for half in halves:
        for j in half:
            shard = order[j]
            move(bx, shard, via_x, place.x_peer).wait_recv()
            move(by, shard, via_y, place.y_peer).wait_recv()
            add(b, shard, via_x, via_y)

            @pl.when(z < shard)
            def _():
                @pl.when(z > 0)
                def _():
                    move(b, shard, up, place.up_peer).wait_recv()
                    add(b, shard, up)

                move(b, shard, up, place.up_peer).start()

            @pl.when(z > shard)
            def _():
                @pl.when(z + 1 < nz)
                def _():
                    move(b, shard, down, place.down_peer).wait_recv()
                    add(b, shard, down)

                move(b, shard, down, place.down_peer).start()

        yield
    total[...] = acc[b, z].astype(f32)

    @pl.when(z > 0)
    def _():
        move(b, z, up, place.up_peer).wait_recv()
        total[...] += box[up, z].astype(f32)

    @pl.when(z + 1 < nz)
    def _():
        move(b, z, down, place.down_peer).wait_recv()
        total[...] += box[down, z].astype(f32)

    result = pltpu.make_async_copy(total, out, one.at[0])
    result.start()
    for shard in range(nz):
        core(shard).wait_send()
        for lane in (far, via_x, via_y):
            move(b, shard, lane, place.x_peer).wait_send()
        pl.when(z < shard)(lambda: move(b, shard, up, place.up_peer).wait_send())
        pl.when(z > shard)(lambda: move(b, shard, down, place.down_peer).wait_send())
    result.wait()
    yield


def reduce_job(array, plan):
    nz = lax.axis_size("seq") // 2
    shape = array.shape[1:]
    return Job(
        [array.reshape((4, nz, 2) + shape)],
        [jax.ShapeDtypeStruct(shape, f32)],
        reduce_scratch(nz, shape, array.dtype),
        reduce_task,
        plan,
    )


def total_scratch(nz, shape, shared):
    return [
        pltpu.VMEM((3,) + shape, f32),
        pltpu.VMEM((2,) + shape, f32),
        pltpu.VMEM((2, nz, shared, LANES), f32),
        pltpu.SemaphoreType.DMA((2, 3)),
        pltpu.SemaphoreType.DMA((2, nz)),
    ]


def total_task(place, src, out, scratch):
    box, sums, lines, pair, chain = scratch
    z, c, nz = place.z, place.c, place.nz
    rows = src.shape[0]
    shared = lines.shape[2]
    tail = pl.ds(rows - shared, shared)

    def swap(source, dst, i, peer):
        return remote(source, dst, pair.at[0, i], pair.at[1, i], peer)

    first = swap(src, box.at[0], 0, place.x_peer)
    first.start()
    yield
    first.wait()
    sums[0] = src[...] + box[0]
    second = swap(sums.at[0], box.at[1], 1, place.y_peer)
    second.start()
    yield
    second.wait()
    sums[1] = sums[0] + box[1]
    third = swap(sums.at[1, tail], box.at[2, tail], 2, place.core_peer)
    third.start()
    yield
    third.wait()
    lines[0, z] = sums[1, tail] + box[2, tail]

    def along(step):
        peer = lax.rem(z + step, nz)
        return remote(lines.at[0, z], lines.at[1, z], chain.at[0, step], chain.at[1, step], (place.b, 2 * peer + c))

    for step in range(1, nz):
        along(step).start()
    lines[1, z] = lines[0, z]
    yield
    for step in range(1, nz):
        along(step).wait_recv()
    value = lines[1, 0]
    for shard in range(1, nz):
        value = value + lines[1, shard]
    out[: rows - shared] = sums[1, : rows - shared]
    out[tail] = value
    for step in range(1, nz):
        along(step).wait_send()
    yield


def prepare(jobs, pos_rows, first_w, second_w, third_w, cols, decay, tables, ids):
    layers, hidden, own = third_w.shape
    length = pos_rows.shape[1]
    rows = (own // 8,) + tables[4].shape
    results = [
        jax.ShapeDtypeStruct((layers, 4, hidden, length), f32),
        jax.ShapeDtypeStruct((layers, own, length), f32),
        jax.ShapeDtypeStruct((layers, own, LANES), f32),
    ] + [jax.ShapeDtypeStruct(rows, f32)] * (2 * layers)

    def body(place, runner, ins, outs, scratch):
        pos, first, second, third, bias, rate = ins[:6]
        factors = ins[6:]
        acts, shaped, squares = outs[:3]
        specs = outs[3:]
        spans, groups = length // SPAN, own // 8
        squares[...] = jnp.zeros_like(squares)
        for part in range(8):
            runner.phase()

            @pl.loop(part * spans // 8, (part + 1) * spans // 8)
            def _(i):
                for layer in range(layers):
                    filter_span(
                        layer, pl.multiple_of(i * SPAN, SPAN), pos, first, second, third, bias, rate, acts, shaped, squares
                    )

        for part in range(6):
            runner.phase()

            @pl.loop(part * groups // 6, (part + 1) * groups // 6)
            def _(group):
                for layer in range(layers):
                    filter_points(layer, group, factors, shaped, squares, *specs[2 * layer : 2 * layer + 2])

    return fused_call(
        "prepare",
        body,
        [pos_rows, first_w, second_w, third_w, cols, decay, *tables],
        results,
        [],
        jobs,
        False,
        ids,
    )


def last(jobs, pos_rows, second_w, third_w, decay, kept, grad_taps, ids):
    layers, hidden, own = third_w.shape
    length = pos_rows.shape[1]
    nz = lax.axis_size("seq") // 2
    each, shared = hidden + 8, FEATURES + hidden
    payload = jax.ShapeDtypeStruct((layers * (each + shared), LANES), f32)

    def body(place, runner, ins, outs, scratch):
        pos, second, third, rate, acts, shaped, squares = ins[:7]
        taps = ins[7:]
        dots, grad_third, grad_second, grad_first, payload_in = scratch[:5]
        for ref in (dots, grad_third, grad_second, grad_first, payload_in):
            ref[...] = jnp.zeros_like(ref)
        runner.phase()
        spans = length // SPAN

        @pl.loop(0, spans)
        def _(i):
            for layer in range(layers):
                filter_back_dot(layer, pl.multiple_of(i * SPAN, SPAN), shaped, taps[layer], dots)

        for part in range(8):
            runner.phase()

            @pl.loop(part * spans // 8, (part + 1) * spans // 8)
            def _(i):
                for layer in range(layers):
                    filter_back_span(
                        layer, pl.multiple_of(i * SPAN, SPAN), pos, second, third, rate, acts, shaped, squares,
                        taps[layer], dots, (grad_third, grad_second, grad_first)
                    )

        for layer in range(layers):
            start = layer * each
            payload_in[start : start + hidden, :own] = grad_third[layer]
            lag = taps[layer][:, 0].reshape(own, LANES)
            pick = jnp.where(lax.broadcasted_iota(jnp.int32, (8, LANES), 1) == 0, 1.0, 0.0)
            payload_in[start + hidden : start + each, :own] = near_dot(pick, lag, 1, 1)
            start = layers * each + layer * shared
            payload_in[start : start + FEATURES, : 2 * hidden] = grad_first[layer]
            payload_in[start + FEATURES : start + shared, :hidden] = grad_second[layer]
        runner.add(total_task(place, payload_in, outs[0], scratch[5:]))

    return fused_call(
        "last",
        body,
        [pos_rows, second_w, third_w, decay, *kept, *grad_taps],
        [payload],
        [
            pltpu.VMEM((layers, own, LANES), f32),
            pltpu.VMEM((layers, hidden, own), f32),
            pltpu.VMEM((layers, hidden, hidden), f32),
            pltpu.VMEM((layers, FEATURES, 2 * hidden), f32),
            pltpu.VMEM(payload.shape, f32),
        ]
        + total_scratch(nz, payload.shape, layers * shared),
        jobs,
        True,
        ids,
    )


def conv_lanes(value, rim_near, rim_far):
    lane = lax.broadcasted_iota(jnp.int32, value.shape, 1)
    near = jnp.where(lane == 0, rim_near, pltpu.roll(value, 1, 1))
    far = jnp.where(lane == 0, rim_far, jnp.where(lane == 1, rim_near, pltpu.roll(value, 2, 1)))
    return near, far


def rows_of(ref, stream, block, count):
    value = ref[stream, pl.ds(block, count)].astype(f32)
    return value.reshape(-1, value.shape[-1])


def short_out(mixed, conv, rim, stream, block, count=1):
    value = rows_of(mixed, stream, block, count)
    side, edge = rows_of(conv, stream, block, count), rows_of(rim, stream, block, count)
    near, far = conv_lanes(value, edge[:, 1:2], edge[:, 0:1])
    return side[:, 0:1] * far + side[:, 1:2] * near + side[:, 2:3] * value


def by_blocks(nblocks, most):
    return max(k for k in range(1, most + 1) if nblocks % k == 0)


def edge_scratch(streams, nblocks, chans):
    rows = pltpu.VMEM((streams, 16, nblocks * chans), f32)
    return [rows, rows, pltpu.VMEM((streams, nblocks, chans, LANES), f32), pltpu.SemaphoreType.DMA((2,))]


def edge_copy(place, scratch, to_right):
    out, came, _, sems = scratch
    ns = 2 * place.nz
    peer = lax.min(place.s + 1, ns - 1) if to_right else lax.max(place.s - 1, 0)
    return remote(out, came, sems.at[0], sems.at[1], (place.b, peer))


def send_edge(place, scratch, tiles_of, first, to_right):
    out = scratch[0]
    row = lax.broadcasted_iota(jnp.int32, (16, LANES), 0)
    lane = lax.broadcasted_iota(jnp.int32, (16, LANES), 1)
    pick = jnp.where(jnp.logical_and(lane == row + first, row < 2), 1.0, 0.0).astype(bf16)
    for stream in range(out.shape[0]):
        high, low = in_two(tiles_of(stream).reshape(-1, LANES))
        out[stream] = contract(
            jnp.concatenate([pick, pick], axis=1), jnp.concatenate([high, low], axis=1), 1, 1
        )
    has = place.s + 1 < 2 * place.nz if to_right else place.s > 0
    pl.when(has)(lambda: edge_copy(place, scratch, to_right).start())


def take_edge(place, scratch, to_right):
    _, came, cols, _ = scratch
    _, nblocks, chans, _ = cols.shape
    comes = place.s > 0 if to_right else place.s + 1 < 2 * place.nz
    sends = place.s + 1 < 2 * place.nz if to_right else place.s > 0

    @pl.when(comes)
    def _():
        edge_copy(place, scratch, to_right).wait_recv()
        row = lax.broadcasted_iota(jnp.int32, (16, LANES), 0)
        lane = lax.broadcasted_iota(jnp.int32, (16, LANES), 1)
        spread = jnp.where(jnp.logical_and(lane == row, row < 2), 1.0, 0.0).astype(bf16)
        both = jnp.concatenate([spread, spread], axis=0)
        for stream in range(cols.shape[0]):
            pair = jnp.concatenate(in_two(came[stream]), axis=0)
            cols[stream] = contract(pair, both, 0, 0).reshape(nblocks, chans, LANES)

    @pl.when(jnp.logical_not(comes))
    def _():
        cols[...] = jnp.zeros_like(cols)

    pl.when(sends)(lambda: edge_copy(place, scratch, to_right).wait_send())


def sub_rows(chans):
    return 16 if chans % 16 == 0 else chans


def mix_body(place, runner, ins, outs, scratch, layer):
    mixed, conv, spec_re, spec_im, skip = ins[:5]
    tables = ins[5:]
    long_out, gated, sig_re, sig_im, rim = outs
    signal, chan_in, chan_out, tok_in, send, recv = scratch[:6]
    edge = [scratch[6], scratch[7], rim, scratch[8]]
    toks = mixed.shape[3]
    ns, groups, quarters, chans, _ = signal.shape
    take = sub_rows(chans)

    def to_chan(g, step):
        peer = lax.rem(place.s + step, ns)
        return remote(
            signal.at[peer, g],
            chan_in.at[g, pl.ds(place.s * quarters, quarters)],
            send.at[0, g, step],
            recv.at[0, g, step],
            (place.b, peer),
        )

    def send_pieces(step, first, value):
        peer = lax.rem(place.s + step, ns)
        count = value.shape[0] // chans
        for k in range(count):
            for q in range(quarters):
                piece = value[k * chans : (k + 1) * chans, q * LANES : (q + 1) * LANES]
                signal[peer, first + k, q] = piece

        @pl.when(step < ns)
        def _():
            for k in range(count):
                to_chan(first + k, step).start()

        @pl.when(step == ns)
        def _():
            for k in range(count):
                for q in range(quarters):
                    chan_in[first + k, place.s * quarters + q] = signal[peer, first + k, q]

    def to_tok(g, step):
        peer = lax.rem(place.s + step, ns)
        return remote(
            chan_out.at[g, pl.ds(peer * quarters, quarters)],
            tok_in.at[place.s, g],
            send.at[1, g, step],
            recv.at[1, g, step],
            (place.b, peer),
        )

    send_edge(place, edge, lambda k: mixed[k, :, :, toks - LANES :].astype(f32), LANES - 2, True)
    runner.phase()
    take_edge(place, edge, True)
    share = by_blocks(groups, 3)
    for first in range(0, groups, share):

        @pl.loop(1, ns + 1)
        def _(step):
            peer = lax.rem(place.s + step, ns)
            block = peer * groups + first
            value = short_out(mixed, conv, rim, 1, block, share) * short_out(mixed, conv, rim, 2, block, share)
            send_pieces(step, first, value.astype(bf16))

    runner.phase()
    for g in range(groups):

        @pl.loop(1, ns)
        def _(step):
            to_chan(g, step).wait_recv()

        @pl.loop(0, chans // take)
        def _(i):
            at = pl.ds(pl.multiple_of(i * take, take), take)
            block = chan_in[g, :, at, :].astype(f32)
            parts = []
            for j in range(take // 8):
                index = (g * chans) // 8 + i * (take // 8) + j
                x = block[:, 8 * j : 8 * j + 8, :]
                re, im = to_points(x, tables, True)
                sig_re[index] = re
                sig_im[index] = im
                tap_re, tap_im = spec_re[index], spec_im[index]
                y = from_points(re * tap_re - im * tap_im, re * tap_im + im * tap_re, tables)
                parts.append(y + skip[layer, index][None] * x)
            chan_out[g, :, at, :] = jnp.concatenate(parts, axis=1).astype(bf16)

        @pl.loop(1, ns)
        def _(step):
            to_tok(g, step).start()

        for q in range(quarters):
            tok_in[place.s, g, q] = chan_out[g, place.s * quarters + q]
        runner.phase()

    for g in range(groups):

        @pl.loop(1, ns)
        def _(step):
            to_tok(g, step).wait_recv()

        @pl.loop(0, ns, unroll=4)
        def _(owner):
            block = owner * groups + g
            value = jnp.concatenate([tok_in[owner, g, q] for q in range(quarters)], axis=1)
            long_out[block] = value
            gated[block] = (short_out(mixed, conv, rim, 0, block) * value.astype(f32)).astype(bf16)

        if g % 2:
            runner.phase()

    for g in range(groups):

        @pl.loop(1, ns)
        def _(step):
            to_chan(g, step).wait_send()
            to_tok(g, step).wait_send()


def mixer_scratch(ns, groups, quarters, chans):
    pieces = pltpu.VMEM((ns, groups, quarters, chans, LANES), bf16)
    lines = pltpu.VMEM((groups, ns * quarters, chans, LANES), bf16)
    sems = pltpu.SemaphoreType.DMA((2, groups, ns))
    return [pieces, lines, lines, pieces, sems, sems]


def mix(jobs, layer, mixed, conv, spec, skip, tables, ids):
    ns = lax.axis_size("seq")
    _, nblocks, chans, toks = mixed.shape
    groups, quarters = nblocks // ns, toks // LANES
    rows = jax.ShapeDtypeStruct((groups * chans // 8,) + tables[4].shape, f32)
    tokens = jax.ShapeDtypeStruct((nblocks, chans, toks), bf16)
    edges = edge_scratch(3, nblocks, chans)
    return fused_call(
        "mix",
        functools.partial(mix_body, layer=layer),
        [mixed, conv, *spec, skip, *tables],
        [tokens, tokens, rows, rows, jax.ShapeDtypeStruct(conv.shape, f32)],
        mixer_scratch(ns, groups, quarters, chans) + edges[:2] + edges[3:],
        jobs,
        True,
        ids,
    )


def unmix_body(place, runner, ins, outs, scratch, layer):
    mixed, conv, rim, long_out, grad_gated, spec_re, spec_im, sig_re, sig_im, skip = ins[:10]
    tables = ins[10:]
    grad_taps, grad_mixed, grad_conv = outs
    pull, chan_in, chan_out, tok_in, send, recv, grad_short, partials = scratch[:8]
    edge = scratch[8:]
    toks = mixed.shape[3]
    runner.phase()
    ns, groups, quarters, chans, _ = pull.shape
    take = sub_rows(chans)

    def to_chan(g, step):
        peer = lax.rem(place.s + step, ns)
        return remote(
            pull.at[peer, g],
            chan_in.at[g, pl.ds(place.s * quarters, quarters)],
            send.at[0, g, step],
            recv.at[0, g, step],
            (place.b, peer),
        )

    def send_pieces(step, first, value):
        peer = lax.rem(place.s + step, ns)
        count = value.shape[0] // chans
        for k in range(count):
            for q in range(quarters):
                piece = value[k * chans : (k + 1) * chans, q * LANES : (q + 1) * LANES]
                pull[peer, first + k, q] = piece

        @pl.when(step < ns)
        def _():
            for k in range(count):
                to_chan(first + k, step).start()

        @pl.when(step == ns)
        def _():
            for k in range(count):
                for q in range(quarters):
                    chan_in[first + k, place.s * quarters + q] = pull[peer, first + k, q]

    def to_tok(g, step):
        peer = lax.rem(place.s + step, ns)
        return remote(
            chan_out.at[g, pl.ds(peer * quarters, quarters)],
            tok_in.at[place.s, g],
            send.at[1, g, step],
            recv.at[1, g, step],
            (place.b, peer),
        )

    share = by_blocks(groups, 3)
    for first in range(0, groups, share):

        @pl.loop(1, ns + 1)
        def _(step):
            block = lax.rem(place.s + step, ns) * groups + first
            gated = grad_gated[pl.ds(block, share)].reshape(share * chans, toks)
            send_pieces(step, first, (gated * short_out(mixed, conv, rim, 0, block, share)).astype(bf16))

    runner.phase()
    for g in range(groups):

        @pl.loop(1, ns)
        def _(step):
            to_chan(g, step).wait_recv()

        @pl.loop(0, chans // take)
        def _(i):
            at = pl.ds(pl.multiple_of(i * take, take), take)
            block = chan_in[g, :, at, :].astype(f32)
            parts = []
            for j in range(take // 8):
                index = (g * chans) // 8 + i * (take // 8) + j
                x = block[:, 8 * j : 8 * j + 8, :]
                re, im = to_points(x, tables, True)
                tap_re, tap_im = spec_re[index], spec_im[index]
                y = from_points(tap_re * re + tap_im * im, tap_re * im - tap_im * re, tables)
                parts.append(y + skip[layer, index][None] * x)
                own_re, own_im = sig_re[index], sig_im[index]
                grad_taps[index] = from_points(
                    own_re * re + own_im * im, own_re * im - own_im * re, tables
                )
            chan_out[g, :, at, :] = jnp.concatenate(parts, axis=1).astype(bf16)

        @pl.loop(1, ns)
        def _(step):
            to_tok(g, step).start()

        for q in range(quarters):
            tok_in[place.s, g, q] = chan_out[g, place.s * quarters + q]
        runner.phase()

    @pl.loop(0, ns * groups, unroll=4)
    def _(block):
        grad_short[0, block] = grad_gated[block] * long_out[block].astype(f32)

    for g in range(groups):

        @pl.loop(1, ns)
        def _(step):
            to_tok(g, step).wait_recv()

        @pl.loop(0, ns, unroll=4)
        def _(owner):
            block = owner * groups + g
            value = jnp.concatenate(
                [tok_in[owner, g, q] for q in range(quarters)], axis=1
            ).astype(f32)
            grad_short[1, block] = value * short_out(mixed, conv, rim, 2, block)
            grad_short[2, block] = value * short_out(mixed, conv, rim, 1, block)

        if g % 2:
            runner.phase()

    send_edge(place, edge, lambda k: grad_short[k, :, :, :LANES], 0, False)
    many = by_blocks(ns * groups, 4)
    ones = jnp.ones((2 * LANES, LANES), bf16)
    for stream in range(3):

        @pl.loop(0, ns * groups // many, unroll=2)
        def _(i):
            at = pl.ds(i * many, many)
            grad = rows_of(grad_short, stream, i * many, many)
            value = rows_of(mixed, stream, i * many, many)
            side = rows_of(rim, stream, i * many, many)
            near, far = conv_lanes(value, side[:, 1:2], side[:, 0:1])
            for k, moved in enumerate((far, near, value)):
                terms = grad * moved
                partial = terms[:, :LANES]
                for q in range(1, quarters):
                    partial += terms[:, q * LANES : (q + 1) * LANES]
                partials[k, at] = partial.reshape(many, chans, LANES)

        sums = [
            product(jnp.concatenate(in_two(partials[k].reshape(-1, LANES)), axis=1), ones)
            for k in range(3)
        ]
        lane = lax.broadcasted_iota(jnp.int32, sums[0].shape, 1)
        found = jnp.where(lane == 0, sums[0], jnp.where(lane == 1, sums[1], sums[2]))
        grad_conv[stream] = found.reshape(ns * groups, chans, LANES)
    runner.phase()
    take_edge(place, edge, False)
    edge_cols = edge[2]
    for stream in range(3):

        @pl.loop(0, ns * groups // many, unroll=2)
        def _(i):
            value = rows_of(grad_short, stream, i * many, many)
            side, after = rows_of(conv, stream, i * many, many), rows_of(edge_cols, stream, i * many, many)
            lane = lax.broadcasted_iota(jnp.int32, value.shape, 1)
            near = jnp.where(lane == toks - 1, after[:, 0:1], pltpu.roll(value, toks - 1, 1))
            far = jnp.where(
                lane == toks - 1,
                after[:, 1:2],
                jnp.where(lane == toks - 2, after[:, 0:1], pltpu.roll(value, toks - 2, 1)),
            )
            total = side[:, 2:3] * value + side[:, 1:2] * near + side[:, 0:1] * far
            grad_mixed[stream, pl.ds(i * many, many)] = total.astype(bf16).reshape(many, chans, toks)

    for g in range(groups):

        @pl.loop(1, ns)
        def _(step):
            to_chan(g, step).wait_send()
            to_tok(g, step).wait_send()


def unmix(jobs, layer, mixed, conv, rim, long_out, grad_gated, spec, sig, skip, tables, ids):
    ns = lax.axis_size("seq")
    _, nblocks, chans, toks = mixed.shape
    groups, quarters = nblocks // ns, toks // LANES
    return fused_call(
        "unmix",
        functools.partial(unmix_body, layer=layer),
        [mixed, conv, rim, long_out, grad_gated, *spec, *sig, skip, *tables],
        [
            jax.ShapeDtypeStruct((groups * chans // 8, ns * quarters, 8, LANES), f32),
            jax.ShapeDtypeStruct(mixed.shape, bf16),
            jax.ShapeDtypeStruct(conv.shape, f32),
        ],
        mixer_scratch(ns, groups, quarters, chans)
        + [pltpu.VMEM(mixed.shape, f32), pltpu.VMEM(conv.shape, f32)]
        + edge_scratch(3, nblocks, chans),
        jobs,
        True,
        ids,
    )


def on_device(
    tokens,
    cotangent,
    norm_gains,
    w_in,
    short_conv,
    w_out,
    w_fc,
    w_proj,
    filt_w1,
    filt_b1,
    filt_w2,
    filt_b2,
    filt_w3,
    skip_gain,
    decay_rate,
):
    layers, _, width3 = w_in.shape
    width = width3 // 3
    ns = lax.axis_size("seq")
    devices = lax.axis_size("batch") * ns
    stream = tokens[0].astype(f32)
    toks = stream.shape[0]
    length = toks * ns
    own_chans = width // ns
    chans = 16 if own_chans % 16 == 0 else own_chans
    groups = own_chans // chans
    nblocks = ns * groups
    blocked = (3, nblocks, chans)
    tables = transform_tables(length)
    pos_rows = position_rows(length, filt_w1.shape[1])

    gain_cols, conv_cols = norm_gains.shape[2], short_conv.shape[2]
    small = jnp.concatenate(
        [
            jnp.pad(norm_gains.reshape(2 * layers, gain_cols).astype(f32), ((0, 0), (0, LANES - gain_cols))),
            jnp.pad(short_conv.reshape(3 * layers, conv_cols).astype(f32), ((0, 0), (0, LANES - conv_cols))),
        ],
        axis=0,
    )
    small = jnp.pad(small, ((0, -small.shape[0] % 8), (0, 0)))[None]

    first_w = jnp.pad(
        jnp.concatenate([filt_w1, filt_b1[:, None]], axis=1),
        ((0, 0), (0, FEATURES - filt_w1.shape[1] - 1), (0, 0)),
    )
    cols = jnp.broadcast_to(filt_b2[:, :, None], filt_b2.shape + (LANES,))
    decay = jnp.broadcast_to(decay_rate[:, :, None], (layers, own_chans, LANES))
    skips = jnp.broadcast_to(
        skip_gain.reshape(layers, -1, 8, 1), (layers, own_chans // 8, 8, LANES)
    )

    mats = (w_in, w_out, w_fc, w_proj)
    jobs = [gather_job(small, 0, GATHER_PLANS[0])]
    jobs += [gather_job(mat, 0, plan) for mat, plan in zip(mats, GATHER_PLANS[1:])]
    jobs += [
        column_job(mat, layer, plan)
        for layer in range(1, layers)
        for mat, plan in zip(mats, COLUMN_PLANS)
    ]
    ids = itertools.count()
    sets = [list(range(layers))] if length <= 8192 else [[layer] for layer in range(layers)]
    kept, specs = [], []
    for part in sets:
        of = slice(part[0], part[-1] + 1)
        filters, found = prepare(
            jobs, pos_rows, first_w[of], filt_w2[of], filt_w3[of], cols[of], decay[of], tables, ids
        )
        kept.append(filters[:3])
        specs += [filters[3 + 2 * k : 5 + 2 * k] for k in range(len(part))]
        gathered = found if part is sets[0] else gathered
        jobs = []
    small_all = gathered[0].reshape(devices, -1, LANES)
    gains = jnp.swapaxes(small_all[:, : 2 * layers, :gain_cols], 0, 1).reshape(layers, 2, width)
    convs = jnp.swapaxes(
        small_all[:, 2 * layers : 5 * layers, :conv_cols], 0, 1
    ).reshape(layers, 3, width3)
    conv_cols_of = [
        jnp.pad(convs[layer].T, ((0, 0), (0, LANES - 3))).reshape(blocked + (LANES,))
        for layer in range(layers)
    ]
    plain = lambda parts: parts.reshape(-1, parts.shape[-1])
    weights = {(i, 0): plain(gathered[1 + i]) for i in range(4)}
    columns = {
        (i, layer): gathered[1 + 4 * layer + i] for layer in range(1, layers) for i in range(4)
    }

    def plane_jobs(layer):
        keys = [(3, layer)] if layer else []
        keys = [key for key in keys + [(0, layer + 1), (1, layer + 1), (2, layer + 1)] if key in columns]
        return keys, [plane_job(columns[key], plan) for key, plan in zip(keys, PLANE_PLANS)]

    saved = []
    for layer in range(layers):
        in_mat = weights[0, layer]
        normed, inv_std = layer_norm_parts(stream)
        norm_in = (normed * gains[layer, 0]).astype(bf16)
        mixed = contract(in_mat, norm_in, 0, 1).astype(bf16)
        mixed = mixed.reshape(blocked + (toks,))
        keys, jobs = plane_jobs(layer)
        (long_out, gated, sig_re, sig_im, rim), arrived = mix(
            jobs, layer, mixed, conv_cols_of[layer], specs[layer], skips, tables, ids
        )
        weights.update({key: plain(parts) for key, parts in zip(keys, arrived)})
        out_mat, fc_mat, proj_mat = (weights[i, layer] for i in (1, 2, 3))
        gated = gated.reshape(width, toks)
        middle = stream + contract(gated, out_mat, 0, 0)
        normed_mid, inv_mid = layer_norm_parts(middle)
        hidden_in = (normed_mid * gains[layer, 1]).astype(bf16)
        hidden_pre = product(hidden_in, fc_mat)
        hidden_act = jax.nn.gelu(hidden_pre).astype(bf16)
        saved.append(
            (normed, inv_std, norm_in, mixed, rim, long_out, gated, (sig_re, sig_im))
            + (normed_mid, inv_mid, hidden_in, hidden_pre, hidden_act)
        )
        stream = middle + product(hidden_act, proj_mat)
    mixed_out = stream.astype(bf16)

    grad = cotangent[0].astype(f32)
    summed = {}
    left_over = []
    small_grads = [None] * layers
    taps_grads = [None] * layers

    def parts_of(grad_mat):
        return grad_mat.reshape(devices, -1, grad_mat.shape[1])

    for layer in reversed(range(layers)):
        in_mat, out_mat, fc_mat, proj_mat = (weights[i, layer] for i in range(4))
        (normed, inv_std, norm_in, mixed, rim, long_out, gated, sig) = saved[layer][:8]
        (normed_mid, inv_mid, hidden_in, hidden_pre, hidden_act) = saved[layer][8:]
        grad_top = grad.astype(bf16)
        grad_act = contract(grad_top, proj_mat, 1, 1)
        grad_proj = contract(hidden_act, grad_top, 0, 0).astype(bf16)
        grad_pre = jax.vjp(jax.nn.gelu, hidden_pre)[1](grad_act)[0].astype(bf16)
        grad_hidden = contract(grad_pre, fc_mat, 1, 1)
        grad_fc = contract(hidden_in, grad_pre, 0, 0).astype(bf16)
        grad_gain_mid = jnp.sum(grad_hidden * normed_mid, axis=0)
        grad_middle = grad + norm_back(grad_hidden * gains[layer, 1], normed_mid, inv_mid)
        grad_mix = grad_middle.astype(bf16)
        grad_gated = contract(out_mat, grad_mix, 1, 1).reshape(nblocks, chans, toks)
        grad_out = contract(gated, grad_mix, 1, 0).astype(bf16)
        pending = [
            (key, parts_of(mat)) for key, mat in (((3, layer), grad_proj), ((2, layer), grad_fc), ((1, layer), grad_out))
        ]
        (taps_grads[layer], grad_mixed, grad_conv), arrived = unmix(
            [reduce_job(parts, plan) for (_, parts), plan in zip(pending, REDUCE_PLANS)],
            layer, mixed, conv_cols_of[layer], rim, long_out, grad_gated, specs[layer], sig, skips, tables, ids
        )
        summed.update({key: total for (key, _), total in zip(pending, arrived)})
        grad_mixed = grad_mixed.reshape(width3, toks)
        grad_norm_in = contract(grad_mixed, in_mat, 0, 1)
        grad_in = contract(norm_in, grad_mixed, 0, 1).astype(bf16)
        grad_gain_in = jnp.sum(grad_norm_in * normed, axis=0)
        grad = grad_middle + norm_back(grad_norm_in * gains[layer, 0], normed, inv_std)
        left_over.append(((0, layer), parts_of(grad_in)))
        small_grads[layer] = (
            jnp.stack([grad_gain_in, grad_gain_mid]),
            jnp.swapaxes(grad_conv.reshape(width3, LANES)[:, :3], 0, 1),
        )

    def rows_for(values, cols):
        pieces = jnp.swapaxes(values.reshape(values.shape[0], devices, cols), 0, 1)
        return jnp.pad(pieces, ((0, 0), (0, 0), (0, LANES - cols)))

    small_rows = jnp.concatenate(
        [rows_for(small_grads[layer][0], gain_cols) for layer in range(layers)]
        + [rows_for(small_grads[layer][1], conv_cols) for layer in range(layers)],
        axis=1,
    )
    small_rows = jnp.pad(small_rows, ((0, 0), (0, -small_rows.shape[1] % 8), (0, 0)))
    hidden = filt_w2.shape[1]
    emb = filt_w1.shape[1]
    left_over.insert(0, ("small", small_rows))
    each, shared = hidden + 8, FEATURES + hidden
    by_column, by_all = [], []
    jobs = [reduce_job(parts, plan) for (_, parts), plan in zip(left_over, LAST_PLANS)]
    for part, acts in zip(sets, kept):
        of = slice(part[0], part[-1] + 1)
        (totals,), arrived = last(
            jobs, pos_rows, filt_w2[of], filt_w3[of], decay[of], acts, taps_grads[of], ids
        )
        if part is sets[0]:
            summed.update({key: total for (key, _), total in zip(left_over, arrived)})
        jobs = []
        by_column.append(totals[: len(part) * each].reshape(-1, each, LANES))
        by_all.append(totals[len(part) * each :].reshape(-1, shared, LANES))
    by_column, by_all = jnp.concatenate(by_column), jnp.concatenate(by_all)
    small_sum = summed["small"]
    block = [jnp.stack([summed[i, layer] for layer in range(layers)]) for i in range(4)]
    gains_grad = small_sum[: 2 * layers, :gain_cols].reshape(layers, 2, gain_cols)
    conv_grad = small_sum[2 * layers : 5 * layers, :conv_cols].reshape(layers, 3, conv_cols)
    return (
        mixed_out[None],
        grad[None],
        gains_grad,
        block[0],
        conv_grad,
        block[1],
        block[2],
        block[3],
        by_all[:, :emb, :hidden],
        by_all[:, emb, :hidden],
        by_all[:, FEATURES:, :hidden],
        by_all[:, emb, hidden : 2 * hidden],
        by_column[:, :hidden, :own_chans],
        by_column[:, hidden, :own_chans],
    )


def solution(mesh):
    both = ("batch", "seq")
    in_specs = (
        P("batch", "seq", None),
        P("batch", "seq", None),
        P(None, None, both),
        P(None, both, None),
        P(None, None, both),
        P(None, both, None),
        P(None, both, None),
        P(None, both, None),
        P(),
        P(),
        P(),
        P(),
        P(None, None, "seq"),
        P(None, "seq"),
        P(None, "seq"),
    )
    out_specs = in_specs[:14]
    return jax.shard_map(
        on_device, mesh=mesh, in_specs=in_specs, out_specs=out_specs, check_vma=False
    )
```

time: 826 us -> 623 us (0.75)
  Pallas kernels: 591 us -> 468 us
  matrix products: 152 us -> 103 us
  local copies, waits for them, and re-layouts: 40.8 us -> 23.4 us
  other arithmetic: 24.8 us -> 15.4 us
    pallas_call x11 -> x6, Pallas kernels: 591 us -> 468 us  [fused_call(): pl.pallas_call(kernel, out_shape=list(results) + flat(lambda j: j.results...]
    dot_general x16 -> x0, matrix products: 53.1 us -> none  [the longest x6 22 us: filter_forward(): jnp.dot(second_w.T, first_act, precision=HIGH) + second_b[:, None]]
    unnamed x183 -> x108, local copies, waits for them, and re-layouts: 15.1 us -> 3.71 us
  transfers between devices with their start and end apart: 4 -> 0, of which waited for: 0 -> 0; matrix products, arithmetic and copies ran while one was open for 4% -> 0% of each run, Pallas kernels for 16% -> 0%
where the time goes in v2:
time: 623 us; the launch traced here: 612 us
  Pallas kernels  468 us (75%)
  matrix products  103 us (17%)
  local copies, waits for them, and re-layouts  23.4 us (4%)
  other arithmetic  15.4 us (2%)
    pallas_call x6, Pallas kernels, fused_call(): pl.pallas_call(kernel, out_shape=list(results) + flat(lambda j: j.results...  468 us
    dot_general x20, matrix products, contract(): lax.dot_general(left_mat, right_mat, (((left_dim,), (right_dim,)), ((), (...  84.4 us
    dot_general x4, matrix products, product(): return jnp.dot(left_mat, right_mat, preferred_element_type=f32)  18.7 us

profile of v2, /device:TPU:0, one launch (start us, length us, event | category | flops | bytes accessed | tf_op | source)
XLA Modules:
  0.0 612.1 jit_solution(10401566305938510446)
XLA Ops:
  8.5 83.9 %prepare.1 = (f32[2,4,64,4096]{3,2,1,0:T(8,128)}, f32[2,96,4096]{2,1,0:T(8,128)}, f32[2,96,128]{2,1,0:T(8,128)}, f32[12,256,128]{2,1,0:T(8,128)}, f32[12,256,128...) custom-call(f32[48,4096]{1,0:T(8,128)} %constant.59.clone.refs_0_, ...), custom_call_target="tpu_custom_call" | custom-call | tf_op jit(solution)/shard_map/prepare/pallas_call | solution.py:369
  97.6 5.6 convolution_convert_fusion.7
  103.2 66.5 %mix.2 = (bf16[48,16,512]{2,1,0:T(8,128)(2,1)}, bf16[48,16,512]{2,1,0:T(8,128)(2,1)}, f32[12,256,128]{2,1,0:T(8,128)}, f32[12,256,128]{2,1,0:T(8,128)}, f32[3,48...) custom-call(bf16[3,48,16,512]{3,2,1,0:T(8,128)(2,1)} %bitcast.169, ...), custom_call_target="tpu_custom_call" | custom-call | tf_op jit(solution)/shard_map/mix/pallas_call | solution.py:369
  172.1 5.4 fusion.58
  177.5 3.8 fusion.63
  181.8 3.6 convolution_convert_fusion.6
  185.4 55.7 %mix.3 = (bf16[48,16,512]{2,1,0:T(8,128)(2,1)}, bf16[48,16,512]{2,1,0:T(8,128)(2,1)}, f32[12,256,128]{2,1,0:T(8,128)}, f32[12,256,128]{2,1,0:T(8,128)}, f32[3,48...) custom-call(bf16[3,48,16,512]{3,2,1,0:T(8,128)(2,1)} %bitcast.171, f32[3,48,16,128]{3,2,1,0:T(8,128)} %bitcast.167, ...), custom_call_target="tpu_custom_call" | custom-call | tf_op jit(solution)/shard_map/mix/pallas_call | solution.py:369
  243.5 4.8 fusion.59
  248.4 4.7 fusion.34
  253.1 6.1 %fusion.13 = bf16[512,3072]{1,0:T(8,128)(2,1)S(1)} fusion(f32[512,3072]{1,0:T(8,128)S(1)} %fusion.59, bf16[3072,768]{1,0:T(8,128)(2,1)S(1)} %bitcast.235, bf16[1,512,768]{2,1,0:T(8,128)(2,1)S(1)} %copy-done.10), kind=kOutput, calls=%fused_computation.17 | convolution fusion | flops 2447376384 | bytes 14942208 | tf_op jit(solution)/shard_map/dot_general | solution.py:30
  262.3 4.9 convolution_convert_fusion.5
  267.8 4.8 convolution_convert_fusion.4
  272.7 3.0 convolution_convert_fusion.9
  277.7 83.4 %unmix.2 = (f32[12,32,8,128]{3,2,1,0:T(8,128)}, bf16[3,48,16,512]{3,2,1,0:T(8,128)(2,1)}, f32[3,48,16,128]{3,2,1,0:T(8,128)}, f32[96,768]{1,0:T(8,128)}, f32[24,3072]{1,0:T(8,128)}, /*index=5*/f32[24,768]{1,0:T(8,128)}) custom-call(bf16[3,48,16,512]{3,2,1,0:T(8,128)(2,1)} %bitcast.172, f32[3,48,16,128]{3,2,1,0:T(8,128)} %bitcast.168, ...), custom_call_target="tpu_custom_call" | custom-call | tf_op jit(solution)/shard_map/unmix/pallas_call | solution.py:369
  361.1 5.8 multiply_reduce_fusion.1
  367.5 9.3 %fusion.6 = bf16[512,3072]{1,0:T(8,128)(2,1)S(1)} fusion(f32[512,3072]{1,0:T(8,128)} %copy-done.39, bf16[3072,768]{1,0:T(8,128)(2,1)} %bitcast.224, f32[512,768]{1,0:T(8,128)S(1)} %multiply_add_fusion.1), kind=kOutput, calls=%fused_computation.10 | convolution fusion | flops 2447769600 | bytes 15728640 | tf_op jit(solution)/shard_map/dot_general | solution.py:30
  376.8 3.5 multiply_reduce_fusion.2
  380.3 5.1 convolution_convert_fusion.3
  385.4 4.1 convolution_convert_fusion.1
  390.0 5.9 convolution_convert_fusion.2
  406.3 89.5 %unmix.3 = (f32[12,32,8,128]{3,2,1,0:T(8,128)}, bf16[3,48,16,512]{3,2,1,0:T(8,128)(2,1)}, f32[3,48,16,128]{3,2,1,0:T(8,128)}, f32[96,768]{1,0:T(8,128)}, f32[24,3072]{1,0:T(8,128)}, /*index=5*/f32[24,768]{1,0:T(8,128)}) custom-call(bf16[3,48,16,512]{3,2,1,0:T(8,128)(2,1)} %bitcast.170, f32[3,48,16,128]{3,2,1,0:T(8,128)} %bitcast.166, ...), custom_call_target="tpu_custom_call" | custom-call | tf_op jit(solution)/shard_map/unmix/pallas_call | solution.py:369
  495.9 5.8 fusion.29
  508.9 4.1 convolution_convert_fusion
  513.0 89.4 %last.1 = (f32[368,128]{1,0:T(8,128)}, f32[16,128]{1,0:T(8,128)}, f32[24,2304]{1,0:T(8,128)}, f32[24,2304]{1,0:T(8,128)}) custom-call(f32[48,4096]{1,0:T(8,128)} %constant.59.clone.refs_0_, f32[2,64,64]{2,1,0:T(8,128)} %refs_1_.1, f32[2,64,96]{2,1,0:T(8,128)} %refs_2_.3, f32[2,96,128]{2,1,0:T(8,128)} %broadcast_in_dim.20.refs_5_.refs_3_, ...), custom_call_target="tpu_custom_call" | custom-call | tf_op jit(solution)/shard_map/last/pallas_call | solution.py:369
  (184 shorter events, 51.6 us)
Async XLA Ops:
  0.6 7.1 %copy-start.34 = (f32[2,96]{1,0:T(2,128)S(1)}, f32[2,96]{1,0:T(2,128)}, u32[]{:S(2)}) copy-start(f32[2,96]{1,0:T(2,128)} %param.36) | copy-start | bytes 2308
  0.7 5.6 copy-start.33
  3.4 94.2 %copy-start.20 = (f32[512]{0:T(512)}, f32[512]{0:T(512)S(1)}, u32[]{:S(2)}) copy-start(f32[512]{0:T(512)S(1)} %broadcast_multiply_fusion.11) | copy-start | bytes 6148
  5.0 92.7 %copy-start.28 = (f32[512]{0:T(512)}, f32[512]{0:T(512)S(1)}, u32[]{:S(2)}) copy-start(f32[512]{0:T(512)S(1)} %add_rsqrt_fusion.3) | copy-start | bytes 6148
  94.5 295.0 %copy-start.27 = (f32[768]{0:T(1024)}, f32[768]{0:T(1024)S(1)}, u32[]{:S(2)}) copy-start(f32[768]{0:T(1024)S(1)} %get-tuple-element.148) | copy-start | bytes 9220
  103.2 66.5 %copy-start.8 = (bf16[4,4,2,24,768]{4,3,2,1,0:T(8,128)(2,1)S(1)}, bf16[4,4,2,24,768]{4,3,2,1,0:T(8,128)(2,1)}, u32[]{:S(2)}) copy-start(bf16[4,4,2,24,768]{4,3,2,1,0:T(8,128)(2,1)} %get-tuple-element.68) | copy-start | bytes 3538948
  171.7 5.8 copy-start.2
  171.7 217.7 %copy-start.23 = (f32[512]{0:T(512)}, f32[512]{0:T(512)S(1)}, u32[]{:S(2)}) copy-start(f32[512]{0:T(512)S(1)} %broadcast_multiply_fusion.10) | copy-start | bytes 6148
  171.8 5.7 slice-start.2
  172.1 217.4 %copy-start.31 = (f32[512]{0:T(512)}, f32[512]{0:T(512)S(1)}, u32[]{:S(2)}) copy-start(f32[512]{0:T(512)S(1)} %add_rsqrt_fusion.2) | copy-start | bytes 6148
  185.4 55.7 %copy-start.4 = (bf16[4,4,2,24,768]{4,3,2,1,0:T(8,128)(2,1)S(1)}, bf16[4,4,2,24,768]{4,3,2,1,0:T(8,128)(2,1)}, u32[]{:S(2)}) copy-start(bf16[4,4,2,24,768]{4,3,2,1,0:T(8,128)(2,1)} %get-tuple-element.76) | copy-start | bytes 3538948
  248.4 10.9 %slice-start.4 = ((s8[4718592]{0:T(1024)(128)(4,1)}), s8[4194304]{0:T(1024)(128)(4,1)S(1)}, s32[]{:S(2)}) async-start(s8[4718592]{0:T(1024)(128)(4,1)} %bitcast.229), calls=%async_computation.4 | async-start | bytes 8388608
  253.1 6.2 %slice-start.5 = ((s8[4718592]{0:T(1024)(128)(4,1)}), s8[524288]{0:T(1024)(128)(4,1)S(1)}, s32[]{:S(2)}) async-start(s8[4718592]{0:T(1024)(128)(4,1)} %bitcast.229), calls=%async_computation.5 | async-start | bytes 1048576
  366.9 9.8 %slice-start = ((s8[4718592]{0:T(1024)(128)(4,1)}), s8[4194304]{0:T(1024)(128)(4,1)S(1)}, s32[]{:S(2)}) async-start(s8[4718592]{0:T(1024)(128)(4,1)} %bitcast.221), calls=%async_computation | async-start | bytes 8388608
  366.9 13.3 %slice-start.8 = ((s8[6291456]{0:T(1024)(128)(4,1)}), s8[4194304]{0:T(1024)(128)(4,1)S(1)}, s32[]{:S(2)}) async-start(s8[6291456]{0:T(1024)(128)(4,1)} %bitcast.244), calls=%async_computation.8 | async-start | bytes 8388608
  367.5 9.3 %copy-start.3 = (f32[512,768]{1,0:T(8,128)S(1)}, f32[512,768]{1,0:T(8,128)}, u32[]{:S(2)}) copy-start(f32[512,768]{1,0:T(8,128)} %copy-done.2) | copy-start | bytes 4718596
  367.5 9.3 %slice-start.1 = ((s8[4718592]{0:T(1024)(128)(4,1)}), s8[524288]{0:T(1024)(128)(4,1)S(1)}, s32[]{:S(2)}) async-start(s8[4718592]{0:T(1024)(128)(4,1)} %bitcast.221), calls=%async_computation.1 | async-start | bytes 1048576
  367.5 12.8 %slice-start.9 = ((s8[6291456]{0:T(1024)(128)(4,1)}), s8[2097152]{0:T(1024)(128)(4,1)S(1)}, s32[]{:S(2)}) async-start(s8[6291456]{0:T(1024)(128)(4,1)} %bitcast.244), calls=%async_computation.9 | async-start | bytes 4194304
  390.0 10.1 %copy-start.6 = (f32[3,48,16,128]{3,2,1,0:T(8,128)S(1)}, f32[3,48,16,128]{3,2,1,0:T(8,128)}, u32[]{:S(2)}) copy-start(f32[3,48,16,128]{3,2,1,0:T(8,128)} %get-tuple-element.95) | copy-start | bytes 3538948
  395.9 6.6 %copy-start.11 = (bf16[48,16,512]{2,1,0:T(8,128)(2,1)S(1)}, bf16[48,16,512]{2,1,0:T(8,128)(2,1)}, u32[]{:S(2)}) copy-start(bf16[48,16,512]{2,1,0:T(8,128)(2,1)} %get-tuple-element.67) | copy-start | bytes 2359300
  406.3 89.5 %copy-start.1 = (bf16[1,512,768]{2,1,0:T(8,128)(2,1)S(1)}, bf16[1,512,768]{2,1,0:T(8,128)(2,1)}, u32[]{:S(2)}) copy-start(bf16[1,512,768]{2,1,0:T(8,128)(2,1)} %param.22) | copy-start | bytes 2359300
  406.3 89.5 %copy-start.21 = (f32[512]{0:T(512)S(1)}, f32[512]{0:T(512)}, u32[]{:S(2)}) copy-start(f32[512]{0:T(512)} %copy-done.20) | copy-start | bytes 6148
  406.3 89.5 %copy-start.25 = (f32[768]{0:T(1024)S(1)}, f32[768]{0:T(1024)}, u32[]{:S(2)}) copy-start(f32[768]{0:T(1024)} %copy-done.24) | copy-start | bytes 9220
  406.3 89.5 %copy-start.29 = (f32[512]{0:T(512)S(1)}, f32[512]{0:T(512)}, u32[]{:S(2)}) copy-start(f32[512]{0:T(512)} %copy-done.28) | copy-start | bytes 6148
  (26 other events, 92.2 us)

commit v3 on v2

--- a/solution.py
+++ b/solution.py
@@ -16,8 +16,8 @@
 GATHER_PLANS = [[0, 1, 3, 5, 7, 9, 12], [0, 1, 3, 5, 7, 9, 12], [0, 2, 4, 6, 8, 10, 12], [0, 2, 5, 8, 10, 12, 14], [0, 3, 6, 9, 12, 14, 16]]
 COLUMN_PLANS = [[2, 5, 8, 11, 14], [2, 5, 8, 11, 14], [3, 7, 10, 13, 15], [4, 8, 12, 14, 16]]
 PLANE_PLANS = [[0, 3, 5, 7], [0, 4, 6, 8], [2, 6, 8, 10]]
-REDUCE_PLANS = [[0, 1, 2, 4, 5, 7, 8, 12], [0, 3, 4, 6, 7, 9, 10, 12], [0, 5, 6, 8, 9, 11, 12, 13]]
-LAST_PLANS = [[0, 1, 1, 2, 2, 3, 3, 5], [0, 1, 1, 3, 3, 5, 5, 7], [0, 2, 2, 4, 5, 7, 8, 9]]
+REDUCE_PLANS = [[0, 1, 2, 4, 5, 8, 9, 12], [0, 3, 3, 7, 7, 10, 10, 12], [0, 2, 4, 8, 9, 11, 11, 12]]
+LAST_PLANS = [[0, 1, 1, 4, 4, 7, 7, 9], [0, 2, 2, 5, 5, 7, 8, 9], [0, 2, 2, 5, 5, 7, 8, 9]]
 f32 = jnp.float32
 bf16 = jnp.bfloat16
 
@@ -92,33 +92,57 @@
     return product(jnp.concatenate([high, high, low], axis=1), right[...])
 
 
-def to_points(x, tables, exact):
+def beside(parts):
+    return jnp.concatenate(parts, axis=1) if len(parts) > 1 else parts[0]
+
+
+def below(parts):
+    return jnp.concatenate(parts, axis=0) if len(parts) > 1 else parts[0]
+
+
+def to_points(xs, tables, exact):
     left, right, _, _, twist_cos, twist_sin = tables
     rows, inside = twist_cos.shape
-    split = x.reshape(rows // 8, inside // LANES, 8, LANES)
-    flat = jnp.concatenate([split[:, k] for k in range(inside // LANES)], axis=2).reshape(rows, inside)
+    flat = []
+    for x in xs:
+        split = x.reshape(rows // 8, inside // LANES, 8, LANES)
+        line = [split[:, k] for k in range(inside // LANES)]
+        flat.append((jnp.concatenate(line, axis=2) if len(line) > 1 else line[0]).reshape(rows, inside))
+    flat = beside(flat)
     if exact:
         flat = flat.astype(bf16)
         turned = product(left[:, : 2 * rows], jnp.concatenate([flat, flat], axis=0))
     else:
         turned = left_product(left, flat)
-    re, im = turned[:rows], turned[rows:]
     cos, sin = twist_cos[...], twist_sin[...]
-    both = jnp.concatenate([re * cos + im * sin, im * cos - re * sin], axis=1)
-    points = right_product(both, right)
-    return points[:, :inside], points[:, inside:]
-
-
-def from_points(re, im, tables):
+    both = []
+    for k in range(len(xs)):
+        re, im = [turned[part, k * inside : (k + 1) * inside] for part in (slice(0, rows), slice(rows, 2 * rows))]
+        both.append(jnp.concatenate([re * cos + im * sin, im * cos - re * sin], axis=1))
+    points = right_product(below(both), right)
+    return [
+        (points[k * rows : (k + 1) * rows, :inside], points[k * rows : (k + 1) * rows, inside:])
+        for k in range(len(xs))
+    ]
+
+
+def from_points(pairs, tables):
     _, _, left, right, twist_cos, twist_sin = tables
     rows, inside = twist_cos.shape
-    back = right_product(jnp.concatenate([re, im], axis=1), right)
-    re, im = back[:, :inside], back[:, inside:]
+    back = right_product(below([jnp.concatenate(pair, axis=1) for pair in pairs]), right)
     cos, sin = twist_cos[...], twist_sin[...]
-    both = jnp.concatenate([re * cos - im * sin, re * sin + im * cos], axis=0)
-    flat = left_product(left, both).reshape(rows // 8, 8, inside)
-    split = [flat[:, None, :, k * LANES : (k + 1) * LANES] for k in range(inside // LANES)]
-    return jnp.concatenate(split, axis=1).reshape(-1, 8, LANES)
+    both = []
+    for k in range(len(pairs)):
+        re, im = back[k * rows : (k + 1) * rows, :inside], back[k * rows : (k + 1) * rows, inside:]
+        both.append(jnp.concatenate([re * cos - im * sin, re * sin + im * cos], axis=0))
+    found = left_product(left, beside(both))
+    results = []
+    for k in range(len(pairs)):
+        flat = found[:, k * inside : (k + 1) * inside].reshape(rows // 8, 8, inside)
+        split = [flat[:, None, :, q * LANES : (q + 1) * LANES] for q in range(inside // LANES)]
+        line = jnp.concatenate(split, axis=1) if len(split) > 1 else split[0]
+        results.append(line.reshape(-1, 8, LANES))
+    return results
 
 
 FEATURES = 48
@@ -201,17 +225,18 @@
     squares[layer] += jnp.sum(value * value, axis=1, keepdims=True)
 
 
-def filter_points(layer, group, tables, shaped, squares, spec_re, spec_im):
-    length = shaped.shape[2]
+def filter_points(group, tables, shaped, squares, specs):
+    layers, _, length = shaped.shape
     rows = pl.ds(pl.multiple_of(group * 8, 8), 8)
-    scale = lax.rsqrt(squares[layer, rows, :1] * (1.0 / length) + 1e-05) * length ** (-0.5)
-    value = shaped[layer, rows, :] * scale
-    x = jnp.concatenate(
-        [value[:, i * LANES : (i + 1) * LANES][None] for i in range(length // LANES)], axis=0
-    )
-    re, im = to_points(x, tables, False)
-    spec_re[group] = re
-    spec_im[group] = im
+    xs = []
+    for layer in range(layers):
+        scale = lax.rsqrt(squares[layer, rows, :1] * (1.0 / length) + 1e-05) * length ** (-0.5)
+        value = shaped[layer, rows, :] * scale
+        line = [value[:, i * LANES : (i + 1) * LANES][None] for i in range(length // LANES)]
+        xs.append(jnp.concatenate(line, axis=0))
+    for layer, (re, im) in enumerate(to_points(xs, tables, False)):
+        specs[2 * layer][group] = re
+        specs[2 * layer + 1][group] = im
 
 
 def filter_back_dot(layer, start, shaped, grad_taps, dots):
@@ -301,8 +326,8 @@
         self.tasks = [[task, list(plan)] for task, plan in zip(tasks, plans, strict=True)]
         self.now = 0
 
-    def add(self, task):
-        self.tasks.insert(0, [task, []])
+    def add(self, task, steps):
+        self.tasks.insert(0, [task, list(range(self.now, self.now + steps))])
 
     def step(self, entry):
         if next(entry[0], "end") == "end":
@@ -343,9 +368,11 @@
         return found, alone
     collective_id = next(ids)
     ns = lax.axis_size("seq")
+    stages = [pltpu.VMEM(a.shape, a.dtype) for a in [*arrays, *results]]
+    stages.append(pltpu.SemaphoreType.DMA((max(1, len(stages)),)))
     counts = [len(arrays)] + [len(j.arrays) for j in jobs]
     counts += [len(results)] + [len(j.results) for j in jobs]
-    counts += [len(scratch)] + [len(j.scratch) for j in jobs]
+    counts += [len(scratch)] + [len(j.scratch) for j in jobs] + [len(stages)]
     n = 1 + len(jobs)
 
     def kernel(*refs):
@@ -353,6 +380,9 @@
         for count in counts:
             parts.append(refs[start : start + count])
             start += count
+        *held, sems = parts[3 * n]
+        ins, outs = held[: len(arrays)], held[len(arrays) :]
+        staged = Staged(parts[0], ins, outs, parts[n], sems)
         place = Place(ns)
         greet(place, seq_peers)
         tasks = [
@@ -361,17 +391,18 @@
         ]
         runner = Runner(tasks, [job.plan for job in jobs])
         if body is not None:
-            body(place, runner, parts[0], parts[n], parts[2 * n])
+            body(place, runner, ins, outs, parts[2 * n], staged)
         runner.finish()
+        staged.finish()
 
     hbm = pl.BlockSpec(memory_space=pl.ANY)
     flat = lambda pick: [item for job in jobs for item in pick(job)]
     found = pl.pallas_call(
         kernel,
         out_shape=list(results) + flat(lambda j: j.results),
-        in_specs=whole(counts[0]) + [hbm] * sum(counts[1:n]),
-        out_specs=whole(counts[n]) + [hbm] * sum(counts[n + 1 : 2 * n]),
-        scratch_shapes=list(scratch) + flat(lambda j: j.scratch),
+        in_specs=[hbm] * sum(counts[:n]),
+        out_specs=[hbm] * sum(counts[n : 2 * n]),
+        scratch_shapes=list(scratch) + flat(lambda j: j.scratch) + stages,
         compiler_params=pltpu.CompilerParams(
             collective_id=collective_id, has_side_effects=True, vmem_limit_bytes=VMEM_LIMIT
         ),
@@ -380,8 +411,34 @@
     return found[: counts[n]], found[counts[n] :]
 
 
-def whole(count):
-    return [pl.BlockSpec(memory_space=pltpu.VMEM)] * count
+class Staged:
+    def __init__(self, sources, ins, outs, targets, sems):
+        self.loads = [pltpu.make_async_copy(a, b, sems.at[k]) for k, (a, b) in enumerate(zip(sources, ins))]
+        first = len(self.loads)
+        self.stores = [
+            pltpu.make_async_copy(a, b, sems.at[first + k]) for k, (a, b) in enumerate(zip(outs, targets))
+        ]
+        self.loading = set(range(first))
+        self.storing = set()
+        for load in self.loads:
+            load.start()
+
+    def need(self, *which):
+        for k in which:
+            if k in self.loading:
+                self.loading.remove(k)
+                self.loads[k].wait()
+
+    def ready(self, *which):
+        for k in which:
+            self.storing.add(k)
+            self.stores[k].start()
+
+    def finish(self):
+        self.need(*sorted(self.loading))
+        self.ready(*[k for k in range(len(self.stores)) if k not in self.storing])
+        for store in self.stores:
+            store.wait()
 
 
 def gather_sems(nz):
@@ -795,13 +852,14 @@
         jax.ShapeDtypeStruct((layers, own, LANES), f32),
     ] + [jax.ShapeDtypeStruct(rows, f32)] * (2 * layers)
 
-    def body(place, runner, ins, outs, scratch):
+    def body(place, runner, ins, outs, scratch, staged):
         pos, first, second, third, bias, rate = ins[:6]
         factors = ins[6:]
         acts, shaped, squares = outs[:3]
         specs = outs[3:]
         spans, groups = length // SPAN, own // 8
         squares[...] = jnp.zeros_like(squares)
+        staged.need(0, 1, 2, 3, 4, 5)
         for part in range(8):
             runner.phase()
 
@@ -812,13 +870,14 @@
                         layer, pl.multiple_of(i * SPAN, SPAN), pos, first, second, third, bias, rate, acts, shaped, squares
                     )
 
+        staged.ready(0, 1, 2)
+        staged.need(*range(6, 6 + TABLES))
         for part in range(6):
             runner.phase()
 
             @pl.loop(part * groups // 6, (part + 1) * groups // 6)
             def _(group):
-                for layer in range(layers):
-                    filter_points(layer, group, factors, shaped, squares, *specs[2 * layer : 2 * layer + 2])
+                filter_points(group, factors, shaped, squares, specs)
 
     return fused_call(
         "prepare",
@@ -839,7 +898,7 @@
     each, shared = hidden + 8, FEATURES + hidden
     payload = jax.ShapeDtypeStruct((layers * (each + shared), LANES), f32)
 
-    def body(place, runner, ins, outs, scratch):
+    def body(place, runner, ins, outs, scratch, staged):
         pos, second, third, rate, acts, shaped, squares = ins[:7]
         taps = ins[7:]
         dots, grad_third, grad_second, grad_first, payload_in = scratch[:5]
@@ -847,12 +906,14 @@
             ref[...] = jnp.zeros_like(ref)
         runner.phase()
         spans = length // SPAN
+        staged.need(5, *range(7, 7 + layers))
 
         @pl.loop(0, spans)
         def _(i):
             for layer in range(layers):
                 filter_back_dot(layer, pl.multiple_of(i * SPAN, SPAN), shaped, taps[layer], dots)
 
+        staged.need(0, 1, 2, 3, 4, 6)
         for part in range(8):
             runner.phase()
 
@@ -873,7 +934,7 @@
             start = layers * each + layer * shared
             payload_in[start : start + FEATURES, : 2 * hidden] = grad_first[layer]
             payload_in[start + FEATURES : start + shared, :hidden] = grad_second[layer]
-        runner.add(total_task(place, payload_in, outs[0], scratch[5:]))
+        runner.add(total_task(place, payload_in, outs[0], scratch[5:]), 4)
 
     return fused_call(
         "last",
@@ -971,7 +1032,7 @@
     return 16 if chans % 16 == 0 else chans
 
 
-def mix_body(place, runner, ins, outs, scratch, layer):
+def mix_body(place, runner, ins, outs, scratch, staged, layer):
     mixed, conv, spec_re, spec_im, skip = ins[:5]
     tables = ins[5:]
     long_out, gated, sig_re, sig_im, rim = outs
@@ -1020,9 +1081,12 @@
             (place.b, peer),
         )
 
+    staged.need(0)
     send_edge(place, edge, lambda k: mixed[k, :, :, toks - LANES :].astype(f32), LANES - 2, True)
     runner.phase()
     take_edge(place, edge, True)
+    staged.ready(4)
+    staged.need(1)
     share = by_blocks(groups, 3)
     for first in range(0, groups, share):
 
@@ -1033,6 +1097,7 @@
             value = short_out(mixed, conv, rim, 1, block, share) * short_out(mixed, conv, rim, 2, block, share)
             send_pieces(step, first, value.astype(bf16))
 
+    staged.need(2, 3, 4, *range(5, 5 + TABLES))
     runner.phase()
     for g in range(groups):
 
@@ -1044,16 +1109,16 @@
         def _(i):
             at = pl.ds(pl.multiple_of(i * take, take), take)
             block = chan_in[g, :, at, :].astype(f32)
-            parts = []
-            for j in range(take // 8):
-                index = (g * chans) // 8 + i * (take // 8) + j
-                x = block[:, 8 * j : 8 * j + 8, :]
-                re, im = to_points(x, tables, True)
-                sig_re[index] = re
-                sig_im[index] = im
-                tap_re, tap_im = spec_re[index], spec_im[index]
-                y = from_points(re * tap_re - im * tap_im, re * tap_im + im * tap_re, tables)
-                parts.append(y + skip[layer, index][None] * x)
+            base = (g * chans) // 8 + i * (take // 8)
+            xs = [block[:, 8 * j : 8 * j + 8, :] for j in range(take // 8)]
+            products = []
+            for j, (re, im) in enumerate(to_points(xs, tables, True)):
+                sig_re[base + j] = re
+                sig_im[base + j] = im
+                tap_re, tap_im = spec_re[base + j], spec_im[base + j]
+                products.append((re * tap_re - im * tap_im, re * tap_im + im * tap_re))
+            found = from_points(products, tables)
+            parts = [y + skip[layer, base + j][None] * xs[j] for j, y in enumerate(found)]
             chan_out[g, :, at, :] = jnp.concatenate(parts, axis=1).astype(bf16)
 
         @pl.loop(1, ns)
@@ -1064,6 +1129,7 @@
             tok_in[place.s, g, q] = chan_out[g, place.s * quarters + q]
         runner.phase()
 
+    staged.ready(2, 3)
     for g in range(groups):
 
         @pl.loop(1, ns)
@@ -1114,7 +1180,7 @@
     )
 
 
-def unmix_body(place, runner, ins, outs, scratch, layer):
+def unmix_body(place, runner, ins, outs, scratch, staged, layer):
     mixed, conv, rim, long_out, grad_gated, spec_re, spec_im, sig_re, sig_im, skip = ins[:10]
     tables = ins[10:]
     grad_taps, grad_mixed, grad_conv = outs
@@ -1122,6 +1188,7 @@
     edge = scratch[8:]
     toks = mixed.shape[3]
     runner.phase()
+    staged.need(0, 1, 2, 4)
     ns, groups, quarters, chans, _ = pull.shape
     take = sub_rows(chans)
 
@@ -1173,6 +1240,7 @@
             gated = grad_gated[pl.ds(block, share)].reshape(share * chans, toks)
             send_pieces(step, first, (gated * short_out(mixed, conv, rim, 0, block, share)).astype(bf16))
 
+    staged.need(5, 6, 7, 8, 9, *range(10, 10 + TABLES))
     runner.phase()
     for g in range(groups):
 
@@ -1184,18 +1252,19 @@
         def _(i):
             at = pl.ds(pl.multiple_of(i * take, take), take)
             block = chan_in[g, :, at, :].astype(f32)
-            parts = []
-            for j in range(take // 8):
-                index = (g * chans) // 8 + i * (take // 8) + j
-                x = block[:, 8 * j : 8 * j + 8, :]
-                re, im = to_points(x, tables, True)
-                tap_re, tap_im = spec_re[index], spec_im[index]
-                y = from_points(tap_re * re + tap_im * im, tap_re * im - tap_im * re, tables)
-                parts.append(y + skip[layer, index][None] * x)
-                own_re, own_im = sig_re[index], sig_im[index]
-                grad_taps[index] = from_points(
-                    own_re * re + own_im * im, own_re * im - own_im * re, tables
-                )
+            base = (g * chans) // 8 + i * (take // 8)
+            count = take // 8
+            xs = [block[:, 8 * j : 8 * j + 8, :] for j in range(count)]
+            signals, taps = [], []
+            for j, (re, im) in enumerate(to_points(xs, tables, True)):
+                tap_re, tap_im = spec_re[base + j], spec_im[base + j]
+                own_re, own_im = sig_re[base + j], sig_im[base + j]
+                signals.append((tap_re * re + tap_im * im, tap_re * im - tap_im * re))
+                taps.append((own_re * re + own_im * im, own_re * im - own_im * re))
+            found = from_points(signals + taps, tables)
+            parts = [found[j] + skip[layer, base + j][None] * xs[j] for j in range(count)]
+            for j in range(count):
+                grad_taps[base + j] = found[count + j]
             chan_out[g, :, at, :] = jnp.concatenate(parts, axis=1).astype(bf16)
 
         @pl.loop(1, ns)
@@ -1205,6 +1274,9 @@
         for q in range(quarters):
             tok_in[place.s, g, q] = chan_out[g, place.s * quarters + q]
         runner.phase()
+
+    staged.ready(0)
+    staged.need(3)
 
     @pl.loop(0, ns * groups, unroll=4)
     def _(block):
@@ -1254,6 +1326,7 @@
         lane = lax.broadcasted_iota(jnp.int32, sums[0].shape, 1)
         found = jnp.where(lane == 0, sums[0], jnp.where(lane == 1, sums[1], sums[2]))
         grad_conv[stream] = found.reshape(ns * groups, chans, LANES)
+    staged.ready(2)
     runner.phase()
     take_edge(place, edge, False)
     edge_cols = edge[2]
@@ -1413,19 +1486,21 @@
         normed_mid, inv_mid = layer_norm_parts(middle)
         hidden_in = (normed_mid * gains[layer, 1]).astype(bf16)
         hidden_pre = product(hidden_in, fc_mat)
-        hidden_act = jax.nn.gelu(hidden_pre).astype(bf16)
+        hidden_act = lax.optimization_barrier(jax.nn.gelu(hidden_pre).astype(bf16))
         saved.append(
             (normed, inv_std, norm_in, mixed, rim, long_out, gated, (sig_re, sig_im))
             + (normed_mid, inv_mid, hidden_in, hidden_pre, hidden_act)
         )
         stream = middle + product(hidden_act, proj_mat)
-    mixed_out = stream.astype(bf16)
-
-    grad = cotangent[0].astype(f32)
+    mixed_out, grad = lax.optimization_barrier((stream.astype(bf16), cotangent[0]))
+    grad = grad.astype(f32)
     summed = {}
     left_over = []
     small_grads = [None] * layers
     taps_grads = [None] * layers
+
+    def scattered(parts):
+        return lax.psum_scatter(parts, ("batch", "seq"), scatter_dimension=0, tiled=False).astype(f32)
 
     def parts_of(grad_mat):
         return grad_mat.reshape(devices, -1, grad_mat.shape[1])
@@ -1445,9 +1520,14 @@
         grad_mix = grad_middle.astype(bf16)
         grad_gated = contract(out_mat, grad_mix, 1, 1).reshape(nblocks, chans, toks)
         grad_out = contract(gated, grad_mix, 1, 0).astype(bf16)
-        pending = [
-            (key, parts_of(mat)) for key, mat in (((3, layer), grad_proj), ((2, layer), grad_fc), ((1, layer), grad_out))
-        ]
+        grad_gated, grad_proj = lax.optimization_barrier((grad_gated, grad_proj))
+        if layer == 0:
+            pending = left_over + [((3, layer), parts_of(grad_proj)), ((2, layer), parts_of(grad_fc))]
+            left_over = [((1, layer), parts_of(grad_out))]
+        else:
+            summed[3, layer] = scattered(parts_of(grad_proj))
+            pending = left_over + [((2, layer), parts_of(grad_fc)), ((1, layer), parts_of(grad_out))]
+            left_over = []
         (taps_grads[layer], grad_mixed, grad_conv), arrived = unmix(
             [reduce_job(parts, plan) for (_, parts), plan in zip(pending, REDUCE_PLANS)],
             layer, mixed, conv_cols_of[layer], rim, long_out, grad_gated, specs[layer], sig, skips, tables, ids
@@ -1476,7 +1556,8 @@
     small_rows = jnp.pad(small_rows, ((0, 0), (0, -small_rows.shape[1] % 8), (0, 0)))
     hidden = filt_w2.shape[1]
     emb = filt_w1.shape[1]
-    left_over.insert(0, ("small", small_rows))
+    left_over.reverse()
+    left_over.append(("small", small_rows))
     each, shared = hidden + 8, FEATURES + hidden
     by_column, by_all = [], []
     jobs = [reduce_job(parts, plan) for (_, parts), plan in zip(left_over, LAST_PLANS)]

time: 623 us -> 584 us (0.937)
  Pallas kernels: 468 us -> 413 us
  between operations: 1.82 us -> 15.2 us
    pallas_call x6, Pallas kernels: 468 us -> 413 us  [fused_call(): pl.pallas_call(kernel, out_shape=list(results) + flat(lambda j: j.results...]
  transfers between devices with their start and end apart: 0 -> 1, of which waited for: 0 -> 0; matrix products, arithmetic and copies ran while one was open for 0% -> 14% of each run, Pallas kernels for 0% -> 40%
where the time goes in v3:
time: 584 us; the launch traced here: 573 us
  Pallas kernels  413 us (71%)
  matrix products  107 us (18%)
  local copies, waits for them, and re-layouts  21.9 us (4%)
  other arithmetic  15.9 us (3%)
  between operations  15.2 us (3%)
    pallas_call x6, Pallas kernels, fused_call(): pl.pallas_call(kernel, out_shape=list(results) + flat(lambda j: j.results...  413 us
    dot_general x20, matrix products, contract(): lax.dot_general(left_mat, right_mat, (((left_dim,), (right_dim,)), ((), (...  84.6 us
    dot_general x4, matrix products, product(): return jnp.dot(left_mat, right_mat, preferred_element_type=f32)  22.4 us
  transfers between devices with their start and end apart: 1, of which 0 were waited for; matrix products, arithmetic and copies ran while one was open for 14% of the time, Pallas kernels for 40%

profile of v3, /device:TPU:0, one launch (start us, length us, event | category | flops | bytes accessed | tf_op | source)
XLA Modules:
  0.0 573.2 jit_solution(1938107329563807323)
XLA Ops:
  14.1 76.0 %prepare.1 = (f32[2,4,64,4096]{3,2,1,0:T(8,128)}, f32[2,96,4096]{2,1,0:T(8,128)}, f32[2,96,128]{2,1,0:T(8,128)}, f32[12,256,128]{2,1,0:T(8,128)}, f32[12,256,128...) custom-call(f32[48,4096]{1,0:T(8,128)} %constant.59.clone.refs_0_, ...), custom_call_target="tpu_custom_call" | custom-call | tf_op jit(solution)/shard_map/prepare/pallas_call | solution.py:400
  96.7 3.7 convolution_convert_fusion.7
  101.0 57.7 %mix.2 = (bf16[48,16,512]{2,1,0:T(8,128)(2,1)}, bf16[48,16,512]{2,1,0:T(8,128)(2,1)}, f32[12,256,128]{2,1,0:T(8,128)}, f32[12,256,128]{2,1,0:T(8,128)}, f32[3,48...) custom-call(bf16[3,48,16,512]{3,2,1,0:T(8,128)(2,1)} %bitcast.155, ...), custom_call_target="tpu_custom_call" | custom-call | tf_op jit(solution)/shard_map/mix/pallas_call | solution.py:400
  161.1 9.2 %multiply_convert_fusion.1 = (bf16[512,3072]{1,0:T(8,128)(2,1)S(1)}, f32[512,3072]{1,0:T(8,128)}) fusion(bf16[768,3072]{1,0:T(8,128)(2,1)} %bitcast.208, f32[512,768]{1,0:T(8,128)S(1)} %get-tuple-element.165, f32[768]{0:T(1024)S(1)} %get-tuple-element.158, f32[512]{0:T(512)S(1)} %add_rsqrt_fusion.2, f32[512]{0:T(512)S(1)} %broadcast_multiply_fusion.10), kind=kOutput, calls=%fused_computation.19 | convolution fusion | flops 2431647744 | bytes 15735808 | tf_op jit(solution)/shard_map/dot_general | solution.py:26
  173.5 3.7 convolution_convert_fusion.6
  177.1 47.7 %mix.3 = (bf16[48,16,512]{2,1,0:T(8,128)(2,1)}, bf16[48,16,512]{2,1,0:T(8,128)(2,1)}, f32[12,256,128]{2,1,0:T(8,128)}, f32[12,256,128]{2,1,0:T(8,128)}, f32[3,48...) custom-call(bf16[3,48,16,512]{3,2,1,0:T(8,128)(2,1)} %bitcast.157, f32[3,48,16,128]{3,2,1,0:T(8,128)} %bitcast.153, ...), custom_call_target="tpu_custom_call" | custom-call | tf_op jit(solution)/shard_map/mix/pallas_call | solution.py:400
  227.3 7.0 %multiply_convert_fusion = (bf16[512,3072]{1,0:T(8,128)(2,1)S(1)}, f32[512,3072]{1,0:T(8,128)S(1)}) fusion(bf16[768,3072]{1,0:T(8,128)(2,1)} %bitcast.216, f32[512,768]{1,0:T(8,128)S(1)} %get-tuple-element.171, f32[768]{0:T(1024)S(1)} %get-tuple-element.156, f32[512]{0:T(512)S(1)} %add_rsqrt_fusion, f32[512]{0:T(512)S(1)} %broadcast_multiply_fusion.8), kind=kOutput, calls=%fused_computation.18 | convolution fusion | flops 2431647744 | bytes 15735808 | tf_op jit(solution)/shard_map/dot_general | solution.py:26
  234.3 3.5 add_convert_fusion
  237.9 4.3 convolution_convert_fusion.5
  242.2 6.6 %fusion.13 = bf16[512,3072]{1,0:T(8,128)(2,1)S(1)} fusion(f32[512,3072]{1,0:T(8,128)S(1)} %get-tuple-element.173, bf16[512,768]{1,0:T(8,128)(2,1)S(1)} %bitcast.179, bf16[3072,768]{1,0:T(8,128)(2,1)S(1)} %bitcast.223), kind=kOutput, calls=%fused_computation.17 | convolution fusion | flops 2447376384 | bytes 14942208 | tf_op jit(solution)/shard_map/dot_general | solution.py:30
  254.5 7.3 %convolution_convert_fusion.4 = bf16[768,3072]{1,0:T(8,128)(2,1)} fusion(bf16[512,3072]{1,0:T(8,128)(2,1)} %copy-done.27, f32[512,768]{1,0:T(8,128)} %copy-done, f32[768]{0:T(1024)S(1)} %get-tuple-element.156, f32[512]{0:T(512)S(1)} %add_rsqrt_fusion, f32[512]{0:T(512)S(1)} %broadcast_multiply_fusion.8), kind=kOutput, calls=%fused_computation.24 | convolution fusion | flops 2419851264 | bytes 9444352 | tf_op jit(solution)/shard_map/dot_general | solution.py:30
  263.6 67.1 %unmix.2 = (f32[12,32,8,128]{3,2,1,0:T(8,128)}, bf16[3,48,16,512]{3,2,1,0:T(8,128)(2,1)}, f32[3,48,16,128]{3,2,1,0:T(8,128)}, f32[24,3072]{1,0:T(8,128)}, f32[24,768]{1,0:T(8,128)}) custom-call(bf16[3,48,16,512]{3,2,1,0:T(8,128)(2,1)} %bitcast.158, f32[3,48,16,128]{3,2,1,0:T(8,128)} %bitcast.154, f32[3,48,16,128]{3,2,1,0:T(8,128)} %get-tuple-element.86.refs_2_, ...), custom_call_target="tpu_custom_call" | custom-call | tf_op jit(solution)/shard_map/unmix/pallas_call | solution.py:400
  330.7 5.2 multiply_reduce_fusion.1
  336.5 10.1 %fusion.6 = bf16[512,3072]{1,0:T(8,128)(2,1)S(1)} fusion(f32[512,3072]{1,0:T(8,128)} %get-tuple-element.167, bf16[3072,768]{1,0:T(8,128)(2,1)} %bitcast.212, f32[512,768]{1,0:T(8,128)S(1)} %multiply_add_fusion.1), kind=kOutput, calls=%fused_computation.10 | convolution fusion | flops 2447769600 | bytes 15728640 | tf_op jit(solution)/shard_map/dot_general | solution.py:30
  346.8 4.0 multiply_reduce_fusion.2
  351.5 3.0 multiply_add_fusion
  356.5 4.4 convolution_convert_fusion.3
  360.9 4.2 convolution_convert_fusion.2
  365.1 4.7 convolution_convert_fusion.1
  369.8 98.4 %unmix.3 = (f32[12,32,8,128]{3,2,1,0:T(8,128)}, bf16[3,48,16,512]{3,2,1,0:T(8,128)(2,1)}, f32[3,48,16,128]{3,2,1,0:T(8,128)}, f32[24,2304]{1,0:T(8,128)}, f32[96,768]{1,0:T(8,128)}, /*index=5*/f32[24,3072]{1,0:T(8,128)}) custom-call(bf16[3,48,16,512]{3,2,1,0:T(8,128)(2,1)} %bitcast.156, f32[3,48,16,128]{3,2,1,0:T(8,128)} %bitcast.152, ...), custom_call_target="tpu_custom_call" | custom-call | tf_op jit(solution)/shard_map/unmix/pallas_call | solution.py:400
  468.3 6.3 %fusion.26 = (f32[768]{0:T(1024)S(1)}, f32[512]{0:T(512)S(1)}, f32[512]{0:T(512)S(1)}, f32[512,768]{1,0:T(8,128)}) fusion(bf16[1,512,768]{2,1,0:T(8,128)(2,1)S(1)} %copy-done.2, f32[512]{0:T(512)S(1)} %add_rsqrt_fusion.3, f32[512]{0:T(512)S(1)} %broadcast_multiply_fusion.11, f32[768]{0:T(1024)S(1)} %get-tuple-element.159, bf16[2304,512]{1,0:T(8,128)(2,1)} %bitcast.230, ...), kind=kOutput, calls=%fused_computation.43 | convolution fusion | flops 1815476480 | bytes 8271872 | tf_op jit(solution)/shard_map/dot_general | solution.py:30
  477.3 3.1 convolution_convert_fusion.8
  480.4 4.2 convolution_convert_fusion
  484.6 66.2 %last.1 = (f32[368,128]{1,0:T(8,128)}, f32[24,2304]{1,0:T(8,128)}, f32[24,768]{1,0:T(8,128)}, f32[16,128]{1,0:T(8,128)}) custom-call(f32[48,4096]{1,0:T(8,128)} %constant.59.clone.refs_0_, f32[2,64,64]{2,1,0:T(8,128)} %refs_1_.1, f32[2,64,96]{2,1,0:T(8,128)} %refs_2_.3, f32[2,96,128]{2,1,0:T(8,128)} %broadcast_in_dim.20.refs_5_.refs_3_, ...), custom_call_target="tpu_custom_call" | custom-call | tf_op jit(solution)/shard_map/last/pallas_call | solution.py:400
  (163 shorter events, 50.3 us)
Async XLA Ops:
  7.2 557.0 %reduce-scatter.2.cloned.1.call-start = ((), (), s32[]{:S(2)}) async-start(), calls=%async_computation.1 | async-start | bytes 4866048 | tf_op jit(solution)/shard_map/reduce_scatter | solution.py:1503
  14.1 78.0 %copy-start.1 = (bf16[1,512,768]{2,1,0:T(8,128)(2,1)S(1)}, bf16[1,512,768]{2,1,0:T(8,128)(2,1)}, u32[]{:S(2)}) copy-start(bf16[1,512,768]{2,1,0:T(8,128)(2,1)} %param.22) | copy-start | bytes 2359300
  101.0 57.7 %copy-start.12 = (bf16[4,4,2,24,768]{4,3,2,1,0:T(8,128)(2,1)S(1)}, bf16[4,4,2,24,768]{4,3,2,1,0:T(8,128)(2,1)}, u32[]{:S(2)}) copy-start(bf16[4,4,2,24,768]{4,3,2,1,0:T(8,128)(2,1)} %get-tuple-element.73) | copy-start | bytes 3538948
  160.8 9.5 %copy-start.3 = (f32[512,768]{1,0:T(8,128)}, f32[512,768]{1,0:T(8,128)S(1)}, u32[]{:S(2)}) copy-start(f32[512,768]{1,0:T(8,128)S(1)} %get-tuple-element.165) | copy-start | bytes 4718596
  160.8 9.5 %slice-start.2 = ((s8[4718592]{0:T(1024)(128)(4,1)}), s8[4194304]{0:T(1024)(128)(4,1)S(1)}, s32[]{:S(2)}) async-start(s8[4718592]{0:T(1024)(128)(4,1)} %bitcast.213), calls=%async_computation.4 | async-start | bytes 8388608
  161.1 9.2 %slice-start.3 = ((s8[4718592]{0:T(1024)(128)(4,1)}), s8[524288]{0:T(1024)(128)(4,1)S(1)}, s32[]{:S(2)}) async-start(s8[4718592]{0:T(1024)(128)(4,1)} %bitcast.213), calls=%async_computation.5 | async-start | bytes 1048576
  177.1 47.7 %copy-start.8 = (bf16[4,4,2,24,768]{4,3,2,1,0:T(8,128)(2,1)S(1)}, bf16[4,4,2,24,768]{4,3,2,1,0:T(8,128)(2,1)}, u32[]{:S(2)}) copy-start(bf16[4,4,2,24,768]{4,3,2,1,0:T(8,128)(2,1)} %get-tuple-element.81) | copy-start | bytes 3538948
  226.9 25.0 %copy-start = (f32[512,768]{1,0:T(8,128)}, f32[512,768]{1,0:T(8,128)S(1)}, u32[]{:S(2)}) copy-start(f32[512,768]{1,0:T(8,128)S(1)} %get-tuple-element.171) | copy-start | bytes 4718596
  226.9 7.3 %slice-start.6 = ((s8[4718592]{0:T(1024)(128)(4,1)}), s8[4194304]{0:T(1024)(128)(4,1)S(1)}, s32[]{:S(2)}) async-start(s8[4718592]{0:T(1024)(128)(4,1)} %bitcast.220), calls=%async_computation.8 | async-start | bytes 8388608
  227.3 7.0 %slice-start.7 = ((s8[4718592]{0:T(1024)(128)(4,1)}), s8[524288]{0:T(1024)(128)(4,1)S(1)}, s32[]{:S(2)}) async-start(s8[4718592]{0:T(1024)(128)(4,1)} %bitcast.220), calls=%async_computation.9 | async-start | bytes 1048576
  237.9 11.0 %slice-start.4 = ((s8[4718592]{0:T(1024)(128)(4,1)}), s8[4194304]{0:T(1024)(128)(4,1)S(1)}, s32[]{:S(2)}) async-start(s8[4718592]{0:T(1024)(128)(4,1)} %bitcast.217), calls=%async_computation.6 | async-start | bytes 8388608
  242.2 6.6 %slice-start.5 = ((s8[4718592]{0:T(1024)(128)(4,1)}), s8[524288]{0:T(1024)(128)(4,1)S(1)}, s32[]{:S(2)}) async-start(s8[4718592]{0:T(1024)(128)(4,1)} %bitcast.217), calls=%async_computation.7 | async-start | bytes 1048576
  254.4 7.3 %copy-start.9 = (bf16[48,16,512]{2,1,0:T(8,128)(2,1)S(1)}, bf16[48,16,512]{2,1,0:T(8,128)(2,1)}, u32[]{:S(2)}) copy-start(bf16[48,16,512]{2,1,0:T(8,128)(2,1)} %get-tuple-element.80) | copy-start | bytes 2359300
  336.0 10.7 %slice-start = ((s8[4718592]{0:T(1024)(128)(4,1)}), s8[4194304]{0:T(1024)(128)(4,1)S(1)}, s32[]{:S(2)}) async-start(s8[4718592]{0:T(1024)(128)(4,1)} %bitcast.209), calls=%async_computation.2 | async-start | bytes 8388608
  336.5 10.2 %copy-start.6 = (f32[512,768]{1,0:T(8,128)}, f32[512,768]{1,0:T(8,128)S(1)}, u32[]{:S(2)}) copy-start(f32[512,768]{1,0:T(8,128)S(1)} %multiply_add_fusion.1) | copy-start | bytes 4718596
  336.5 10.2 %copy-start.4 = (f32[512,768]{1,0:T(8,128)S(1)}, f32[512,768]{1,0:T(8,128)}, u32[]{:S(2)}) copy-start(f32[512,768]{1,0:T(8,128)} %copy-done.3) | copy-start | bytes 4718596
  336.5 10.2 %slice-start.1 = ((s8[4718592]{0:T(1024)(128)(4,1)}), s8[524288]{0:T(1024)(128)(4,1)S(1)}, s32[]{:S(2)}) async-start(s8[4718592]{0:T(1024)(128)(4,1)} %bitcast.209), calls=%async_computation.3 | async-start | bytes 1048576
  351.5 5.0 copy-start.29
  369.8 98.5 %copy-start.2 = (bf16[1,512,768]{2,1,0:T(8,128)(2,1)S(1)}, bf16[1,512,768]{2,1,0:T(8,128)(2,1)}, u32[]{:S(2)}) copy-start(bf16[1,512,768]{2,1,0:T(8,128)(2,1)} %param.22) | copy-start | bytes 2359300
  484.6 73.1 %copy-start.19 = (f32[24,768]{1,0:T(8,128)S(1)}, f32[24,768]{1,0:T(8,128)}, u32[]{:S(2)}) copy-start(f32[24,768]{1,0:T(8,128)} %get-tuple-element.110) | copy-start | bytes 221188
  484.6 75.3 %copy-start.15 = (f32[24,3072]{1,0:T(8,128)S(1)}, f32[24,3072]{1,0:T(8,128)}, u32[]{:S(2)}) copy-start(f32[24,3072]{1,0:T(8,128)} %get-tuple-element.112) | copy-start | bytes 884740
  484.6 75.3 %copy-start.17 = (f32[24,3072]{1,0:T(8,128)S(1)}, f32[24,3072]{1,0:T(8,128)}, u32[]{:S(2)}) copy-start(f32[24,3072]{1,0:T(8,128)} %get-tuple-element.111) | copy-start | bytes 884740
  550.8 9.9 %copy-start.18 = (f32[24,2304]{1,0:T(8,128)S(1)}, f32[24,2304]{1,0:T(8,128)}, u32[]{:S(2)}) copy-start(f32[24,2304]{1,0:T(8,128)} %get-tuple-element.108) | copy-start | bytes 663556
  556.4 6.0 %copy-start.10 = (f32[512,768]{1,0:T(8,128)S(1)}, f32[512,768]{1,0:T(8,128)}, u32[]{:S(2)}) copy-start(f32[512,768]{1,0:T(8,128)} %get-tuple-element.177) | copy-start | bytes 4718596
  (15 other events, 49.5 us)
Sparse Core Ops, SparseCore 0:
  254.6 112.6 reduce-scatter.1

commit v4 on v3

--- a/solution.py
+++ b/solution.py
@@ -15,8 +15,10 @@
 VMEM_LIMIT = 58 * 1024 * 1024
 GATHER_PLANS = [[0, 1, 3, 5, 7, 9, 12], [0, 1, 3, 5, 7, 9, 12], [0, 2, 4, 6, 8, 10, 12], [0, 2, 5, 8, 10, 12, 14], [0, 3, 6, 9, 12, 14, 16]]
 COLUMN_PLANS = [[2, 5, 8, 11, 14], [2, 5, 8, 11, 14], [3, 7, 10, 13, 15], [4, 8, 12, 14, 16]]
-PLANE_PLANS = [[0, 3, 5, 7], [0, 4, 6, 8], [2, 6, 8, 10]]
-REDUCE_PLANS = [[0, 1, 2, 4, 5, 8, 9, 12], [0, 3, 3, 7, 7, 10, 10, 12], [0, 2, 4, 8, 9, 11, 11, 12]]
+PLANE_PLANS = [[0, 4, 7, 11], [0, 5, 8, 11], [0, 6, 9, 11]]
+REDUCE_PLANS = [[0, 1, 2, 4, 5, 8, 9, 12], [0, 3, 3, 7, 7, 10, 10, 12]]
+PLANE_REDUCE_PLANS = [[0, 1, 1, 7, 7, 11, 11, 12], [0, 1, 1, 9, 9, 12, 12, 12], [0, 1, 1, 11, 11, 12, 12, 12]]
+CHAIN_PLANS = [[0, 1, 3, 6], [1, 2, 4, 7], [2, 3, 6, 9]]
 LAST_PLANS = [[0, 1, 1, 4, 4, 7, 7, 9], [0, 2, 2, 5, 5, 7, 8, 9], [0, 2, 2, 5, 5, 7, 8, 9]]
 f32 = jnp.float32
 bf16 = jnp.bfloat16
@@ -30,6 +32,18 @@
     return lax.dot_general(
         left_mat, right_mat, (((left_dim,), (right_dim,)), ((), ())), preferred_element_type=f32
     )
+
+
+def gelu(x):
+    return x * (0.5 + 0.5 * jnp.tanh(x * (GELU_SCALE + GELU_SCALE * GELU_CUBE * (x * x))))
+
+
+def gelu_slope(x):
+    square = x * x
+    turn = jnp.tanh(x * (GELU_SCALE + GELU_SCALE * GELU_CUBE * square))
+    half = 0.5 + 0.5 * turn
+    steep = GELU_SCALE + 3.0 * GELU_SCALE * GELU_CUBE * square
+    return half * (1.0 + x * (1.0 - turn) * steep)
 
 
 def layer_norm_parts(stream):
@@ -147,6 +161,8 @@
 
 FEATURES = 48
 SPAN = 512
+GELU_SCALE = math.sqrt(2.0 / math.pi)
+GELU_CUBE = 0.044715
 
 
 def position_rows(length, emb_width):
@@ -210,17 +226,17 @@
     return jnp.exp(lane.astype(f32) * (-1.0 / length) * decay)
 
 
-def filter_span(layer, start, pos, first_w, second_w, third_w, cols, decay, acts, shaped, squares):
+def filter_span(layer, start, pos, first_w, second_w, third_w, rates, acts, shaped, squares):
     length = pos.shape[1]
     at = pl.ds(start, SPAN)
     act, slope = sin_cos(full_dot(first_w[layer], pos[:, at]))
     acts[layer, 0, :, at] = act
     acts[layer, 1, :, at] = slope
-    act, slope = sin_cos(full_dot(second_w[layer], act) + cols[layer][:, :1])
+    act, slope = sin_cos(full_dot(second_w[layer], act) + rates[layer, : act.shape[0], :1])
     acts[layer, 2, :, at] = act
     acts[layer, 3, :, at] = slope
     raw = near_dot(third_w[layer], act, 0, 0)
-    value = raw * window_of(decay[layer][:, :1], start, raw.shape, length)
+    value = raw * window_of(rates[layer, act.shape[0] :, :1], start, raw.shape, length)
     shaped[layer, :, at] = value
     squares[layer] += jnp.sum(value * value, axis=1, keepdims=True)
 
@@ -255,7 +271,7 @@
 
 
 def filter_back_span(
-    layer, start, pos, second_w, third_w, decay, acts, shaped, squares, grad_taps, dots, grads
+    layer, start, pos, second_w, third_w, rates, acts, shaped, squares, grad_taps, dots, grads
 ):
     length = pos.shape[1]
     at = pl.ds(start, SPAN)
@@ -266,7 +282,7 @@
     grad = taps_span(grad_taps, start)
     value = shaped[layer, :, at]
     grad = (grad - value * cross) * (scale * length ** (-0.5))
-    grad = grad * window_of(decay[layer][:, :1], start, grad.shape, length)
+    grad = grad * window_of(rates[layer, second_w.shape[1] :, :1], start, grad.shape, length)
     grad_third[layer] += near_dot(acts[layer, 2, :, at], grad, 1, 1)
     second = near_dot(third_w[layer], grad, 1, 0) * acts[layer, 3, :, at]
     grad_second[layer] += near_dot(acts[layer, 0, :, at], second, 1, 1)
@@ -774,6 +790,178 @@
     yield
 
 
+def plane_reduce_task(place, src, out, scratch):
+    acc, other, box, one, near, send, recv = scratch
+    kind = acc.dtype
+    b, z, c, nz = place.b, place.z, place.c, place.nz
+    bx, by, bd = place.x_peer[0], place.y_peer[0], lax.bitwise_xor(b, 3)
+    far, via_x, via_y = range(3)
+    order = far_first(place)
+    halves = [range(0, nz // 2), range(nz // 2, nz)]
+
+    def add(target, shard, *lanes):
+        value = acc[target, shard].astype(f32)
+        for lane in lanes:
+            value += box[lane, shard].astype(f32)
+        acc[target, shard] = value.astype(kind)
+
+    def move(part, shard, lane, peer):
+        return remote(acc.at[part, shard], box.at[lane, shard], send.at[lane, shard], recv.at[lane, shard], peer)
+
+    def mine(shard):
+        return pltpu.make_async_copy(src.at[:, shard, c], acc.at[:, shard], near.at[0, shard])
+
+    def core(shard):
+        return remote(src.at[:, shard, 1 - c], other.at[:, shard], near.at[1, shard], near.at[2, shard], place.core_peer)
+
+    for shard in order:
+        core(shard).start()
+        mine(shard).start()
+    yield
+    for half in halves:
+        for j in half:
+            shard = order[j]
+            mine(shard).wait()
+            core(shard).wait_recv()
+
+            @pl.loop(0, 4)
+            def _(part):
+                acc[part, shard] = (
+                    acc[part, shard].astype(f32) + other[part, shard].astype(f32)
+                ).astype(kind)
+
+            if j % 2 == 0:
+                move(bd, shard, far, place.x_peer).start()
+                move(bx, shard, via_x, place.x_peer).start()
+            else:
+                move(bd, shard, far, place.y_peer).start()
+                move(by, shard, via_y, place.y_peer).start()
+        yield
+    for half in halves:
+        for j in half:
+            shard = order[j]
+            move(bd, shard, far, place.x_peer).wait_recv()
+            if j % 2 == 0:
+                add(by, shard, far)
+                move(by, shard, via_y, place.y_peer).start()
+            else:
+                add(bx, shard, far)
+                move(bx, shard, via_x, place.x_peer).start()
+        yield
+    for half in halves:
+        for j in half:
+            shard = order[j]
+            move(bx, shard, via_x, place.x_peer).wait_recv()
+            move(by, shard, via_y, place.y_peer).wait_recv()
+            add(b, shard, via_x, via_y)
+        yield
+    result = pltpu.make_async_copy(acc.at[b], out, one.at[0])
+    result.start()
+    for shard in range(nz):
+        core(shard).wait_send()
+        for lane in (far, via_x, via_y):
+            move(b, shard, lane, place.x_peer).wait_send()
+    result.wait()
+    yield
+
+
+def chain_reduce_task(place, src, out, scratch):
+    acc, box, total, one, send, recv = scratch
+    kind = acc.dtype
+    z, nz = place.z, place.nz
+    up, down = range(2)
+    order = far_first(place)
+    halves = [range(0, nz // 2), range(nz // 2, nz)]
+
+    def add(shard, lane):
+        acc[shard] = (acc[shard].astype(f32) + box[lane, shard].astype(f32)).astype(kind)
+
+    def move(shard, lane):
+        peer = place.down_peer if lane else place.up_peer
+        return remote(acc.at[shard], box.at[lane, shard], send.at[lane, shard], recv.at[lane, shard], peer)
+
+    load = pltpu.make_async_copy(src, acc, one.at[0])
+    load.start()
+    yield
+    load.wait()
+    for half in halves:
+        for j in half:
+            shard = order[j]
+
+            @pl.when(z < shard)
+            def _():
+                @pl.when(z > 0)
+                def _():
+                    move(shard, up).wait_recv()
+                    add(shard, up)
+
+                move(shard, up).start()
+
+            @pl.when(z > shard)
+            def _():
+                @pl.when(z + 1 < nz)
+                def _():
+                    move(shard, down).wait_recv()
+                    add(shard, down)
+
+                move(shard, down).start()
+
+        yield
+    total[...] = acc[z].astype(f32)
+
+    @pl.when(z > 0)
+    def _():
+        move(z, up).wait_recv()
+        total[...] += box[up, z].astype(f32)
+
+    @pl.when(z + 1 < nz)
+    def _():
+        move(z, down).wait_recv()
+        total[...] += box[down, z].astype(f32)
+
+    result = pltpu.make_async_copy(total, out, one.at[1])
+    result.start()
+    for shard in range(nz):
+        pl.when(z < shard)(lambda: move(shard, up).wait_send())
+        pl.when(z > shard)(lambda: move(shard, down).wait_send())
+    result.wait()
+    yield
+
+
+def plane_reduce_job(array, plan):
+    nz = lax.axis_size("seq") // 2
+    shape = array.shape[1:]
+    acc, other, box, _, one, near, _, _ = reduce_scratch(nz, shape, array.dtype)
+    sems = pltpu.SemaphoreType.DMA((3, nz))
+    return Job(
+        [array.reshape((4, nz, 2) + shape)],
+        [jax.ShapeDtypeStruct((nz,) + shape, array.dtype)],
+        [acc, other, pltpu.VMEM((3, nz) + shape, array.dtype), one, near, sems, sems],
+        plane_reduce_task,
+        plan,
+    )
+
+
+def chain_reduce_job(array, plan):
+    nz, *shape = array.shape
+    shape = tuple(shape)
+    sems = pltpu.SemaphoreType.DMA((2, nz))
+    return Job(
+        [array],
+        [jax.ShapeDtypeStruct(shape, f32)],
+        [
+            pltpu.VMEM((nz,) + shape, array.dtype),
+            pltpu.VMEM((2, nz) + shape, array.dtype),
+            pltpu.VMEM(shape, f32),
+            pltpu.SemaphoreType.DMA((2,)),
+            sems,
+            sems,
+        ],
+        chain_reduce_task,
+        plan,
+    )
+
+
 def reduce_job(array, plan):
     nz = lax.axis_size("seq") // 2
     shape = array.shape[1:]
@@ -788,61 +976,65 @@
 
 def total_scratch(nz, shape, shared):
     return [
-        pltpu.VMEM((3,) + shape, f32),
-        pltpu.VMEM((2,) + shape, f32),
-        pltpu.VMEM((2, nz, shared, LANES), f32),
+        pltpu.VMEM((4,) + shape, bf16),
+        pltpu.VMEM((2, shared, LANES), bf16),
+        pltpu.VMEM((nz + 1, shared, LANES), bf16),
+        pltpu.VMEM(shape, f32),
         pltpu.SemaphoreType.DMA((2, 3)),
         pltpu.SemaphoreType.DMA((2, nz)),
     ]
 
 
 def total_task(place, src, out, scratch):
-    box, sums, lines, pair, chain = scratch
+    box, pair_box, lines, sums, pair, chain = scratch
     z, c, nz = place.z, place.c, place.nz
     rows = src.shape[0]
-    shared = lines.shape[2]
+    shared = lines.shape[1]
     tail = pl.ds(rows - shared, shared)
 
     def swap(source, dst, i, peer):
         return remote(source, dst, pair.at[0, i], pair.at[1, i], peer)
 
-    first = swap(src, box.at[0], 0, place.x_peer)
+    box[0] = src[...].astype(bf16)
+    first = swap(box.at[0], box.at[2], 0, place.x_peer)
     first.start()
     yield
     first.wait()
-    sums[0] = src[...] + box[0]
-    second = swap(sums.at[0], box.at[1], 1, place.y_peer)
+    sums[...] = box[0].astype(f32) + box[2].astype(f32)
+    box[1] = sums[...].astype(bf16)
+    second = swap(box.at[1], box.at[3], 1, place.y_peer)
     second.start()
     yield
     second.wait()
-    sums[1] = sums[0] + box[1]
-    third = swap(sums.at[1, tail], box.at[2, tail], 2, place.core_peer)
+    sums[...] = box[1].astype(f32) + box[3].astype(f32)
+    pair_box[0] = sums[tail].astype(bf16)
+    third = swap(pair_box.at[0], pair_box.at[1], 2, place.core_peer)
     third.start()
     yield
     third.wait()
-    lines[0, z] = sums[1, tail] + box[2, tail]
+    lines[nz] = (pair_box[0].astype(f32) + pair_box[1].astype(f32)).astype(bf16)
 
     def along(step):
         peer = lax.rem(z + step, nz)
-        return remote(lines.at[0, z], lines.at[1, z], chain.at[0, step], chain.at[1, step], (place.b, 2 * peer + c))
+        return remote(lines.at[nz], lines.at[z], chain.at[0, step], chain.at[1, step], (place.b, 2 * peer + c))
 
     for step in range(1, nz):
         along(step).start()
-    lines[1, z] = lines[0, z]
+    lines[z] = lines[nz]
     yield
     for step in range(1, nz):
         along(step).wait_recv()
-    value = lines[1, 0]
+    value = lines[0].astype(f32)
     for shard in range(1, nz):
-        value = value + lines[1, shard]
-    out[: rows - shared] = sums[1, : rows - shared]
+        value = value + lines[shard].astype(f32)
+    out[: rows - shared] = sums[: rows - shared]
     out[tail] = value
     for step in range(1, nz):
         along(step).wait_send()
     yield
 
 
-def prepare(jobs, pos_rows, first_w, second_w, third_w, cols, decay, tables, ids):
+def prepare(jobs, pos_rows, first_w, second_w, third_w, rates, tables, ids):
     layers, hidden, own = third_w.shape
     length = pos_rows.shape[1]
     rows = (own // 8,) + tables[4].shape
@@ -853,13 +1045,13 @@
     ] + [jax.ShapeDtypeStruct(rows, f32)] * (2 * layers)
 
     def body(place, runner, ins, outs, scratch, staged):
-        pos, first, second, third, bias, rate = ins[:6]
-        factors = ins[6:]
+        pos, first, second, third, rate = ins[:5]
+        factors = ins[5:]
         acts, shaped, squares = outs[:3]
         specs = outs[3:]
         spans, groups = length // SPAN, own // 8
         squares[...] = jnp.zeros_like(squares)
-        staged.need(0, 1, 2, 3, 4, 5)
+        staged.need(0, 1, 2, 3, 4)
         for part in range(8):
             runner.phase()
 
@@ -867,11 +1059,11 @@
             def _(i):
                 for layer in range(layers):
                     filter_span(
-                        layer, pl.multiple_of(i * SPAN, SPAN), pos, first, second, third, bias, rate, acts, shaped, squares
+                        layer, pl.multiple_of(i * SPAN, SPAN), pos, first, second, third, rate, acts, shaped, squares
                     )
 
         staged.ready(0, 1, 2)
-        staged.need(*range(6, 6 + TABLES))
+        staged.need(*range(5, 5 + TABLES))
         for part in range(6):
             runner.phase()
 
@@ -882,7 +1074,7 @@
     return fused_call(
         "prepare",
         body,
-        [pos_rows, first_w, second_w, third_w, cols, decay, *tables],
+        [pos_rows, first_w, second_w, third_w, rates, *tables],
         results,
         [],
         jobs,
@@ -891,11 +1083,11 @@
     )
 
 
-def last(jobs, pos_rows, second_w, third_w, decay, kept, grad_taps, ids):
+def last(jobs, pos_rows, second_w, third_w, rates, kept, grad_taps, ids):
     layers, hidden, own = third_w.shape
     length = pos_rows.shape[1]
     nz = lax.axis_size("seq") // 2
-    each, shared = hidden + 8, FEATURES + hidden
+    each, shared = hidden + 8, hidden
     payload = jax.ShapeDtypeStruct((layers * (each + shared), LANES), f32)
 
     def body(place, runner, ins, outs, scratch, staged):
@@ -932,14 +1124,17 @@
             pick = jnp.where(lax.broadcasted_iota(jnp.int32, (8, LANES), 1) == 0, 1.0, 0.0)
             payload_in[start + hidden : start + each, :own] = near_dot(pick, lag, 1, 1)
             start = layers * each + layer * shared
-            payload_in[start : start + FEATURES, : 2 * hidden] = grad_first[layer]
-            payload_in[start + FEATURES : start + shared, :hidden] = grad_second[layer]
+            payload_in[start : start + FEATURES, :hidden] = grad_first[layer][:, :hidden]
+            payload_in[start + FEATURES : start + FEATURES + 8, :hidden] = pltpu.roll(
+                grad_first[layer][FEATURES - 16 : FEATURES - 8], hidden, 1
+            )[:, :hidden]
+            payload_in[start : start + hidden, hidden : 2 * hidden] = grad_second[layer]
         runner.add(total_task(place, payload_in, outs[0], scratch[5:]), 4)
 
     return fused_call(
         "last",
         body,
-        [pos_rows, second_w, third_w, decay, *kept, *grad_taps],
+        [pos_rows, second_w, third_w, rates, *kept, *grad_taps],
         [payload],
         [
             pltpu.VMEM((layers, own, LANES), f32),
@@ -1422,8 +1617,9 @@
         jnp.concatenate([filt_w1, filt_b1[:, None]], axis=1),
         ((0, 0), (0, FEATURES - filt_w1.shape[1] - 1), (0, 0)),
     )
-    cols = jnp.broadcast_to(filt_b2[:, :, None], filt_b2.shape + (LANES,))
-    decay = jnp.broadcast_to(decay_rate[:, :, None], (layers, own_chans, LANES))
+    hidden = filt_w2.shape[1]
+    both = jnp.concatenate([filt_b2, decay_rate], axis=1)
+    rates = jnp.broadcast_to(both[:, :, None], both.shape + (LANES,))
     skips = jnp.broadcast_to(
         skip_gain.reshape(layers, -1, 8, 1), (layers, own_chans // 8, 8, LANES)
     )
@@ -1442,7 +1638,7 @@
     for part in sets:
         of = slice(part[0], part[-1] + 1)
         filters, found = prepare(
-            jobs, pos_rows, first_w[of], filt_w2[of], filt_w3[of], cols[of], decay[of], tables, ids
+            jobs, pos_rows, first_w[of], filt_w2[of], filt_w3[of], rates[of], tables, ids
         )
         kept.append(filters[:3])
         specs += [filters[3 + 2 * k : 5 + 2 * k] for k in range(len(part))]
@@ -1486,7 +1682,7 @@
         normed_mid, inv_mid = layer_norm_parts(middle)
         hidden_in = (normed_mid * gains[layer, 1]).astype(bf16)
         hidden_pre = product(hidden_in, fc_mat)
-        hidden_act = lax.optimization_barrier(jax.nn.gelu(hidden_pre).astype(bf16))
+        hidden_act = lax.optimization_barrier(gelu(hidden_pre).astype(bf16))
         saved.append(
             (normed, inv_std, norm_in, mixed, rim, long_out, gated, (sig_re, sig_im))
             + (normed_mid, inv_mid, hidden_in, hidden_pre, hidden_act)
@@ -1512,7 +1708,7 @@
         grad_top = grad.astype(bf16)
         grad_act = contract(grad_top, proj_mat, 1, 1)
         grad_proj = contract(hidden_act, grad_top, 0, 0).astype(bf16)
-        grad_pre = jax.vjp(jax.nn.gelu, hidden_pre)[1](grad_act)[0].astype(bf16)
+        grad_pre = (grad_act * gelu_slope(hidden_pre)).astype(bf16)
         grad_hidden = contract(grad_pre, fc_mat, 1, 1)
         grad_fc = contract(hidden_in, grad_pre, 0, 0).astype(bf16)
         grad_gain_mid = jnp.sum(grad_hidden * normed_mid, axis=0)
@@ -1529,10 +1725,15 @@
             pending = left_over + [((2, layer), parts_of(grad_fc)), ((1, layer), parts_of(grad_out))]
             left_over = []
         (taps_grads[layer], grad_mixed, grad_conv), arrived = unmix(
-            [reduce_job(parts, plan) for (_, parts), plan in zip(pending, REDUCE_PLANS)],
+            [reduce_job(parts, plan) for (_, parts), plan in zip(pending, REDUCE_PLANS)]
+            if layer
+            else [plane_reduce_job(parts, plan) for (_, parts), plan in zip(pending, PLANE_REDUCE_PLANS)],
             layer, mixed, conv_cols_of[layer], rim, long_out, grad_gated, specs[layer], sig, skips, tables, ids
         )
-        summed.update({key: total for (key, _), total in zip(pending, arrived)})
+        if layer == 0:
+            half_way = [(key, part) for (key, _), part in zip(pending, arrived)]
+        else:
+            summed.update({key: total for (key, _), total in zip(pending, arrived)})
         grad_mixed = grad_mixed.reshape(width3, toks)
         grad_norm_in = contract(grad_mixed, in_mat, 0, 1)
         grad_in = contract(norm_in, grad_mixed, 0, 1).astype(bf16)
@@ -1554,20 +1755,20 @@
         axis=1,
     )
     small_rows = jnp.pad(small_rows, ((0, 0), (0, -small_rows.shape[1] % 8), (0, 0)))
-    hidden = filt_w2.shape[1]
     emb = filt_w1.shape[1]
     left_over.reverse()
     left_over.append(("small", small_rows))
-    each, shared = hidden + 8, FEATURES + hidden
+    each, shared = hidden + 8, hidden
     by_column, by_all = [], []
     jobs = [reduce_job(parts, plan) for (_, parts), plan in zip(left_over, LAST_PLANS)]
+    jobs += [chain_reduce_job(part, plan) for (_, part), plan in zip(half_way, CHAIN_PLANS)]
     for part, acts in zip(sets, kept):
         of = slice(part[0], part[-1] + 1)
         (totals,), arrived = last(
-            jobs, pos_rows, filt_w2[of], filt_w3[of], decay[of], acts, taps_grads[of], ids
+            jobs, pos_rows, filt_w2[of], filt_w3[of], rates[of], acts, taps_grads[of], ids
         )
         if part is sets[0]:
-            summed.update({key: total for (key, _), total in zip(left_over, arrived)})
+            summed.update({key: total for (key, _), total in zip(left_over + half_way, arrived)})
         jobs = []
         by_column.append(totals[: len(part) * each].reshape(-1, each, LANES))
         by_all.append(totals[len(part) * each :].reshape(-1, shared, LANES))
@@ -1587,8 +1788,8 @@
         block[3],
         by_all[:, :emb, :hidden],
         by_all[:, emb, :hidden],
-        by_all[:, FEATURES:, :hidden],
-        by_all[:, emb, hidden : 2 * hidden],
+        by_all[:, :, hidden : 2 * hidden],
+        by_all[:, FEATURES + emb - 32, :hidden],
         by_column[:, :hidden, :own_chans],
         by_column[:, hidden, :own_chans],
     )

time: 584 us -> 551 us (0.943)
  Pallas kernels: 413 us -> 387 us
    pallas_call x6, Pallas kernels: 413 us -> 387 us  [fused_call(): pl.pallas_call(kernel, out_shape=list(results) + flat(lambda j: j.results...]
  transfers between devices with their start and end apart: 1 -> 1, of which waited for: 0 -> 0; matrix products, arithmetic and copies ran while one was open for 14% -> 14% of each run, Pallas kernels for 40% -> 39%
where the time goes in v4:
time: 551 us; the launch traced here: 542 us
  Pallas kernels  387 us (70%)
  matrix products  104 us (19%)
  local copies, waits for them, and re-layouts  19.9 us (4%)
  other arithmetic  16.7 us (3%)
  between operations  15.2 us (3%)
    pallas_call x6, Pallas kernels, fused_call(): pl.pallas_call(kernel, out_shape=list(results) + flat(lambda j: j.results...  387 us
    dot_general x20, matrix products, contract(): lax.dot_general(left_mat, right_mat, (((left_dim,), (right_dim,)), ((), (...  81.9 us
    dot_general x4, matrix products, product(): return jnp.dot(left_mat, right_mat, preferred_element_type=f32)  22 us
  transfers between devices with their start and end apart: 1, of which 0 were waited for; matrix products, arithmetic and copies ran while one was open for 14% of the time, Pallas kernels for 39%

profile of v4, /device:TPU:0, one launch (start us, length us, event | category | flops | bytes accessed | tf_op | source)
XLA Modules:
  0.0 542.3 jit_solution(16078198638816448268)
XLA Ops:
  12.8 76.0 %prepare.1 = (f32[2,4,64,4096]{3,2,1,0:T(8,128)}, f32[2,96,4096]{2,1,0:T(8,128)}, f32[2,96,128]{2,1,0:T(8,128)}, f32[12,256,128]{2,1,0:T(8,128)}, f32[12,256,128...) custom-call(f32[48,4096]{1,0:T(8,128)} %constant.56.clone.refs_0_, ...), custom_call_target="tpu_custom_call" | custom-call | tf_op jit(solution)/shard_map/prepare/pallas_call | solution.py:416
  95.4 3.7 convolution_convert_fusion.7
  99.8 50.8 %mix.2 = (bf16[48,16,512]{2,1,0:T(8,128)(2,1)}, bf16[48,16,512]{2,1,0:T(8,128)(2,1)}, f32[12,256,128]{2,1,0:T(8,128)}, f32[12,256,128]{2,1,0:T(8,128)}, f32[3,48...) custom-call(bf16[3,48,16,512]{3,2,1,0:T(8,128)(2,1)} %bitcast.155, ...), custom_call_target="tpu_custom_call" | custom-call | tf_op jit(solution)/shard_map/mix/pallas_call | solution.py:416
  153.0 9.0 %multiply_convert_fusion.3 = (bf16[512,3072]{1,0:T(8,128)(2,1)S(1)}, f32[512,3072]{1,0:T(8,128)}) fusion(bf16[768,3072]{1,0:T(8,128)(2,1)} %bitcast.208, f32[512,768]{1,0:T(8,128)S(1)} %get-tuple-element.171, f32[768]{0:T(1024)S(1)} %get-tuple-element.164, f32[512]{0:T(512)S(1)} %add_rsqrt_fusion.2, f32[512]{0:T(512)S(1)} %broadcast_multiply_fusion.10), kind=kOutput, calls=%fused_computation.6 | convolution fusion | flops 2430074880 | bytes 15735808 | tf_op jit(solution)/shard_map/dot_general | solution.py:28
  165.1 3.7 convolution_convert_fusion.6
  168.8 48.4 %mix.3 = (bf16[48,16,512]{2,1,0:T(8,128)(2,1)}, bf16[48,16,512]{2,1,0:T(8,128)(2,1)}, f32[12,256,128]{2,1,0:T(8,128)}, f32[12,256,128]{2,1,0:T(8,128)}, f32[3,48...) custom-call(bf16[3,48,16,512]{3,2,1,0:T(8,128)(2,1)} %bitcast.157, f32[3,48,16,128]{3,2,1,0:T(8,128)} %bitcast.153, ...), custom_call_target="tpu_custom_call" | custom-call | tf_op jit(solution)/shard_map/mix/pallas_call | solution.py:416
  219.7 6.8 %multiply_convert_fusion.2 = (bf16[512,3072]{1,0:T(8,128)(2,1)S(1)}, f32[512,3072]{1,0:T(8,128)S(1)}) fusion(bf16[768,3072]{1,0:T(8,128)(2,1)} %bitcast.216, f32[512,768]{1,0:T(8,128)S(1)} %get-tuple-element.177, f32[768]{0:T(1024)S(1)} %get-tuple-element.162, f32[512]{0:T(512)S(1)} %add_rsqrt_fusion, f32[512]{0:T(512)S(1)} %broadcast_multiply_fusion.8), kind=kOutput, calls=%fused_computation.2 | convolution fusion | flops 2430074880 | bytes 15735808 | tf_op jit(solution)/shard_map/dot_general | solution.py:28
  226.5 3.5 add_convert_fusion
  230.0 4.3 convolution_convert_fusion.5
  234.3 5.1 multiply_convert_fusion.1
  245.1 7.3 %convolution_convert_fusion.4 = bf16[768,3072]{1,0:T(8,128)(2,1)} fusion(bf16[512,3072]{1,0:T(8,128)(2,1)} %copy-done.26, f32[512,768]{1,0:T(8,128)} %copy-done, f32[768]{0:T(1024)S(1)} %get-tuple-element.162, f32[512]{0:T(512)S(1)} %add_rsqrt_fusion, f32[512]{0:T(512)S(1)} %broadcast_multiply_fusion.8), kind=kOutput, calls=%fused_computation.14 | convolution fusion | flops 2419851264 | bytes 9444352 | tf_op jit(solution)/shard_map/dot_general | solution.py:32
  254.3 66.6 %unmix.2 = (f32[12,32,8,128]{3,2,1,0:T(8,128)}, bf16[3,48,16,512]{3,2,1,0:T(8,128)(2,1)}, f32[3,48,16,128]{3,2,1,0:T(8,128)}, f32[24,3072]{1,0:T(8,128)}, f32[24,768]{1,0:T(8,128)}) custom-call(bf16[3,48,16,512]{3,2,1,0:T(8,128)(2,1)} %bitcast.158, f32[3,48,16,128]{3,2,1,0:T(8,128)} %bitcast.154, f32[3,48,16,128]{3,2,1,0:T(8,128)} %get-tuple-element.89.refs_2_, ...), custom_call_target="tpu_custom_call" | custom-call | tf_op jit(solution)/shard_map/unmix/pallas_call | solution.py:416
  320.9 5.2 multiply_reduce_fusion.1
  326.7 8.9 %multiply_convert_fusion = bf16[512,3072]{1,0:T(8,128)(2,1)S(1)} fusion(f32[512,3072]{1,0:T(8,128)} %get-tuple-element.173, bf16[3072,768]{1,0:T(8,128)(2,1)} %bitcast.212, f32[512,768]{1,0:T(8,128)S(1)} %multiply_add_fusion.5), kind=kOutput, calls=%fused_computation | convolution fusion | flops 2439905280 | bytes 15728640 | tf_op jit(solution)/shard_map/dot_general | solution.py:32
  335.8 4.0 multiply_reduce_fusion.2
  340.5 3.0 multiply_add_fusion.4
  345.5 4.4 convolution_convert_fusion.3
  349.9 4.2 convolution_convert_fusion.2
  354.1 4.7 convolution_convert_fusion.1
  358.8 76.9 %unmix.3 = (f32[12,32,8,128]{3,2,1,0:T(8,128)}, bf16[3,48,16,512]{3,2,1,0:T(8,128)(2,1)}, f32[3,48,16,128]{3,2,1,0:T(8,128)}, bf16[4,24,2304]{2,1,0:T(8,128)(2,1...) custom-call(bf16[3,48,16,512]{3,2,1,0:T(8,128)(2,1)} %bitcast.156, f32[3,48,16,128]{3,2,1,0:T(8,128)} %bitcast.152, ...), custom_call_target="tpu_custom_call" | custom-call | tf_op jit(solution)/shard_map/unmix/pallas_call | solution.py:416
  435.8 6.3 %fusion.12 = (f32[768]{0:T(1024)S(1)}, f32[512]{0:T(512)S(1)}, f32[512]{0:T(512)S(1)}, f32[512,768]{1,0:T(8,128)}) fusion(bf16[1,512,768]{2,1,0:T(8,128)(2,1)S(1)} %copy-done.2, f32[512]{0:T(512)S(1)} %add_rsqrt_fusion.3, f32[512]{0:T(512)S(1)} %broadcast_multiply_fusion.11, f32[768]{0:T(1024)S(1)} %get-tuple-element.165, bf16[2304,512]{1,0:T(8,128)(2,1)} %bitcast.230, ...), kind=kOutput, calls=%fused_computation.33 | convolution fusion | flops 1815476480 | bytes 8271872 | tf_op jit(solution)/shard_map/dot_general | solution.py:32
  444.7 3.1 convolution_convert_fusion.8
  447.9 4.2 convolution_convert_fusion
  452.0 67.7 %last.1 = (f32[272,128]{1,0:T(8,128)}, f32[24,2304]{1,0:T(8,128)}, f32[24,768]{1,0:T(8,128)}, f32[16,128]{1,0:T(8,128)}, f32[24,2304]{1,0:T(8,128)}, /*index=5*/f32[96,768]{1,0:T(8,128)}, f32[24,3072]{1,0:T(8,128)}) custom-call(f32[48,4096]{1,0:T(8,128)} %constant.56.clone.refs_0_, f32[2,64,64]{2,1,0:T(8,128)} %refs_1_.1, f32[2,64,96]{2,1,0:T(8,128)} %refs_2_.3, ...), custom_call_target="tpu_custom_call" | custom-call | tf_op jit(solution)/shard_map/last/pallas_call | solution.py:416
  (161 shorter events, 49.1 us)
Async XLA Ops:
  7.2 526.0 %reduce-scatter.2.cloned.1.call-start = ((), (), s32[]{:S(2)}) async-start(), calls=%async_computation.1 | async-start | bytes 4866048 | tf_op jit(solution)/shard_map/reduce_scatter | solution.py:1699
  12.8 78.0 %copy-start.1 = (bf16[1,512,768]{2,1,0:T(8,128)(2,1)S(1)}, bf16[1,512,768]{2,1,0:T(8,128)(2,1)}, u32[]{:S(2)}) copy-start(bf16[1,512,768]{2,1,0:T(8,128)(2,1)} %param.22) | copy-start | bytes 2359300
  99.8 50.8 %copy-start.12 = (bf16[4,4,2,24,768]{4,3,2,1,0:T(8,128)(2,1)S(1)}, bf16[4,4,2,24,768]{4,3,2,1,0:T(8,128)(2,1)}, u32[]{:S(2)}) copy-start(bf16[4,4,2,24,768]{4,3,2,1,0:T(8,128)(2,1)} %get-tuple-element.76) | copy-start | bytes 3538948
  152.6 9.4 %copy-start.3 = (f32[512,768]{1,0:T(8,128)}, f32[512,768]{1,0:T(8,128)S(1)}, u32[]{:S(2)}) copy-start(f32[512,768]{1,0:T(8,128)S(1)} %get-tuple-element.171) | copy-start | bytes 4718596
  152.6 9.4 %slice-start.2 = ((s8[4718592]{0:T(1024)(128)(4,1)}), s8[4194304]{0:T(1024)(128)(4,1)S(1)}, s32[]{:S(2)}) async-start(s8[4718592]{0:T(1024)(128)(4,1)} %bitcast.213), calls=%async_computation.4 | async-start | bytes 8388608
  153.0 9.0 %slice-start.3 = ((s8[4718592]{0:T(1024)(128)(4,1)}), s8[524288]{0:T(1024)(128)(4,1)S(1)}, s32[]{:S(2)}) async-start(s8[4718592]{0:T(1024)(128)(4,1)} %bitcast.213), calls=%async_computation.5 | async-start | bytes 1048576
  168.8 48.5 %copy-start.8 = (bf16[4,4,2,24,768]{4,3,2,1,0:T(8,128)(2,1)S(1)}, bf16[4,4,2,24,768]{4,3,2,1,0:T(8,128)(2,1)}, u32[]{:S(2)}) copy-start(bf16[4,4,2,24,768]{4,3,2,1,0:T(8,128)(2,1)} %get-tuple-element.84) | copy-start | bytes 3538948
  219.3 23.2 %copy-start = (f32[512,768]{1,0:T(8,128)}, f32[512,768]{1,0:T(8,128)S(1)}, u32[]{:S(2)}) copy-start(f32[512,768]{1,0:T(8,128)S(1)} %get-tuple-element.177) | copy-start | bytes 4718596
  219.3 7.1 %slice-start.6 = ((s8[4718592]{0:T(1024)(128)(4,1)}), s8[4194304]{0:T(1024)(128)(4,1)S(1)}, s32[]{:S(2)}) async-start(s8[4718592]{0:T(1024)(128)(4,1)} %bitcast.220), calls=%async_computation.8 | async-start | bytes 8388608
  219.6 6.8 %slice-start.7 = ((s8[4718592]{0:T(1024)(128)(4,1)}), s8[524288]{0:T(1024)(128)(4,1)S(1)}, s32[]{:S(2)}) async-start(s8[4718592]{0:T(1024)(128)(4,1)} %bitcast.220), calls=%async_computation.9 | async-start | bytes 1048576
  230.0 9.5 %slice-start.4 = ((s8[4718592]{0:T(1024)(128)(4,1)}), s8[4194304]{0:T(1024)(128)(4,1)S(1)}, s32[]{:S(2)}) async-start(s8[4718592]{0:T(1024)(128)(4,1)} %bitcast.217), calls=%async_computation.6 | async-start | bytes 8388608
  234.3 5.2 slice-start.5
  245.1 7.3 %copy-start.9 = (bf16[48,16,512]{2,1,0:T(8,128)(2,1)S(1)}, bf16[48,16,512]{2,1,0:T(8,128)(2,1)}, u32[]{:S(2)}) copy-start(bf16[48,16,512]{2,1,0:T(8,128)(2,1)} %get-tuple-element.83) | copy-start | bytes 2359300
  326.2 9.5 %slice-start = ((s8[4718592]{0:T(1024)(128)(4,1)}), s8[4194304]{0:T(1024)(128)(4,1)S(1)}, s32[]{:S(2)}) async-start(s8[4718592]{0:T(1024)(128)(4,1)} %bitcast.209), calls=%async_computation.2 | async-start | bytes 8388608
  326.7 9.0 %copy-start.6 = (f32[512,768]{1,0:T(8,128)}, f32[512,768]{1,0:T(8,128)S(1)}, u32[]{:S(2)}) copy-start(f32[512,768]{1,0:T(8,128)S(1)} %multiply_add_fusion.5) | copy-start | bytes 4718596
  326.7 9.0 %copy-start.4 = (f32[512,768]{1,0:T(8,128)S(1)}, f32[512,768]{1,0:T(8,128)}, u32[]{:S(2)}) copy-start(f32[512,768]{1,0:T(8,128)} %copy-done.3) | copy-start | bytes 4718596
  326.7 9.0 %slice-start.1 = ((s8[4718592]{0:T(1024)(128)(4,1)}), s8[524288]{0:T(1024)(128)(4,1)S(1)}, s32[]{:S(2)}) async-start(s8[4718592]{0:T(1024)(128)(4,1)} %bitcast.209), calls=%async_computation.3 | async-start | bytes 1048576
  340.5 5.0 copy-start.28
  345.5 4.4 copy-start.22
  358.8 76.9 %copy-start.2 = (bf16[1,512,768]{2,1,0:T(8,128)(2,1)S(1)}, bf16[1,512,768]{2,1,0:T(8,128)(2,1)}, u32[]{:S(2)}) copy-start(bf16[1,512,768]{2,1,0:T(8,128)(2,1)} %param.22) | copy-start | bytes 2359300
  452.0 74.6 %copy-start.18 = (f32[24,768]{1,0:T(8,128)S(1)}, f32[24,768]{1,0:T(8,128)}, u32[]{:S(2)}) copy-start(f32[24,768]{1,0:T(8,128)} %get-tuple-element.116) | copy-start | bytes 221188
  519.8 10.9 %copy-start.15 = (f32[24,3072]{1,0:T(8,128)S(1)}, f32[24,3072]{1,0:T(8,128)}, u32[]{:S(2)}) copy-start(f32[24,3072]{1,0:T(8,128)} %get-tuple-element.118) | copy-start | bytes 884740
  519.8 10.9 %copy-start.17 = (f32[24,3072]{1,0:T(8,128)S(1)}, f32[24,3072]{1,0:T(8,128)}, u32[]{:S(2)}) copy-start(f32[24,3072]{1,0:T(8,128)} %get-tuple-element.117) | copy-start | bytes 884740
  525.4 6.0 %copy-start.10 = (f32[512,768]{1,0:T(8,128)S(1)}, f32[512,768]{1,0:T(8,128)}, u32[]{:S(2)}) copy-start(f32[512,768]{1,0:T(8,128)} %get-tuple-element.183) | copy-start | bytes 4718596
  (14 other events, 45.1 us)
Sparse Core Ops, SparseCore 0:
  245.2 112.3 reduce-scatter.1

commit v5 on v4

--- a/solution.py
+++ b/solution.py
@@ -16,8 +16,8 @@
 GATHER_PLANS = [[0, 1, 3, 5, 7, 9, 12], [0, 1, 3, 5, 7, 9, 12], [0, 2, 4, 6, 8, 10, 12], [0, 2, 5, 8, 10, 12, 14], [0, 3, 6, 9, 12, 14, 16]]
 COLUMN_PLANS = [[2, 5, 8, 11, 14], [2, 5, 8, 11, 14], [3, 7, 10, 13, 15], [4, 8, 12, 14, 16]]
 PLANE_PLANS = [[0, 4, 7, 11], [0, 5, 8, 11], [0, 6, 9, 11]]
-REDUCE_PLANS = [[0, 1, 2, 4, 5, 8, 9, 12], [0, 3, 3, 7, 7, 10, 10, 12]]
 PLANE_REDUCE_PLANS = [[0, 1, 1, 7, 7, 11, 11, 12], [0, 1, 1, 9, 9, 12, 12, 12], [0, 1, 1, 11, 11, 12, 12, 12]]
+UNMIX_CHAIN_PLANS = [[0, 8, 10, 12], [0, 8, 10, 12]]
 CHAIN_PLANS = [[0, 1, 3, 6], [1, 2, 4, 7], [2, 3, 6, 9]]
 LAST_PLANS = [[0, 1, 1, 4, 4, 7, 7, 9], [0, 2, 2, 5, 5, 7, 8, 9], [0, 2, 2, 5, 5, 7, 8, 9]]
 f32 = jnp.float32
@@ -1682,7 +1682,7 @@
         normed_mid, inv_mid = layer_norm_parts(middle)
         hidden_in = (normed_mid * gains[layer, 1]).astype(bf16)
         hidden_pre = product(hidden_in, fc_mat)
-        hidden_act = lax.optimization_barrier(gelu(hidden_pre).astype(bf16))
+        hidden_act = gelu(hidden_pre).astype(bf16)
         saved.append(
             (normed, inv_std, norm_in, mixed, rim, long_out, gated, (sig_re, sig_im))
             + (normed_mid, inv_mid, hidden_in, hidden_pre, hidden_act)
@@ -1691,7 +1691,7 @@
     mixed_out, grad = lax.optimization_barrier((stream.astype(bf16), cotangent[0]))
     grad = grad.astype(f32)
     summed = {}
-    left_over = []
+    left_over, half_way = [], []
     small_grads = [None] * layers
     taps_grads = [None] * layers
 
@@ -1725,15 +1725,12 @@
             pending = left_over + [((2, layer), parts_of(grad_fc)), ((1, layer), parts_of(grad_out))]
             left_over = []
         (taps_grads[layer], grad_mixed, grad_conv), arrived = unmix(
-            [reduce_job(parts, plan) for (_, parts), plan in zip(pending, REDUCE_PLANS)]
-            if layer
-            else [plane_reduce_job(parts, plan) for (_, parts), plan in zip(pending, PLANE_REDUCE_PLANS)],
+            [plane_reduce_job(parts, plan) for (_, parts), plan in zip(pending, PLANE_REDUCE_PLANS)]
+            + [chain_reduce_job(part, plan) for (_, part), plan in zip(half_way, UNMIX_CHAIN_PLANS)],
             layer, mixed, conv_cols_of[layer], rim, long_out, grad_gated, specs[layer], sig, skips, tables, ids
         )
-        if layer == 0:
-            half_way = [(key, part) for (key, _), part in zip(pending, arrived)]
-        else:
-            summed.update({key: total for (key, _), total in zip(pending, arrived)})
+        summed.update({key: total for (key, _), total in zip(half_way, arrived[len(pending) :])})
+        half_way = [(key, part) for (key, _), part in zip(pending, arrived)]
         grad_mixed = grad_mixed.reshape(width3, toks)
         grad_norm_in = contract(grad_mixed, in_mat, 0, 1)
         grad_in = contract(norm_in, grad_mixed, 0, 1).astype(bf16)

time: 551 us -> 539 us (0.978)
  Pallas kernels: 387 us -> 373 us
    pallas_call x6, Pallas kernels: 387 us -> 373 us  [fused_call(): pl.pallas_call(kernel, out_shape=list(results) + flat(lambda j: j.results...]
  transfers between devices with their start and end apart: 1 -> 1, of which waited for: 0 -> 0; matrix products, arithmetic and copies ran while one was open for 14% -> 15% of each run, Pallas kernels for 39% -> 37%
where the time goes in v5:
time: 539 us; the launch traced here: 530 us
  Pallas kernels  373 us (69%)
  matrix products  105 us (19%)
  local copies, waits for them, and re-layouts  20.1 us (4%)
  other arithmetic  16.7 us (3%)
  between operations  15.2 us (3%)
    pallas_call x6, Pallas kernels, fused_call(): pl.pallas_call(kernel, out_shape=list(results) + flat(lambda j: j.results...  373 us
    dot_general x20, matrix products, contract(): lax.dot_general(left_mat, right_mat, (((left_dim,), (right_dim,)), ((), (...  86 us
    dot_general x4, matrix products, product(): return jnp.dot(left_mat, right_mat, preferred_element_type=f32)  19.2 us
  transfers between devices with their start and end apart: 1, of which 0 were waited for; matrix products, arithmetic and copies ran while one was open for 15% of the time, Pallas kernels for 37%

profile of v5, /device:TPU:0, one launch (start us, length us, event | category | flops | bytes accessed | tf_op | source)
XLA Modules:
  0.0 530.0 jit_solution(12766422763401005932)
XLA Ops:
  12.8 76.0 %prepare.1 = (f32[2,4,64,4096]{3,2,1,0:T(8,128)}, f32[2,96,4096]{2,1,0:T(8,128)}, f32[2,96,128]{2,1,0:T(8,128)}, f32[12,256,128]{2,1,0:T(8,128)}, f32[12,256,128...) custom-call(f32[48,4096]{1,0:T(8,128)} %constant.56.clone.refs_0_, ...), custom_call_target="tpu_custom_call" | custom-call | tf_op jit(solution)/shard_map/prepare/pallas_call | solution.py:416
  95.4 3.7 convolution_convert_fusion.7
  99.8 50.8 %mix.2 = (bf16[48,16,512]{2,1,0:T(8,128)(2,1)}, bf16[48,16,512]{2,1,0:T(8,128)(2,1)}, f32[12,256,128]{2,1,0:T(8,128)}, f32[12,256,128]{2,1,0:T(8,128)}, f32[3,48...) custom-call(bf16[3,48,16,512]{3,2,1,0:T(8,128)(2,1)} %bitcast.153, ...), custom_call_target="tpu_custom_call" | custom-call | tf_op jit(solution)/shard_map/mix/pallas_call | solution.py:416
  153.0 5.5 %fusion.35 = f32[512,3072]{1,0:T(8,128)S(1)} fusion(bf16[768,3072]{1,0:T(8,128)(2,1)} %bitcast.204, f32[512,768]{1,0:T(8,128)S(1)} %get-tuple-element.175, f32[768]{0:T(1024)S(1)} %get-tuple-element.168, f32[512]{0:T(512)S(1)} %add_rsqrt_fusion.2, f32[512]{0:T(512)S(1)} %broadcast_multiply_fusion.10), kind=kOutput, calls=%fused_computation.124 | convolution fusion | flops 2417491968 | bytes 12590080 | tf_op jit(solution)/shard_map/dot_general | solution.py:28
  158.6 3.6 fusion.40
  162.8 3.6 convolution_convert_fusion.6
  166.4 48.2 %mix.3 = (bf16[48,16,512]{2,1,0:T(8,128)(2,1)}, bf16[48,16,512]{2,1,0:T(8,128)(2,1)}, f32[12,256,128]{2,1,0:T(8,128)}, f32[12,256,128]{2,1,0:T(8,128)}, f32[3,48...) custom-call(bf16[3,48,16,512]{3,2,1,0:T(8,128)(2,1)} %bitcast.151, f32[3,48,16,128]{3,2,1,0:T(8,128)} %bitcast.149, ...), custom_call_target="tpu_custom_call" | custom-call | tf_op jit(solution)/shard_map/mix/pallas_call | solution.py:416
  217.0 5.6 %fusion.36 = f32[512,3072]{1,0:T(8,128)S(1)} fusion(bf16[768,3072]{1,0:T(8,128)(2,1)} %bitcast.212, f32[512,768]{1,0:T(8,128)S(1)} %get-tuple-element.179, f32[768]{0:T(1024)S(1)} %get-tuple-element.166, f32[512]{0:T(512)S(1)} %add_rsqrt_fusion, f32[512]{0:T(512)S(1)} %broadcast_multiply_fusion.8), kind=kOutput, calls=%fused_computation.125 | convolution fusion | flops 2417491968 | bytes 12590080 | tf_op jit(solution)/shard_map/dot_general | solution.py:28
  222.7 4.5 add_convert_fusion
  227.1 4.7 multiply_convert_fusion.1
  231.8 5.1 convolution_convert_fusion.5
  242.5 7.3 %convolution_convert_fusion.4 = bf16[768,3072]{1,0:T(8,128)(2,1)} fusion(bf16[512,3072]{1,0:T(8,128)(2,1)} %copy-done.27, f32[512,768]{1,0:T(8,128)} %copy-done, f32[768]{0:T(1024)S(1)} %get-tuple-element.166, f32[512]{0:T(512)S(1)} %add_rsqrt_fusion, f32[512]{0:T(512)S(1)} %broadcast_multiply_fusion.8), kind=kOutput, calls=%fused_computation.14 | convolution fusion | flops 2419851264 | bytes 9444352 | tf_op jit(solution)/shard_map/dot_general | solution.py:32
  251.7 57.7 %unmix.2 = (f32[12,32,8,128]{3,2,1,0:T(8,128)}, bf16[3,48,16,512]{3,2,1,0:T(8,128)(2,1)}, f32[3,48,16,128]{3,2,1,0:T(8,128)}, bf16[4,24,3072]{2,1,0:T(8,128)(2,1)}, bf16[4,24,768]{2,1,0:T(8,128)(2,1)}) custom-call(bf16[3,48,16,512]{3,2,1,0:T(8,128)(2,1)} %bitcast.152, f32[3,48,16,128]{3,2,1,0:T(8,128)} %bitcast.150, ...), custom_call_target="tpu_custom_call" | custom-call | tf_op jit(solution)/shard_map/unmix/pallas_call | solution.py:416
  309.4 5.3 multiply_reduce_fusion.1
  315.2 9.0 %multiply_convert_fusion = bf16[512,3072]{1,0:T(8,128)(2,1)S(1)} fusion(f32[512,3072]{1,0:T(8,128)} %copy-done.24, bf16[3072,768]{1,0:T(8,128)(2,1)} %bitcast.208, f32[512,768]{1,0:T(8,128)S(1)} %multiply_add_fusion.5), kind=kOutput, calls=%fused_computation | convolution fusion | flops 2439905280 | bytes 15728640 | tf_op jit(solution)/shard_map/dot_general | solution.py:32
  324.3 4.0 multiply_reduce_fusion.2
  334.1 8.1 %convolution_convert_fusion.3 = bf16[3072,768]{1,0:T(8,128)(2,1)} fusion(f32[512,768]{1,0:T(8,128)S(1)} %copy-done.7, f32[512,3072]{1,0:T(8,128)} %copy-done.24), kind=kOutput, calls=%fused_computation.13 | convolution fusion | flops 2431254528 | bytes 12582912 | tf_op jit(solution)/shard_map/dot_general | solution.py:32
  342.2 4.2 convolution_convert_fusion.2
  346.4 4.7 convolution_convert_fusion.1
  351.1 68.3 %unmix.3 = (f32[12,32,8,128]{3,2,1,0:T(8,128)}, bf16[3,48,16,512]{3,2,1,0:T(8,128)(2,1)}, f32[3,48,16,128]{3,2,1,0:T(8,128)}, bf16[4,24,2304]{2,1,0:T(8,128)(2,1...) custom-call(bf16[3,48,16,512]{3,2,1,0:T(8,128)(2,1)} %bitcast.154, ...), custom_call_target="tpu_custom_call" | custom-call | tf_op jit(solution)/shard_map/unmix/pallas_call | solution.py:416
  419.3 6.3 %fusion.12 = (f32[768]{0:T(1024)S(1)}, f32[512]{0:T(512)S(1)}, f32[512]{0:T(512)S(1)}, f32[512,768]{1,0:T(8,128)}) fusion(bf16[1,512,768]{2,1,0:T(8,128)(2,1)S(1)} %copy-done.2, f32[512]{0:T(512)S(1)} %add_rsqrt_fusion.3, f32[512]{0:T(512)S(1)} %broadcast_multiply_fusion.11, f32[768]{0:T(1024)S(1)} %get-tuple-element.169, bf16[2304,512]{1,0:T(8,128)(2,1)} %bitcast.226, ...), kind=kOutput, calls=%fused_computation.33 | convolution fusion | flops 1815476480 | bytes 8271872 | tf_op jit(solution)/shard_map/dot_general | solution.py:32
  428.3 3.1 convolution_convert_fusion.8
  431.4 4.2 convolution_convert_fusion
  435.6 71.8 %last.1 = (f32[272,128]{1,0:T(8,128)}, f32[24,2304]{1,0:T(8,128)}, f32[24,768]{1,0:T(8,128)}, f32[16,128]{1,0:T(8,128)}, f32[24,2304]{1,0:T(8,128)}, /*index=5*/f32[96,768]{1,0:T(8,128)}, f32[24,3072]{1,0:T(8,128)}) custom-call(f32[48,4096]{1,0:T(8,128)} %constant.56.clone.refs_0_, f32[2,64,64]{2,1,0:T(8,128)} %refs_1_.1, f32[2,64,96]{2,1,0:T(8,128)} %refs_2_.3, ...), custom_call_target="tpu_custom_call" | custom-call | tf_op jit(solution)/shard_map/last/pallas_call | solution.py:416
  (159 shorter events, 49.7 us)
Async XLA Ops:
  7.2 513.7 %reduce-scatter.2.cloned.1.call-start = ((), (), s32[]{:S(2)}) async-start(), calls=%async_computation.1 | async-start | bytes 4866048 | tf_op jit(solution)/shard_map/reduce_scatter | solution.py:1699
  12.8 77.9 %copy-start.1 = (bf16[1,512,768]{2,1,0:T(8,128)(2,1)S(1)}, bf16[1,512,768]{2,1,0:T(8,128)(2,1)}, u32[]{:S(2)}) copy-start(bf16[1,512,768]{2,1,0:T(8,128)(2,1)} %param.22) | copy-start | bytes 2359300
  99.8 50.8 %copy-start.12 = (bf16[4,4,2,24,768]{4,3,2,1,0:T(8,128)(2,1)S(1)}, bf16[4,4,2,24,768]{4,3,2,1,0:T(8,128)(2,1)}, u32[]{:S(2)}) copy-start(bf16[4,4,2,24,768]{4,3,2,1,0:T(8,128)(2,1)} %get-tuple-element.78) | copy-start | bytes 3538948
  152.6 5.9 %copy-start.3 = (f32[512,768]{1,0:T(8,128)}, f32[512,768]{1,0:T(8,128)S(1)}, u32[]{:S(2)}) copy-start(f32[512,768]{1,0:T(8,128)S(1)} %get-tuple-element.175) | copy-start | bytes 4718596
  152.6 5.9 %slice-start.2 = ((s8[4718592]{0:T(1024)(128)(4,1)}), s8[4194304]{0:T(1024)(128)(4,1)S(1)}, s32[]{:S(2)}) async-start(s8[4718592]{0:T(1024)(128)(4,1)} %bitcast.209), calls=%async_computation.4 | async-start | bytes 8388608
  153.0 5.6 %slice-start.3 = ((s8[4718592]{0:T(1024)(128)(4,1)}), s8[524288]{0:T(1024)(128)(4,1)S(1)}, s32[]{:S(2)}) async-start(s8[4718592]{0:T(1024)(128)(4,1)} %bitcast.209), calls=%async_computation.5 | async-start | bytes 1048576
  166.4 48.2 %copy-start.8 = (bf16[4,4,2,24,768]{4,3,2,1,0:T(8,128)(2,1)S(1)}, bf16[4,4,2,24,768]{4,3,2,1,0:T(8,128)(2,1)}, u32[]{:S(2)}) copy-start(bf16[4,4,2,24,768]{4,3,2,1,0:T(8,128)(2,1)} %get-tuple-element.86) | copy-start | bytes 3538948
  216.6 23.3 %copy-start = (f32[512,768]{1,0:T(8,128)}, f32[512,768]{1,0:T(8,128)S(1)}, u32[]{:S(2)}) copy-start(f32[512,768]{1,0:T(8,128)S(1)} %get-tuple-element.179) | copy-start | bytes 4718596
  216.6 6.0 %slice-start.6 = ((s8[4718592]{0:T(1024)(128)(4,1)}), s8[4194304]{0:T(1024)(128)(4,1)S(1)}, s32[]{:S(2)}) async-start(s8[4718592]{0:T(1024)(128)(4,1)} %bitcast.216), calls=%async_computation.8 | async-start | bytes 8388608
  216.9 5.7 %slice-start.7 = ((s8[4718592]{0:T(1024)(128)(4,1)}), s8[524288]{0:T(1024)(128)(4,1)S(1)}, s32[]{:S(2)}) async-start(s8[4718592]{0:T(1024)(128)(4,1)} %bitcast.216), calls=%async_computation.9 | async-start | bytes 1048576
  222.6 14.3 %slice-start.4 = ((s8[4718592]{0:T(1024)(128)(4,1)}), s8[4194304]{0:T(1024)(128)(4,1)S(1)}, s32[]{:S(2)}) async-start(s8[4718592]{0:T(1024)(128)(4,1)} %bitcast.213), calls=%async_computation.6 | async-start | bytes 8388608
  227.1 9.8 %slice-start.5 = ((s8[4718592]{0:T(1024)(128)(4,1)}), s8[524288]{0:T(1024)(128)(4,1)S(1)}, s32[]{:S(2)}) async-start(s8[4718592]{0:T(1024)(128)(4,1)} %bitcast.213), calls=%async_computation.7 | async-start | bytes 1048576
  231.8 5.1 copy-start.27
  242.5 7.3 %copy-start.9 = (bf16[48,16,512]{2,1,0:T(8,128)(2,1)S(1)}, bf16[48,16,512]{2,1,0:T(8,128)(2,1)}, u32[]{:S(2)}) copy-start(bf16[48,16,512]{2,1,0:T(8,128)(2,1)} %get-tuple-element.85) | copy-start | bytes 2359300
  314.7 9.6 %slice-start = ((s8[4718592]{0:T(1024)(128)(4,1)}), s8[4194304]{0:T(1024)(128)(4,1)S(1)}, s32[]{:S(2)}) async-start(s8[4718592]{0:T(1024)(128)(4,1)} %bitcast.205), calls=%async_computation.2 | async-start | bytes 8388608
  315.2 9.1 %copy-start.6 = (f32[512,768]{1,0:T(8,128)}, f32[512,768]{1,0:T(8,128)S(1)}, u32[]{:S(2)}) copy-start(f32[512,768]{1,0:T(8,128)S(1)} %multiply_add_fusion.5) | copy-start | bytes 4718596
  315.2 9.1 %copy-start.4 = (f32[512,768]{1,0:T(8,128)S(1)}, f32[512,768]{1,0:T(8,128)}, u32[]{:S(2)}) copy-start(f32[512,768]{1,0:T(8,128)} %copy-done.3) | copy-start | bytes 4718596
  315.2 9.1 %slice-start.1 = ((s8[4718592]{0:T(1024)(128)(4,1)}), s8[524288]{0:T(1024)(128)(4,1)S(1)}, s32[]{:S(2)}) async-start(s8[4718592]{0:T(1024)(128)(4,1)} %bitcast.205), calls=%async_computation.3 | async-start | bytes 1048576
  334.1 8.1 %copy-start.22 = (bf16[3,48,16,512]{3,2,1,0:T(8,128)(2,1)S(1)}, bf16[3,48,16,512]{3,2,1,0:T(8,128)(2,1)}, u32[]{:S(2)}) copy-start(bf16[3,48,16,512]{3,2,1,0:T(8,128)(2,1)} %get-tuple-element.96) | copy-start | bytes 7077892
  351.1 68.3 %copy-start.2 = (bf16[1,512,768]{2,1,0:T(8,128)(2,1)S(1)}, bf16[1,512,768]{2,1,0:T(8,128)(2,1)}, u32[]{:S(2)}) copy-start(bf16[1,512,768]{2,1,0:T(8,128)(2,1)} %param.22) | copy-start | bytes 2359300
  435.6 78.7 %copy-start.18 = (f32[24,768]{1,0:T(8,128)S(1)}, f32[24,768]{1,0:T(8,128)}, u32[]{:S(2)}) copy-start(f32[24,768]{1,0:T(8,128)} %get-tuple-element.120) | copy-start | bytes 221188
  507.4 10.9 %copy-start.15 = (f32[24,3072]{1,0:T(8,128)S(1)}, f32[24,3072]{1,0:T(8,128)}, u32[]{:S(2)}) copy-start(f32[24,3072]{1,0:T(8,128)} %get-tuple-element.122) | copy-start | bytes 884740
  507.4 10.9 %copy-start.17 = (f32[24,3072]{1,0:T(8,128)S(1)}, f32[24,3072]{1,0:T(8,128)}, u32[]{:S(2)}) copy-start(f32[24,3072]{1,0:T(8,128)} %get-tuple-element.121) | copy-start | bytes 884740
  513.1 6.0 %copy-start.10 = (f32[512,768]{1,0:T(8,128)S(1)}, f32[512,768]{1,0:T(8,128)}, u32[]{:S(2)}) copy-start(f32[512,768]{1,0:T(8,128)} %get-tuple-element.183) | copy-start | bytes 4718596
  (13 other events, 45.2 us)
Sparse Core Ops, SparseCore 0:
  242.6 107.8 reduce-scatter.1
